TPU v7x, 32 devices: a whole 2x2x4 slice. The times are simulated.
32 devices in a mesh: rep: 8 (over y, x, core), grp: 4 (over z).
Axes of the slice: x: 2, y: 2, z: 4, core: 2. Of those that a mesh axis runs over, the one named last changes fastest.
Arguments:
- latents: bfloat16 [256, 16, 256], P(('rep', 'grp')), may hold values from -6 to 6
- noise: bfloat16 [256, 16, 256], P(('rep', 'grp')), may hold values from -6 to 6
- timesteps: int32 [256], P(('rep', 'grp')), may hold values from 0 to 999
- labels: int32 [256], P(('rep', 'grp')), may hold values from 0 to 999
- emb_table: float32 [1656, 384], P('grp'), may hold values from -4 to 4
- emb_mom: float32 [1656, 384], P('grp'), may hold values from -0.005859375 to 0.005859375
- emb_ema: float32 [1656, 384], P('grp'), may hold values from -4 to 4
- w_in: float32 [2, 384, 4992], P(None, 'grp'), may hold values from -4 to 4
- in_mom: float32 [2, 384, 4992], P(None, 'grp'), may hold values from -0.005859375 to 0.005859375
- in_ema: float32 [2, 384, 4992], P(None, 'grp'), may hold values from -4 to 4
- w_out: float32 [2, 1920, 384], P(None, 'grp'), may hold values from -4 to 4
- out_mom: float32 [2, 1920, 384], P(None, 'grp'), may hold values from -0.005859375 to 0.005859375
- out_ema: float32 [2, 1920, 384], P(None, 'grp'), may hold values from -4 to 4
- head: float32 [384, 784], P('grp'), may hold values from -4 to 4
- head_mom: float32 [384, 784], P('grp'), may hold values from -0.005859375 to 0.005859375
- head_ema: float32 [384, 784], P('grp'), may hold values from -4 to 4
Outputs:
- loss: float32 [], replicated
- new_emb_table: float32 [1656, 384], P('grp')
- new_emb_mom: float32 [1656, 384], P('grp')
- new_emb_ema: float32 [1656, 384], P('grp')
- new_w_in: float32 [2, 384, 4992], P(None, 'grp')
- new_in_mom: float32 [2, 384, 4992], P(None, 'grp')
- new_in_ema: float32 [2, 384, 4992], P(None, 'grp')
- new_w_out: float32 [2, 1920, 384], P(None, 'grp')
- new_out_mom: float32 [2, 1920, 384], P(None, 'grp')
- new_out_ema: float32 [2, 1920, 384], P(None, 'grp')
- new_head: float32 [384, 784], P('grp')
- new_head_mom: float32 [384, 784], P('grp')
- new_head_ema: float32 [384, 784], P('grp')
All inputs are finite; a program needn't handle non-finite values.
Results may differ from a plain program's by a relative error of at most 0.012.
Values may be sent and summed in bfloat16 or wider, within the bound.
No kernel may reach another device: no remote copies, remote signals or barrier semaphores. Data moves between devices by JAX's collectives and lax.ppermute only.
A program may use at most 256 MiB of HBM per device.

v0:
```python
import math

import jax
import jax.numpy as jnp
from jax import lax
from jax.sharding import PartitionSpec as P

D = 384
HEADS = 6
HEAD_DIM = 64
FREQ = 256
CLASSES = 1000
PATCH_IN = 16
GRID = 16
LAYERS = 2
TOK = 256


EPSILON = 1e-06
MOMENTUM = 0.9
LEARN = 30.0
DECAY = 0.7
HIGH = lax.Precision.HIGHEST


def plan(steps_in):
    anchor = math.cos(0.5 * math.pi * 0.008 / 1.008)
    fraction = (steps_in.astype(jnp.float32) / 1000.0 + 0.008) / 1.008
    levels = jnp.cos(0.5 * math.pi * fraction)
    return levels * levels / (anchor * anchor)


def time_features(steps_in, feat_width):
    half_width = feat_width // 2
    frequencies = jnp.exp(
        -math.log(10000.0) * jnp.arange(half_width, dtype=jnp.float32) / half_width
    )
    angles = steps_in.astype(jnp.float32)[:, None] * frequencies[None, :]
    return jnp.concatenate([jnp.cos(angles), jnp.sin(angles)], axis=1)


def positions(grid_side, model_width):
    quarter = model_width // 4
    omegas = jnp.exp(-math.log(10000.0) * jnp.arange(quarter, dtype=jnp.float32) / quarter)
    places = jnp.arange(grid_side * grid_side, dtype=jnp.int32)
    column = (places % grid_side).astype(jnp.float32)[:, None] * omegas[None, :]
    row_pos = (places // grid_side).astype(jnp.float32)[:, None] * omegas[None, :]
    return jnp.concatenate(
        [jnp.sin(column), jnp.cos(column), jnp.sin(row_pos), jnp.cos(row_pos)], axis=1
    )


def swish_act(values):
    return values / (1.0 + jnp.exp(-values))


def gelu_tanh(values):
    return (
        0.5
        * values
        * (1.0 + jnp.tanh(0.7978845608 * (values + 0.044715 * values * values * values)))
    )


def modulate(hidden, shift_vec, scale_vec):
    centered = hidden - jnp.mean(hidden, axis=-1, keepdims=True)
    variance = jnp.mean(centered * centered, axis=-1, keepdims=True)
    normed = centered * lax.rsqrt(variance + EPSILON)
    return normed * (1.0 + scale_vec[:, None, :]) + shift_vec[:, None, :]


def small_dot(left, right):
    return jnp.dot(left.astype(jnp.float32), right.astype(jnp.float32), precision=HIGH)


def split_heads(qkv_low):
    images, tokens_n, _ = qkv_low.shape
    split_qkv = qkv_low.reshape(images, tokens_n, 3, HEADS, HEAD_DIM)
    return (split_qkv[:, :, 0], split_qkv[:, :, 1], split_qkv[:, :, 2])


def attend(qkv_low, score_scale):
    images, tokens_n, _ = qkv_low.shape
    queries, keys_all, values = split_heads(qkv_low)
    scores = (
        jnp.einsum("inhe,imhe->ihnm", queries, keys_all, preferred_element_type=jnp.float32)
        * score_scale
    )
    row_peak = jnp.max(scores, axis=-1, keepdims=True)
    exps = jnp.exp(scores - row_peak)
    row_total = jnp.sum(exps, axis=-1, keepdims=True)
    probabilities = (exps / row_total).astype(jnp.bfloat16)
    attended = jnp.einsum(
        "ihnm,imhe->inhe", probabilities, values, preferred_element_type=jnp.float32
    )
    return (attended.reshape(images, tokens_n, HEADS * HEAD_DIM), row_peak + jnp.log(row_total))


def attend_back(qkv_low, log_total, grad_low, score_scale):
    images, tokens_n, _ = qkv_low.shape
    queries, keys_all, values = split_heads(qkv_low)
    scores = (
        jnp.einsum("inhe,imhe->ihnm", queries, keys_all, preferred_element_type=jnp.float32)
        * score_scale
    )
    probabilities = jnp.exp(scores - log_total)
    grad_heads = grad_low.reshape(images, tokens_n, HEADS, HEAD_DIM)
    grad_values = jnp.einsum(
        "ihnm,inhe->imhe",
        probabilities.astype(jnp.bfloat16),
        grad_heads,
        preferred_element_type=jnp.float32,
    )
    grad_probs = jnp.einsum(
        "inhe,imhe->ihnm", grad_heads, values, preferred_element_type=jnp.float32
    )
    inner = jnp.sum(probabilities * grad_probs, axis=-1, keepdims=True)
    grad_scores = (probabilities * (grad_probs - inner)).astype(jnp.bfloat16)
    grad_queries = (
        jnp.einsum("ihnm,imhe->inhe", grad_scores, keys_all, preferred_element_type=jnp.float32)
        * score_scale
    )
    grad_keys = (
        jnp.einsum("ihnm,inhe->imhe", grad_scores, queries, preferred_element_type=jnp.float32)
        * score_scale
    )
    stacked = jnp.stack([grad_queries, grad_keys, grad_values], axis=2)
    return stacked.reshape(images, tokens_n, 3 * HEADS * HEAD_DIM)


def advance(weight, moment, average, gradient):
    new_moment = MOMENTUM * moment + gradient
    new_weight = weight - LEARN * (gradient + MOMENTUM * new_moment)
    new_average = DECAY * average + (1.0 - DECAY) * new_weight
    return (new_weight, new_moment, new_average)


def local(
    latents,
    noise,
    timesteps,
    labels,
    emb_table,
    emb_mom,
    emb_ema,
    w_in,
    in_mom,
    in_ema,
    w_out,
    out_mom,
    out_ema,
    head,
    head_mom,
    head_ema,
):
    low_emb = emb_table.astype(jnp.bfloat16)
    low_in = w_in.astype(jnp.bfloat16)
    low_out = w_out.astype(jnp.bfloat16)
    low_head = head.astype(jnp.bfloat16)
    emb_full, in_full, out_full, head_full = (
        lax.all_gather(low_emb, "grp", axis=0, tiled=True),
        lax.all_gather(low_in, "grp", axis=1, tiled=True),
        lax.all_gather(low_out, "grp", axis=1, tiled=True),
        lax.all_gather(low_head, "grp", axis=0, tiled=True),
    )
    images = latents.shape[0]
    score_scale = 1.0 / math.sqrt(HEAD_DIM)
    levels = plan(timesteps)
    noise_level = jnp.sqrt(jnp.maximum(1.0 - levels, 0.0))
    noise_f = noise.astype(jnp.float32)
    noisy_in = (
        jnp.sqrt(levels)[:, None, None] * latents.astype(jnp.float32)
        + noise_level[:, None, None] * noise_f
    ).astype(jnp.bfloat16)
    time_feats = time_features(timesteps, FREQ).astype(jnp.bfloat16)
    w_patch = emb_full[:PATCH_IN]
    w_time1 = emb_full[PATCH_IN : PATCH_IN + FREQ]
    w_time2 = emb_full[PATCH_IN + FREQ : PATCH_IN + FREQ + D]
    w_class = emb_full[PATCH_IN + FREQ + D :]
    pre_time = jnp.dot(time_feats, w_time1, preferred_element_type=jnp.float32)
    time_act = swish_act(pre_time).astype(jnp.bfloat16)
    one_hot = (labels[:, None] == jnp.arange(CLASSES, dtype=jnp.int32)[None, :]).astype(
        jnp.bfloat16
    )
    condition = jnp.dot(time_act, w_time2, preferred_element_type=jnp.float32) + jnp.dot(
        one_hot, w_class, preferred_element_type=jnp.float32
    )
    cond_act = swish_act(condition).astype(jnp.bfloat16)
    hidden = (
        jnp.einsum("icn,cd->ind", noisy_in, w_patch, preferred_element_type=jnp.float32)
        + positions(GRID, D)[None]
    )
    saved = []
    for layer_idx in range(LAYERS):
        w_ada = in_full[layer_idx, :, : 6 * D]
        w_qkv = in_full[layer_idx, :, 6 * D : 9 * D]
        w_fc1 = in_full[layer_idx, :, 9 * D :]
        w_proj = out_full[layer_idx, :D]
        w_fc2 = out_full[layer_idx, D:]
        modulation = jnp.dot(cond_act, w_ada, preferred_element_type=jnp.float32)
        shift_a, scale_a, gate_a, shift_b, scale_b, gate_b = jnp.split(modulation, 6, axis=1)
        normed_a = modulate(hidden, shift_a, scale_a).astype(jnp.bfloat16)
        qkv_low = jnp.einsum(
            "ind,dc->inc", normed_a, w_qkv, preferred_element_type=jnp.float32
        ).astype(jnp.bfloat16)
        attended, log_total = attend(qkv_low, score_scale)
        attended = attended.astype(jnp.bfloat16)
        branch_a = jnp.einsum("ind,de->ine", attended, w_proj, preferred_element_type=jnp.float32)
        middle = hidden + gate_a[:, None, :] * branch_a
        normed_b = modulate(middle, shift_b, scale_b).astype(jnp.bfloat16)
        pre_act = jnp.einsum("ind,df->inf", normed_b, w_fc1, preferred_element_type=jnp.float32)
        activated = gelu_tanh(pre_act).astype(jnp.bfloat16)
        branch_b = jnp.einsum("inf,fd->ind", activated, w_fc2, preferred_element_type=jnp.float32)
        saved.append(
            (
                hidden,
                modulation,
                normed_a,
                qkv_low,
                log_total,
                attended,
                branch_a,
                middle,
                normed_b,
                pre_act,
                activated,
                branch_b,
            )
        )
        hidden = middle + gate_b[:, None, :] * branch_b
    w_final = head_full[:, : 2 * D]
    w_y = head_full[:, 2 * D :]
    final_mods = jnp.dot(cond_act, w_final, preferred_element_type=jnp.float32)
    shift_f, scale_f = jnp.split(final_mods, 2, axis=1)
    normed_f = modulate(hidden, shift_f, scale_f).astype(jnp.bfloat16)
    output = jnp.einsum("ind,dc->icn", normed_f, w_y, preferred_element_type=jnp.float32)
    residue = output - noise_f
    entries_n = images * lax.axis_size("rep") * lax.axis_size("grp") * TOK * PATCH_IN
    loss_value = lax.psum(jnp.sum(residue * residue), ("rep", "grp")) / entries_n
    grad_output = (2.0 / entries_n * residue).astype(jnp.bfloat16)
    grad_wy = jnp.einsum("ind,icn->dc", normed_f, grad_output, preferred_element_type=jnp.float32)
    grad_nf = jnp.einsum("icn,dc->ind", grad_output, w_y, preferred_element_type=jnp.float32)
    _, pull_mod = jax.vjp(modulate, hidden, shift_f, scale_f)
    grad_hidden, grad_shift_f, grad_scale_f = pull_mod(grad_nf)
    grad_final = jnp.concatenate([grad_shift_f, grad_scale_f], axis=1)
    grad_wfinal = small_dot(cond_act.T, grad_final)
    grad_cond_act = small_dot(grad_final, w_final.T)
    summed_in = []
    summed_out = []
    for layer_idx in reversed(range(LAYERS)):
        (
            hidden_in,
            modulation,
            normed_a,
            qkv_low,
            log_total,
            attended,
            branch_a,
            middle,
            normed_b,
            pre_act,
            activated,
            branch_b,
        ) = saved[layer_idx]
        layer_in_w = in_full[layer_idx]
        layer_out_w = out_full[layer_idx]
        w_ada = layer_in_w[:, : 6 * D]
        w_qkv = layer_in_w[:, 6 * D : 9 * D]
        w_fc1 = layer_in_w[:, 9 * D :]
        w_proj = layer_out_w[:D]
        w_fc2 = layer_out_w[D:]
        shift_a, scale_a, gate_a, shift_b, scale_b, gate_b = jnp.split(modulation, 6, axis=1)
        grad_bb = (gate_b[:, None, :] * grad_hidden).astype(jnp.bfloat16)
        grad_gate_b = jnp.sum(grad_hidden * branch_b, axis=1)
        grad_fc2 = jnp.einsum("inf,ind->fd", activated, grad_bb, preferred_element_type=jnp.float32)
        grad_act = jnp.einsum("ind,fd->inf", grad_bb, w_fc2, preferred_element_type=jnp.float32)
        _, pull_gelu = jax.vjp(gelu_tanh, pre_act)
        grad_pre = pull_gelu(grad_act)[0].astype(jnp.bfloat16)
        grad_fc1 = jnp.einsum("ind,inf->df", normed_b, grad_pre, preferred_element_type=jnp.float32)
        grad_nb = jnp.einsum("inf,df->ind", grad_pre, w_fc1, preferred_element_type=jnp.float32)
        _, pull_mod = jax.vjp(modulate, middle, shift_b, scale_b)
        grad_mid, grad_shift_b, grad_scale_b = pull_mod(grad_nb)
        grad_mid = grad_mid + grad_hidden
        grad_ba = (gate_a[:, None, :] * grad_mid).astype(jnp.bfloat16)
        grad_gate_a = jnp.sum(grad_mid * branch_a, axis=1)
        grad_proj = jnp.einsum("ind,ine->de", attended, grad_ba, preferred_element_type=jnp.float32)
        grad_att = jnp.einsum(
            "ine,de->ind", grad_ba, w_proj, preferred_element_type=jnp.float32
        ).astype(jnp.bfloat16)
        grad_qkv = attend_back(qkv_low, log_total, grad_att, score_scale).astype(jnp.bfloat16)
        grad_wqkv = jnp.einsum(
            "ind,inc->dc", normed_a, grad_qkv, preferred_element_type=jnp.float32
        )
        grad_na = jnp.einsum("inc,dc->ind", grad_qkv, w_qkv, preferred_element_type=jnp.float32)
        _, pull_mod = jax.vjp(modulate, hidden_in, shift_a, scale_a)
        grad_below, grad_shift_a, grad_scale_a = pull_mod(grad_na)
        grad_hidden = grad_below + grad_mid
        grad_mods = jnp.concatenate(
            [grad_shift_a, grad_scale_a, grad_gate_a, grad_shift_b, grad_scale_b, grad_gate_b],
            axis=1,
        )
        grad_ada = small_dot(cond_act.T, grad_mods)
        grad_cond_act = grad_cond_act + small_dot(grad_mods, w_ada.T)
        grad_layer_in = jnp.concatenate([grad_ada, grad_wqkv, grad_fc1], axis=1)
        grad_layer_out = jnp.concatenate([grad_proj, grad_fc2], axis=0)
        summed_in.append(grad_layer_in)
        summed_out.append(grad_layer_out)
    grad_tok = grad_hidden.astype(jnp.bfloat16)
    grad_patch = jnp.einsum("icn,ind->cd", noisy_in, grad_tok, preferred_element_type=jnp.float32)
    _, pull_swish = jax.vjp(swish_act, condition)
    grad_cond = pull_swish(grad_cond_act)[0]
    grad_class = small_dot(one_hot.T, grad_cond)
    grad_time2 = small_dot(time_act.T, grad_cond)
    grad_tact = small_dot(grad_cond, w_time2.T)
    _, pull_swish = jax.vjp(swish_act, pre_time)
    grad_pre_time = pull_swish(grad_tact)[0]
    grad_time1 = small_dot(time_feats.T, grad_pre_time)
    grad_emb = jnp.concatenate([grad_patch, grad_time1, grad_time2, grad_class], axis=0)
    grad_head = jnp.concatenate([grad_wfinal, grad_wy], axis=1)
    stacked_in = jnp.stack(summed_in[::-1])
    stacked_out = jnp.stack(summed_out[::-1])
    shards = (
        lax.psum_scatter(grad_emb, "grp", scatter_dimension=0, tiled=True),
        lax.psum_scatter(stacked_in, "grp", scatter_dimension=1, tiled=True),
        lax.psum_scatter(stacked_out, "grp", scatter_dimension=1, tiled=True),
        lax.psum_scatter(grad_head, "grp", scatter_dimension=0, tiled=True),
    )
    emb_grad, in_grad, out_grad, head_grad = lax.psum(
        (shards[0], shards[1], shards[2], shards[3]), "rep"
    )
    emb_new = advance(emb_table, emb_mom, emb_ema, emb_grad)
    in_new = advance(w_in, in_mom, in_ema, in_grad)
    out_new = advance(w_out, out_mom, out_ema, out_grad)
    head_new = advance(head, head_mom, head_ema, head_grad)
    return (
        loss_value,
        emb_new[0],
        emb_new[1],
        emb_new[2],
        in_new[0],
        in_new[1],
        in_new[2],
        out_new[0],
        out_new[1],
        out_new[2],
        head_new[0],
        head_new[1],
        head_new[2],
    )


def solution(mesh):
    placed = (
        P(("rep", "grp"), None, None),
        P(("rep", "grp"), None, None),
        P(("rep", "grp")),
        P(("rep", "grp")),
        P("grp", None),
        P("grp", None),
        P("grp", None),
        P(None, "grp", None),
        P(None, "grp", None),
        P(None, "grp", None),
        P(None, "grp", None),
        P(None, "grp", None),
        P(None, "grp", None),
        P("grp", None),
        P("grp", None),
        P("grp", None),
    )
    return jax.shard_map(
        local,
        mesh=mesh,
        in_specs=placed,
        out_specs=(
            P(),
            P("grp", None),
            P("grp", None),
            P("grp", None),
            P(None, "grp", None),
            P(None, "grp", None),
            P(None, "grp", None),
            P(None, "grp", None),
            P(None, "grp", None),
            P(None, "grp", None),
            P("grp", None),
            P("grp", None),
            P("grp", None),
        ),
        check_vma=False,
    )
```

profile of v0, /device:TPU:0, one launch (start us, length us, event | category | flops | bytes accessed | tf_op | source)
XLA Modules:
  0.0 997.3 jit_solution(8185330983066026907)
XLA Ops:
  14.1 28.0 %all_gather.15 = bf16[384,784]{1,0:T(8,128)(2,1)S(1)} all-gather(bf16[96,784]{1,0:T(8,128)(2,1)S(1)} %convert_element_type.193), channel_id=1, replica_groups=mesh['rep'=8,'grp'=4] {'grp'}, dimensions={0}, use_global_device_ids=true | all-gather | bytes 752640 | tf_op jit(solution)/shard_map/all_gather | solution.py:164
  43.5 9.1 all-gather.9.cloned.1.call-done
  60.9 131.2 %all-gather.5.cloned.1.call-done = bf16[2,384,4992]{2,1,0:T(8,128)(2,1)} async-done(((bf16[2,96,4992]{2,1,0:T(8,128)(2,1)}), bf16[2,384,4992]{2,1,0:T(8,128)(2,1)}) %all-gather.5.cloned.1.call-update) | async-done | bytes 7667728 | tf_op jit(solution)/shard_map/all_gather | solution.py:162
  195.2 5.8 convolution_convert_fusion.1
  200.9 6.7 copy.91
  219.3 5.8 fusion.34
  225.1 27.6 %all-gather.7.cloned.1.call-done = bf16[2,1920,384]{2,1,0:T(8,128)(2,1)} async-done(((bf16[2,480,384]{2,1,0:T(8,128)(2,1)}), bf16[2,1920,384]{2,1,0:T(8,128)(2,1)}) %all-gather.7.cloned.1.call-update) | async-done | bytes 2949136 | tf_op jit(solution)/shard_map/all_gather | solution.py:163
  263.5 7.9 fusion.143
  273.6 5.7 convolution_convert_fusion
  279.3 7.0 copy.97
  303.0 6.4 fusion.59
  309.4 8.7 fusion.141
  326.8 9.2 convolution_bitcast_fusion
  338.1 15.8 %fusion.8 = bf16[8,256,1536]{2,1,0:T(8,128)(2,1)S(1)} fusion(f32[8,256,1536]{2,1,0:T(8,128)} %fusion.59, bf16[2,1920,384]{2,1,0:T(8,128)(2,1)S(1)} %copy-done.65, f32[8,256,384]{2,1,0:T(8,128)S(1)} %get-tuple-element.51, f32[8,256]{1,0:T(8,128)S(1)} %negate_multiply_fusion.4, f32[8,384]{1,0:T(8,128)S(1)} %copy-done.133), kind=kOutput, calls=%fused_computation.16 | convolution fusion | flops 2493775872 | bytes 23220224 | tf_op jit(solution)/shard_map/ind,fd->inf/dot_general | solution.py:276
  370.5 8.7 fusion.47
  379.1 9.8 multiply_reduce_fusion.1
  389.0 7.0 multiply_convert_fusion.1
  411.5 5.2 multiply_reduce_fusion.15
  421.5 13.6 %fusion.4 = bf16[8,256,1536]{2,1,0:T(8,128)(2,1)S(1)} fusion(f32[8,256,1536]{2,1,0:T(8,128)S(1)} %bitcast.268, bf16[2,1920,384]{2,1,0:T(8,128)(2,1)} %all-gather.7.cloned.1.call-done, f32[8,256,384]{2,1,0:T(8,128)S(1)} %get-tuple-element.47, f32[8,384]{1,0:T(8,128)S(1)} %copy-done.132), kind=kOutput, calls=%fused_computation.12 | convolution fusion | flops 2492989440 | bytes 23212032 | tf_op jit(solution)/shard_map/ind,fd->inf/dot_general | solution.py:276
  435.1 6.1 multiply_reduce_fusion.14
  456.6 9.0 convolution_bitcast_fusion.1
  468.8 14.2 %multiply_reduce_fusion = (f32[8,6,256]{2,1,0:T(8,128)S(1)}, f32[8,6,256,256]{2,3,1,0:T(8,128)}) fusion(f32[8,6,256,256]{2,3,1,0:T(8,128)} %copy-done, f32[8,6,256]{2,1,0:T(8,128)S(1)} %log_add_fusion.1, bf16[8,256,6,64]{1,3,2,0:T(8,128)(2,1)} %bitcast.263, bf16[8,256,3,6,64]{1,4,3,2,0:T(8,128)(2,1)} %bitcast.249), kind=kOutput, calls=%fused_computation.22 | convolution fusion | flops 415223808 | bytes 28409856 | tf_op jit(solution)/shard_map/inhe,imhe->ihnm/dot_general | solution.py:114
  483.0 7.4 multiply_convert_fusion
  502.3 5.3 multiply_reduce_fusion.13
  518.5 6.9 convolution_bitcast_fusion.5
  538.4 11.7 %pad_maximum_fusion = f32[2,384,4992]{2,1,0:T(8,128)} fusion(f32[1,384,4992]{2,1,0:T(8,128)} %maximum_bitcast_fusion.1, f32[1,384,4992]{2,1,0:T(8,128)} %maximum_bitcast_fusion), kind=kLoop, calls=%fused_computation.8 | loop fusion | flops 3833856 | bytes 30670848 | tf_op jit(solution)/shard_map/stack | solution.py:320
  564.2 77.3 %fusion = f32[416,384]{1,0:T(8,128)S(1)} fusion(f32[1656,384]{1,0:T(8,128)S(1)} %pad_maximum_fusion.4), kind=kCustom, calls=%all-reduce-scatter | all-reduce-scatter fusion | flops 638977 | bytes 3183104
  641.5 7.1 collective-permute-start
  651.6 208.2 %reduce-scatter.6.cloned.1.call-done = f32[2,96,4992]{2,1,0:T(8,128)} async-done(((f32[2,384,4992]{2,1,0:T(8,128)}), f32[2,96,4992]{2,1,0:T(8,128)}) %reduce-scatter.6.cloned.1.call-update) | async-done | bytes 3833872 | tf_op jit(solution)/shard_map/reduce_scatter | solution.py:324
  859.8 42.7 %psum.35 = f32[]{:T(128)} all-reduce(f32[]{:T(128)} %get-tuple-element.99), channel_id=1, replica_groups=mesh['rep'=8,'grp'=4] {'rep','grp'}, use_global_device_ids=true, to_apply=%region_15.16 | all-reduce | flops 1 | bytes 8 | tf_op jit(solution)/shard_map/psum | solution.py:239
  903.1 67.8 %all-reduce.5.cloned.1.call-done = (f32[414,384]{1,0:T(8,128)}, f32[2,96,4992]{2,1,0:T(8,128)}, f32[2,480,384]{2,1,0:T(8,128)}, f32[96,784]{1,0:T(8,128)}) async-done(((f32[414,384]{1,0:T(8,128)}, f32[2,96,4992]{2,1,0:T(8,128)}, f32[2,480,384]{2,1,0:T(8,128)}, f32[96,784]{1,0:T(8,128)}), (f32[414,384]{1,0:T(8,128)}, f32[2,96,4992]{2,1,0:T(8,128)}, f32[2,480,384]{2,1,0:T(8,128)}, ...) | async-done | bytes 6245392 | tf_op jit(solution)/shard_map/psum | solution.py:328
  978.1 10.8 %multiply_add_fusion.4 = (f32[2,96,4992]{2,1,0:T(8,128)}, f32[2,96,4992]{2,1,0:T(8,128)}, f32[2,96,4992]{2,1,0:T(8,128)}) fusion(f32[2,96,4992]{2,1,0:T(8,128)} %param.25, f32[2,96,4992]{2,1,0:T(8,128)} %param.23, f32[2,96,4992]{2,1,0:T(8,128)} %get-tuple-element.29, f32[2,96,4992]{2,1,0:T(8,128)} %param.24), kind=kLoop, calls=%fused_computation.61 | loop fusion | flops 8626176 | bytes 26836992 | tf_op jit(solution)/shard_map/add | solution.py:134
  (469 shorter events, 184.5 us)
Async XLA Ops:
  7.2 45.4 %all-gather.9.cloned.1.call-start = ((), (), s32[]{:S(2)}) async-start(), calls=%async_computation.8 | async-start | bytes 1597440 | tf_op jit(solution)/shard_map/all_gather | solution.py:161
  9.1 183.0 %all-gather.5.cloned.1.call-start = ((), (), s32[]{:S(2)}) async-start(), calls=%async_computation.3 | async-start | bytes 9584640 | tf_op jit(solution)/shard_map/all_gather | solution.py:162
  12.8 239.9 %all-gather.7.cloned.1.call-start = ((), (), s32[]{:S(2)}) async-start(), calls=%async_computation.4 | async-start | bytes 3686400 | tf_op jit(solution)/shard_map/all_gather | solution.py:163
  13.9 40.7 %copy-start.138 = (s32[8]{0:T(128)S(1)}, s32[8]{0:T(128)}, u32[]{:S(2)}) copy-start(s32[8]{0:T(128)} %param.19) | copy-start | bytes 100
  13.9 637.7 %reduce-scatter.10.cloned.1.call-start = ((), (), s32[]{:S(2)}) async-start(), calls=%async_computation.7 | async-start | bytes 1720320 | tf_op jit(solution)/shard_map/reduce_scatter | solution.py:326
  14.0 42.3 %copy-start.134 = (f32[8]{0:T(128)}, f32[8]{0:T(128)S(1)}, u32[]{:S(2)}) copy-start(f32[8]{0:T(128)S(1)} %get-tuple-element.60) | copy-start | bytes 100
  14.1 42.2 %copy-start.136 = (f32[8]{0:T(128)}, f32[8]{0:T(128)S(1)}, u32[]{:S(2)}) copy-start(f32[8]{0:T(128)S(1)} %maximum_sqrt_fusion) | copy-start | bytes 100
  43.5 209.3 %copy-start.14 = (f32[256,384]{1,0:T(8,128)}, f32[256,384]{1,0:T(8,128)S(1)}, u32[]{:S(2)}) copy-start(f32[256,384]{1,0:T(8,128)S(1)} %pad_maximum_fusion.6) | copy-start | bytes 1179652
  55.5 136.7 %copy-start.77 = (bf16[8,384]{1,0:T(8,128)(2,1)}, bf16[8,384]{1,0:T(8,128)(2,1)S(1)}, u32[]{:S(2)}) copy-start(bf16[8,384]{1,0:T(8,128)(2,1)S(1)} %get-tuple-element.87) | copy-start | bytes 18436
  58.1 194.6 %copy-start.6 = (f32[8,256,384]{2,1,0:T(8,128)}, f32[8,256,384]{2,1,0:T(8,128)S(1)}, u32[]{:S(2)}) copy-start(f32[8,256,384]{2,1,0:T(8,128)S(1)} %get-tuple-element.90) | copy-start | bytes 9437188
  194.6 63.6 %copy-start.45 = (f32[8,384]{1,0:T(8,128)}, f32[8,384]{1,0:T(8,128)S(1)}, u32[]{:S(2)}) copy-start(f32[8,384]{1,0:T(8,128)S(1)} %get-tuple-element.73) | copy-start | bytes 36868
  271.3 28.0 %copy-start.9 = (f32[8,256,384]{2,1,0:T(8,128)}, f32[8,256,384]{2,1,0:T(8,128)S(1)}, u32[]{:S(2)}) copy-start(f32[8,256,384]{2,1,0:T(8,128)S(1)} %get-tuple-element.57) | copy-start | bytes 9437188
  302.0 58.1 %copy-start.2 = (f32[8,256,384]{2,1,0:T(8,128)}, f32[8,256,384]{2,1,0:T(8,128)S(1)}, u32[]{:S(2)}) copy-start(f32[8,256,384]{2,1,0:T(8,128)S(1)} %get-tuple-element.55) | copy-start | bytes 9437188
  302.1 58.1 %copy-start.49 = (f32[8,256]{1,0:T(8,128)}, f32[8,256]{1,0:T(8,128)S(1)}, u32[]{:S(2)}) copy-start(f32[8,256]{1,0:T(8,128)S(1)} %broadcast_multiply_fusion.1) | copy-start | bytes 24580
  302.7 57.4 %copy-start.60 = (f32[8,256]{1,0:T(8,128)}, f32[8,256]{1,0:T(8,128)S(1)}, u32[]{:S(2)}) copy-start(f32[8,256]{1,0:T(8,128)S(1)} %fusion.116) | copy-start | bytes 24580
  325.3 79.1 %copy-start.97 = (f32[8,384]{1,0:T(8,128)}, f32[8,384]{1,0:T(8,128)S(1)}, u32[]{:S(2)}) copy-start(f32[8,384]{1,0:T(8,128)S(1)} %get-tuple-element.21) | copy-start | bytes 36868
  325.3 79.1 %copy-start.98 = (f32[8,384]{1,0:T(8,128)}, f32[8,384]{1,0:T(8,128)S(1)}, u32[]{:S(2)}) copy-start(f32[8,384]{1,0:T(8,128)S(1)} %get-tuple-element.26) | copy-start | bytes 36868
  338.1 15.8 %copy-start.27 = (bf16[384,4992]{1,0:T(8,128)(2,1)}, bf16[384,4992]{1,0:T(8,128)(2,1)S(1)}, u32[]{:S(2)}) copy-start(bf16[384,4992]{1,0:T(8,128)(2,1)S(1)} %get-tuple-element.63) | copy-start | bytes 11501572
  370.5 18.5 %slice-start.3 = ((s8[12582912]{0:T(1024)(128)(4,1)}), s8[4194304]{0:T(1024)(128)(4,1)S(1)}, s32[]{:S(2)}) async-start(s8[12582912]{0:T(1024)(128)(4,1)} %bitcast.245), calls=%async_computation.13 | async-start | bytes 8388608
  370.5 18.5 %slice-start.4 = ((s8[12582912]{0:T(1024)(128)(4,1)}), s8[4194304]{0:T(1024)(128)(4,1)S(1)}, s32[]{:S(2)}) async-start(s8[12582912]{0:T(1024)(128)(4,1)} %bitcast.245), calls=%async_computation.14 | async-start | bytes 8388608
  406.3 245.3 %reduce-scatter.8.cloned.1.call-start = ((), (), s32[]{:S(2)}) async-start(), calls=%async_computation.6 | async-start | bytes 7372800 | tf_op jit(solution)/shard_map/reduce_scatter | solution.py:325
  421.4 22.4 %copy-start.24 = (f32[8,256,384]{2,1,0:T(8,128)}, f32[8,256,384]{2,1,0:T(8,128)S(1)}, u32[]{:S(2)}) copy-start(f32[8,256,384]{2,1,0:T(8,128)S(1)} %get-tuple-element.47) | copy-start | bytes 9437188
  468.8 391.0 %reduce-scatter.6.cloned.1.call-start = ((), (), s32[]{:S(2)}) async-start(), calls=%async_computation.5 | async-start | bytes 19169280 | tf_op jit(solution)/shard_map/reduce_scatter | solution.py:324
  550.2 420.8 %all-reduce.5.cloned.1.call-start = ((), (), s32[]{:S(2)}) async-start(), calls=%async_computation.9 | async-start | bytes 12582912 | tf_op jit(solution)/shard_map/psum | solution.py:328
  564.0 84.7 %copy-start.140 = (u32[32]{0:T(128)S(1)}, u32[32]{0:T(128)}, u32[]{:S(2)}) copy-start(u32[32]{0:T(128)} %constant.133) | copy-start | bytes 388
  641.5 8.6 collective-permute-start
  859.8 111.1 %copy-start.44 = (f32[96,784]{1,0:T(8,128)S(1)}, f32[96,784]{1,0:T(8,128)}, u32[]{:S(2)}) copy-start(f32[96,784]{1,0:T(8,128)} %param.29) | copy-start | bytes 903172
  859.8 111.1 %copy-start.72 = (f32[96,784]{1,0:T(8,128)S(1)}, f32[96,784]{1,0:T(8,128)}, u32[]{:S(2)}) copy-start(f32[96,784]{1,0:T(8,128)} %param.31) | copy-start | bytes 903172
  859.8 111.1 %copy-start.73 = (f32[96,784]{1,0:T(8,128)S(1)}, f32[96,784]{1,0:T(8,128)}, u32[]{:S(2)}) copy-start(f32[96,784]{1,0:T(8,128)} %param.30) | copy-start | bytes 903172
  859.8 113.4 %copy-start.35 = (f32[414,384]{1,0:T(8,128)S(1)}, f32[414,384]{1,0:T(8,128)}, u32[]{:S(2)}) copy-start(f32[414,384]{1,0:T(8,128)} %param.20) | copy-start | bytes 1907716
  859.8 113.4 %copy-start.54 = (f32[414,384]{1,0:T(8,128)S(1)}, f32[414,384]{1,0:T(8,128)}, u32[]{:S(2)}) copy-start(f32[414,384]{1,0:T(8,128)} %param.22) | copy-start | bytes 1907716
  859.8 113.4 %copy-start.55 = (f32[414,384]{1,0:T(8,128)S(1)}, f32[414,384]{1,0:T(8,128)}, u32[]{:S(2)}) copy-start(f32[414,384]{1,0:T(8,128)} %param.21) | copy-start | bytes 1907716
  (135 other events, 726.0 us)
Sparse Core Ops, SparseCore 0:
  10.2 42.4 all-gather.8
  54.8 137.3 all-gather.4
  194.3 58.3 all-gather.6
  406.4 30.9 reduce-scatter.9
  468.9 105.2 reduce-scatter.7
  576.5 283.1 reduce-scatter.5
  864.0 106.8 all-reduce.4
where the time goes:
time: 1010 us; the launch traced here: 997 us
  waiting for transfers between devices  444 us (44%)
  matrix products  239 us (24%)
  blocking collectives  148 us (15%)
  other arithmetic  99.6 us (10%)
  local copies, waits for them, and re-layouts  39.6 us (4%)
  between operations  19.2 us (2%)
    reduce_scatter x1, waiting for transfers between devices, local(): lax.psum_scatter(stacked_in, 'grp', scatter_dimension=1, tiled=True)  208 us
    all_gather x1, waiting for transfers between devices, local(): lax.all_gather(low_in, 'grp', axis=1, tiled=True)  131 us
    unnamed x1, blocking collectives  77.3 us
    psum x1, waiting for transfers between devices, local(): lax.psum((shards[0], shards[1], shards[2], shards[3]), 'rep')  67.8 us
    psum x1, blocking collectives, local(): lax.psum(jnp.sum(residue * residue), ('rep', 'grp')) / entries_n  42.7 us
    dot_general x2, matrix products, local(): jnp.einsum('ind,fd->inf', grad_bb, w_fc2, preferred_element_type=jnp.floa...  29.4 us
    all_gather x1, blocking collectives, local(): lax.all_gather(low_head, 'grp', axis=0, tiled=True)  28 us
    all_gather x1, waiting for transfers between devices, local(): lax.all_gather(low_out, 'grp', axis=1, tiled=True)  27.6 us
  transfers between devices with their start and end apart: 8, of which 6 were waited for; matrix products, arithmetic and copies ran while one was open for 27% of the time, Pallas kernels for 0%

commit v1 on v0

v1 whole, which is shorter than its diff:
```python
import functools
import math

import jax
import jax.numpy as jnp
from jax import lax
from jax.experimental import pallas as pl
from jax.experimental.pallas import tpu as pltpu
from jax.sharding import PartitionSpec as P

D = 384
HEADS = 6
HEAD_DIM = 64
FF = 1536
TOK = 256
PATCH_IN = 16
EPSILON = 1e-06
BF = jnp.bfloat16
F32 = jnp.float32
VMEM_LIMIT = 58 * 1024 * 1024


def mm(left, right):
    return lax.dot_general(left, right, (((1,), (0,)), ((), ())), preferred_element_type=F32)


def mm_nt(left, right):
    return lax.dot_general(left, right, (((1,), (1,)), ((), ())), preferred_element_type=F32)


def norm_parts(x):
    centered = x - jnp.mean(x, axis=0, keepdims=True)
    variance = jnp.mean(centered * centered, axis=0, keepdims=True)
    inv = lax.rsqrt(variance + EPSILON)
    return centered * inv, inv


def norm_back(d, normed, inv, scale1):
    dn = d * scale1
    m1 = jnp.mean(dn, axis=0, keepdims=True)
    m2 = jnp.mean(dn * normed, axis=0, keepdims=True)
    return (dn - m1 - normed * m2) * inv


def column(mods_ref, index, image):
    block = mods_ref[pl.ds(index * D, D), :]
    lane = lax.broadcasted_iota(jnp.int32, block.shape, 1)
    return jnp.sum(jnp.where(lane == image, block, 0.0), axis=1, keepdims=True)


def put_column(out_ref, index, image, values):
    total = jnp.sum(values, axis=1, keepdims=True)
    rows = pl.ds(index * D, D)
    old = out_ref[rows, :]
    lane = lax.broadcasted_iota(jnp.int32, old.shape, 1)
    out_ref[rows, :] = jnp.where(lane == image, total, old)


def half_zero(x, half):
    row = lax.broadcasted_iota(jnp.int32, x.shape, 0)
    keep = row < HEAD_DIM if half == 0 else row >= HEAD_DIM
    return jnp.where(keep, x, jnp.zeros_like(x))


def attention_forward(qkv_ref, b, lse_ref, att_ref, att_lanes):
    for pair in range(HEADS // 2):
        lo = 2 * HEAD_DIM * pair
        q2 = qkv_ref[b, lo : lo + 128, :]
        k2 = qkv_ref[b, D + lo : D + lo + 128, :].T
        for half in range(2):
            head = 2 * pair + half
            scores = mm(k2, half_zero(q2, half))
            peak = jnp.max(scores, axis=0, keepdims=True)
            exps = jnp.exp(scores - peak)
            total = jnp.sum(exps, axis=0, keepdims=True)
            vrow = 2 * D + HEAD_DIM * head
            out = mm(qkv_ref[b, vrow : vrow + HEAD_DIM, :], exps.astype(BF))
            att_ref[HEAD_DIM * head : HEAD_DIM * (head + 1), att_lanes] = (
                out * (1.0 / total)
            ).astype(BF)
            lse_ref[b, head : head + 1, :] = peak + jnp.log(total)


def attention_backward(qkv_ref, b, lse_ref, go_ref, gqkv_ref, lanes):
    for pair in range(HEADS // 2):
        lo = 2 * HEAD_DIM * pair
        q2 = qkv_ref[b, lo : lo + 128, :]
        k2 = qkv_ref[b, D + lo : D + lo + 128, :].T
        v2 = qkv_ref[b, 2 * D + lo : 2 * D + lo + 128, :].T
        g2 = go_ref[b, lo : lo + 128, :]
        for half in range(2):
            head = 2 * pair + half
            row = HEAD_DIM * head
            scores = mm(k2, half_zero(q2, half))
            probs = jnp.exp(scores - lse_ref[b, head : head + 1, :])
            gprobs = mm(v2, half_zero(g2, half))
            inner = jnp.sum(probs * gprobs, axis=0, keepdims=True)
            gscores = (probs * (gprobs - inner)).astype(BF)
            gq = mm(qkv_ref[b, D + row : D + row + HEAD_DIM, :], gscores)
            gk = mm_nt(qkv_ref[b, row : row + HEAD_DIM, :], gscores)
            gv = mm_nt(go_ref[b, row : row + HEAD_DIM, :], probs.astype(BF))
            gqkv_ref[row : row + HEAD_DIM, lanes] = (gq * (1.0 / math.sqrt(HEAD_DIM))).astype(BF)
            gqkv_ref[D + row : D + row + HEAD_DIM, lanes] = gk.astype(BF)
            gqkv_ref[2 * D + row : 2 * D + row + HEAD_DIM, lanes] = gv.astype(BF)


def project_qkv(wqkv_t_ref, normed_ref, lanes, qkv_ref, b):
    qkv = mm(wqkv_t_ref[...], normed_ref[:, lanes])
    qkv_ref[b, 0:D, :] = (qkv[0:D] * (1.0 / math.sqrt(HEAD_DIM))).astype(BF)
    qkv_ref[b, D:, :] = qkv[D:].astype(BF)


GELU_C = 0.7978845608
GELU_A = 0.044715


def gelu_both(v):
    square = v * v
    t = jnp.tanh(v * (GELU_C + (GELU_C * GELU_A) * square))
    half = 0.5 + 0.5 * t
    slope = half + 0.5 * v * (1.0 - t * t) * (GELU_C + (3.0 * GELU_C * GELU_A) * square)
    return v * half, slope


def gelu_one(v):
    t = jnp.tanh(v * (GELU_C + (GELU_C * GELU_A) * (v * v)))
    return v * (0.5 + 0.5 * t)


def accumulate(acc_ref, value, first):
    @pl.when(first)
    def _():
        acc_ref[...] = value

    @pl.when(jnp.logical_not(first))
    def _():
        acc_ref[...] += value


FF_CHUNK = 512


def pack_blocks(pack_ref, start, acc_ref):
    members = pack_ref.shape[0]
    rows = D // members
    for g in range(members):
        for c in range(acc_ref.shape[1] // D):
            pack_ref[g, start + rows * c : start + rows * (c + 1), :] = acc_ref[
                rows * g : rows * (g + 1), D * c : D * (c + 1)
            ].astype(BF)


def pack_outer(pack_ref, awo_ref, awf_ref, awg_ref, awy_ref):
    members, total, _ = pack_ref.shape
    rows = (D + FF) // members
    for g in range(members):
        low, high = rows * g, rows * (g + 1)
        if low < D:
            cut = min(high, D)
            pack_ref[g, 0 : cut - low, :] = awo_ref[low:cut, :].astype(BF)
        if high > D:
            cut = max(low, D)
            pack_ref[g, cut - low : rows, :] = awg_ref[cut - D : high - D, :].astype(BF)
    pack_blocks(pack_ref, rows, awf_ref)
    used = rows + FF // members
    pack_ref[:, used:, :] = jnp.zeros_like(pack_ref[:, used:, :])
    if awy_ref is not None:
        for g in range(members):
            pack_ref[g, used : used + PATCH_IN, :] = awy_ref[...].astype(BF)


def att_fwd_kernel(B, noisy_ref, wp_t_ref, pos_ref, mods_ref, wqkv_t_ref, wo_t_ref,
                   qkv_ref, lse_ref, att_out_ref, br_ref, mid_ref, normed_ref, att_ref):
    step = pl.program_id(0)
    for b in range(B):
        image = step * B + b
        lanes = slice(TOK * b, TOK * (b + 1))
        hidden = mm(wp_t_ref[...], noisy_ref[b]) + pos_ref[...]
        normed, _ = norm_parts(hidden)
        shift = column(mods_ref, 0, image)
        scale = column(mods_ref, 1, image)
        gate = column(mods_ref, 2, image)
        normed_ref[:, lanes] = (normed * (1.0 + scale) + shift).astype(BF)
        project_qkv(wqkv_t_ref, normed_ref, lanes, qkv_ref, b)
        attention_forward(qkv_ref, b, lse_ref, att_ref, lanes)
        att_out_ref[b] = att_ref[:, lanes]
        branch = mm(wo_t_ref[...], att_ref[:, lanes])
        br_ref[b] = branch
        mid_ref[b] = hidden + gate * branch


def ffn_fwd_kernel(B, mid_ref, mods_ref, wf_t_ref, wg_t_ref, br_ref, hid_ref, normed_ref):
    step = pl.program_id(0)
    for b in range(B):
        image = step * B + b
        lanes = slice(TOK * b, TOK * (b + 1))
        mid = mid_ref[b]
        normed, _ = norm_parts(mid)
        shift = column(mods_ref, 3, image)
        scale = column(mods_ref, 4, image)
        gate = column(mods_ref, 5, image)
        normed_ref[:, lanes] = (normed * (1.0 + scale) + shift).astype(BF)
        branch = None
        for f in range(0, FF, FF_CHUNK):
            pre = mm(wf_t_ref[f : f + FF_CHUNK, :], normed_ref[:, lanes])
            part = mm(wg_t_ref[:, f : f + FF_CHUNK], gelu_one(pre).astype(BF))
            branch = part if branch is None else branch + part
        br_ref[b] = branch
        hid_ref[b] = mid + gate * branch


def out_bwd(b, image, lanes, gmid, branch, gate, wo_ref, gba_ref, go_ref, gm_ref, gm_base):
    put_column(gm_ref, gm_base, image, gmid * branch)
    gba_ref[:, lanes] = (gate * gmid).astype(BF)
    go_ref[b] = mm(wo_ref[...], gba_ref[:, lanes]).astype(BF)


def block_kernel(B, entries, hid_ref, noise_ref, mods_ref, modf_ref, wqkv_t_ref, wo_t_ref, wf_t_ref,
                 wg_t_ref, wo_ref, wf_ref, wg_ref, wy_t_ref, wy_ref,
                 qkv_ref, lse_ref, go_ref, gmid_ref, gm_ref, gmf_ref, loss_ref,
                 pack_ref,
                 normed_ref, att_ref, slope_ref, act_ref, gpre_ref, gba_ref, gbb_ref, normf_ref, gout_ref,
                 awo_ref, awf_ref, awg_ref, awy_ref):
    step = pl.program_id(0)
    first = step == 0

    @pl.when(first)
    def _():
        gm_ref[...] = jnp.zeros_like(gm_ref)
        gmf_ref[...] = jnp.zeros_like(gmf_ref)
        loss_ref[...] = jnp.zeros_like(loss_ref)

    for b in range(B):
        image = step * B + b
        lanes = slice(TOK * b, TOK * (b + 1))
        hidden = hid_ref[b]
        normed, _ = norm_parts(hidden)
        normed_ref[:, lanes] = (
            normed * (1.0 + column(mods_ref, 1, image)) + column(mods_ref, 0, image)
        ).astype(BF)
        project_qkv(wqkv_t_ref, normed_ref, lanes, qkv_ref, b)
        attention_forward(qkv_ref, b, lse_ref, att_ref, lanes)
        branch_a = mm(wo_t_ref[...], att_ref[:, lanes])
        gate_a = column(mods_ref, 2, image)
        mid = hidden + gate_a * branch_a
        normed_b, inv_b = norm_parts(mid)
        scale_b = 1.0 + column(mods_ref, 4, image)
        normed_ref[:, lanes] = (normed_b * scale_b + column(mods_ref, 3, image)).astype(BF)
        branch_b = None
        for f in range(0, FF, FF_CHUNK):
            rows = slice(f, f + FF_CHUNK)
            pre = mm(wf_t_ref[rows, :], normed_ref[:, lanes])
            act, slope = gelu_both(pre)
            slope_ref[rows, :] = slope
            act_ref[rows, lanes] = act.astype(BF)
            part = mm(wg_t_ref[:, rows], act_ref[rows, lanes])
            branch_b = part if branch_b is None else branch_b + part
        gate_b = column(mods_ref, 5, image)
        hidden2 = mid + gate_b * branch_b
        normed_f, inv_f = norm_parts(hidden2)
        scale_f = 1.0 + column(modf_ref, 1, image)
        normf_ref[:, lanes] = (normed_f * scale_f + column(modf_ref, 0, image)).astype(BF)
        residue = mm(wy_t_ref[...], normf_ref[:, lanes]) - noise_ref[b].astype(F32)
        loss_ref[...] += residue * residue
        gout_ref[:, lanes] = ((2.0 / entries) * residue).astype(BF)
        gnf = mm(wy_ref[...], gout_ref[:, lanes])
        put_column(gmf_ref, 0, image, gnf)
        put_column(gmf_ref, 1, image, gnf * normed_f)
        ghid = norm_back(gnf, normed_f, inv_f, scale_f)
        put_column(gm_ref, 3, image, ghid * branch_b)
        gbb_ref[:, lanes] = (gate_b * ghid).astype(BF)
        gnb = None
        for f in range(0, FF, FF_CHUNK):
            rows = slice(f, f + FF_CHUNK)
            gact = mm(wg_ref[rows, :], gbb_ref[:, lanes])
            gpre_ref[rows, lanes] = (gact * slope_ref[rows, :]).astype(BF)
            part = mm(wf_ref[:, rows], gpre_ref[rows, lanes])
            gnb = part if gnb is None else gnb + part
        put_column(gm_ref, 1, image, gnb)
        put_column(gm_ref, 2, image, gnb * normed_b)
        gmid = ghid + norm_back(gnb, normed_b, inv_b, scale_b)
        gmid_ref[b] = gmid
        out_bwd(b, image, lanes, gmid, branch_a, gate_a, wo_ref, gba_ref, go_ref, gm_ref, 0)
    accumulate(awo_ref, mm_nt(att_ref[...], gba_ref[...]), first)
    accumulate(awf_ref, mm_nt(normed_ref[...], gpre_ref[...]), first)
    accumulate(awg_ref, mm_nt(act_ref[...], gbb_ref[...]), first)
    accumulate(awy_ref, mm_nt(gout_ref[...], normf_ref[...]), first)

    @pl.when(step == pl.num_programs(0) - 1)
    def _():
        pack_outer(pack_ref, awo_ref, awf_ref, awg_ref, awy_ref)


def ffn_bwd_kernel(B, ghid_ref, mid_ref, att_ref, bra_ref, brb_ref, mods_ref, wf_t_ref, wo_ref, wf_ref,
                   wg_ref, go_ref, gmid_ref, gm_ref, pack_ref,
                   normed_ref, act_ref, gpre_ref, gba_ref, gbb_ref, atts_ref, awo_ref, awf_ref, awg_ref):
    step = pl.program_id(0)
    first = step == 0

    @pl.when(first)
    def _():
        gm_ref[...] = jnp.zeros_like(gm_ref)

    for b in range(B):
        image = step * B + b
        lanes = slice(TOK * b, TOK * (b + 1))
        ghid = ghid_ref[b]
        put_column(gm_ref, 3, image, ghid * brb_ref[b])
        gbb_ref[:, lanes] = (column(mods_ref, 5, image) * ghid).astype(BF)
        normed_b, inv_b = norm_parts(mid_ref[b])
        scale_b = 1.0 + column(mods_ref, 4, image)
        normed_ref[:, lanes] = (normed_b * scale_b + column(mods_ref, 3, image)).astype(BF)
        atts_ref[:, lanes] = att_ref[b]
        gnb = None
        for f in range(0, FF, FF_CHUNK):
            rows = slice(f, f + FF_CHUNK)
            act, slope = gelu_both(mm(wf_t_ref[rows, :], normed_ref[:, lanes]))
            act_ref[rows, lanes] = act.astype(BF)
            gact = mm(wg_ref[rows, :], gbb_ref[:, lanes])
            gpre_ref[rows, lanes] = (gact * slope).astype(BF)
            part = mm(wf_ref[:, rows], gpre_ref[rows, lanes])
            gnb = part if gnb is None else gnb + part
        put_column(gm_ref, 1, image, gnb)
        put_column(gm_ref, 2, image, gnb * normed_b)
        gmid = ghid + norm_back(gnb, normed_b, inv_b, scale_b)
        gmid_ref[b] = gmid
        out_bwd(b, image, lanes, gmid, bra_ref[b], column(mods_ref, 2, image), wo_ref, gba_ref, go_ref,
                gm_ref, 0)
    accumulate(awo_ref, mm_nt(atts_ref[...], gba_ref[...]), first)
    accumulate(awf_ref, mm_nt(normed_ref[...], gpre_ref[...]), first)
    accumulate(awg_ref, mm_nt(act_ref[...], gbb_ref[...]), first)

    @pl.when(step == pl.num_programs(0) - 1)
    def _():
        pack_outer(pack_ref, awo_ref, awf_ref, awg_ref, None)


def att_bwd_kernel(B, bottom, *refs):
    if bottom:
        (noisy_ref, wp_t_ref, pos_ref, qkv_ref, lse_ref, go_ref, gmid_ref, mods_ref, wqkv_ref,
         gm_ref, pack_ref, normed_ref, gqkv_ref, tok_ref, noi_ref, awqkv_ref, awp_ref) = refs
    else:
        (hid_ref, qkv_ref, lse_ref, go_ref, gmid_ref, mods_ref, wqkv_ref,
         ghid_ref, gm_ref, pack_ref, normed_ref, gqkv_ref, awqkv_ref) = refs
    step = pl.program_id(0)
    first = step == 0

    @pl.when(first)
    def _():
        gm_ref[...] = jnp.zeros_like(gm_ref)

    for b in range(B):
        image = step * B + b
        lanes = slice(TOK * b, TOK * (b + 1))
        hidden = mm(wp_t_ref[...], noisy_ref[b]) + pos_ref[...] if bottom else hid_ref[b]
        normed, inv = norm_parts(hidden)
        scale = 1.0 + column(mods_ref, 1, image)
        normed_ref[:, lanes] = (normed * scale + column(mods_ref, 0, image)).astype(BF)
        attention_backward(qkv_ref, b, lse_ref, go_ref, gqkv_ref, lanes)
        gna = mm(wqkv_ref[...], gqkv_ref[:, lanes])
        put_column(gm_ref, 0, image, gna)
        put_column(gm_ref, 1, image, gna * normed)
        ghid = gmid_ref[b] + norm_back(gna, normed, inv, scale)
        if bottom:
            tok_ref[:, lanes] = ghid.astype(BF)
            noi_ref[:, lanes] = noisy_ref[b]
        else:
            ghid_ref[b] = ghid
    accumulate(awqkv_ref, mm_nt(normed_ref[...], gqkv_ref[...]), first)
    if bottom:
        accumulate(awp_ref, mm_nt(noi_ref[...], tok_ref[...]), first)

    @pl.when(step == pl.num_programs(0) - 1)
    def _():
        pack_blocks(pack_ref, 0, awqkv_ref)
        used = 3 * D // pack_ref.shape[0]
        pack_ref[:, used:, :] = jnp.zeros_like(pack_ref[:, used:, :])
        if bottom:
            pack_ref[0, used : used + PATCH_IN, :] = awp_ref[...].astype(BF)


def whole(*shape):
    return pl.BlockSpec(shape, lambda i: (0,) * len(shape))


def images(B, *shape):
    return pl.BlockSpec((B,) + shape, lambda i: (i,) + (0,) * len(shape))


def sds(shape, dtype):
    return jax.ShapeDtypeStruct(shape, dtype)


def run_kernel(kernel, n, B, in_specs, outs, scratch, flops, args):
    out_specs = [spec for spec, _, _ in outs]
    out_shape = [sds(shape, dtype) for _, shape, dtype in outs]
    moved = sum(a.size * a.dtype.itemsize for a in args) + sum(
        math.prod(o.shape) * o.dtype.itemsize for o in out_shape
    )
    return pl.pallas_call(
        kernel,
        grid=(n // B,),
        in_specs=in_specs,
        out_specs=out_specs,
        out_shape=out_shape,
        scratch_shapes=[pltpu.VMEM(shape, dtype) for shape, dtype in scratch],
        compiler_params=pltpu.CompilerParams(vmem_limit_bytes=VMEM_LIMIT),
        cost_estimate=pl.CostEstimate(flops=flops, bytes_accessed=moved, transcendentals=0),
    )(*args)


MODS = whole(6 * D, 128)


def att_forward(noisy, wp_t, pos, mods, wqkv_t, wo_t, B):
    n = noisy.shape[0]
    T = B * TOK
    return run_kernel(
        functools.partial(att_fwd_kernel, B), n, B,
        [images(B, PATCH_IN, TOK), whole(D, PATCH_IN), whole(D, TOK), MODS, whole(3 * D, D), whole(D, D)],
        [(images(B, 3 * D, TOK), (n, 3 * D, TOK), BF), (images(B, 8, TOK), (n, 8, TOK), F32),
         (images(B, D, TOK), (n, D, TOK), BF), (images(B, D, TOK), (n, D, TOK), F32),
         (images(B, D, TOK), (n, D, TOK), F32)],
        [((D, T), BF), ((D, T), BF)],
        2 * n * TOK * (4 * D * D + 2 * D * TOK), (noisy, wp_t, pos, mods, wqkv_t, wo_t))


def ffn_forward(mid, mods, wf_t, wg_t, B):
    n = mid.shape[0]
    T = B * TOK
    return run_kernel(
        functools.partial(ffn_fwd_kernel, B), n, B,
        [images(B, D, TOK), MODS, whole(FF, D), whole(D, FF)],
        [(images(B, D, TOK), (n, D, TOK), F32), (images(B, D, TOK), (n, D, TOK), F32)],
        [((D, T), BF)],
        2 * n * TOK * 2 * D * FF, (mid, mods, wf_t, wg_t))


def block_step(hid, noise, mods, modf, wqkv_t, wo_t, wf_t, wg_t, wo, wf, wg, wy_t, wy, entries, B, pack):
    n = hid.shape[0]
    T = B * TOK
    return run_kernel(
        functools.partial(block_kernel, B, entries), n, B,
        [images(B, D, TOK), images(B, PATCH_IN, TOK), MODS, whole(2 * D, 128), whole(3 * D, D), whole(D, D),
         whole(FF, D), whole(D, FF), whole(D, D), whole(D, FF), whole(FF, D), whole(PATCH_IN, D),
         whole(D, PATCH_IN)],
        [(images(B, 3 * D, TOK), (n, 3 * D, TOK), BF), (images(B, 8, TOK), (n, 8, TOK), F32),
         (images(B, D, TOK), (n, D, TOK), BF), (images(B, D, TOK), (n, D, TOK), F32),
         (whole(4 * D, 128), (4 * D, 128), F32), (whole(2 * D, 128), (2 * D, 128), F32),
         (whole(PATCH_IN, TOK), (PATCH_IN, TOK), F32),
         (whole(*pack), pack, BF)],
        [((D, T), BF), ((D, T), BF), ((FF, TOK), F32), ((FF, T), BF), ((FF, T), BF), ((D, T), BF), ((D, T), BF),
         ((D, T), BF), ((PATCH_IN, T), BF), ((D, D), F32), ((D, FF), F32), ((FF, D), F32), ((PATCH_IN, D), F32)],
        2 * n * TOK * (4 * D * D + 2 * D * TOK + 6 * D * FF + 2 * D * D),
        (hid, noise, mods, modf, wqkv_t, wo_t, wf_t, wg_t, wo, wf, wg, wy_t, wy))


def ffn_backward(ghid, mid, att, bra, brb, mods, wf_t, wo, wf, wg, B, pack):
    n = mid.shape[0]
    T = B * TOK
    full = images(B, D, TOK)
    return run_kernel(
        functools.partial(ffn_bwd_kernel, B), n, B,
        [full, full, full, full, full, MODS, whole(FF, D), whole(D, D), whole(D, FF), whole(FF, D)],
        [(full, (n, D, TOK), BF), (full, (n, D, TOK), F32), (whole(4 * D, 128), (4 * D, 128), F32),
         (whole(*pack), pack, BF)],
        [((D, T), BF), ((FF, T), BF), ((FF, T), BF), ((D, T), BF), ((D, T), BF), ((D, T), BF),
         ((D, D), F32), ((D, FF), F32), ((FF, D), F32)],
        2 * n * TOK * (5 * D * FF + 2 * D * D), (ghid, mid, att, bra, brb, mods, wf_t, wo, wf, wg))


def att_backward(source, qkv, lse, go, gmid, mods, wqkv, B, bottom, pack):
    n = qkv.shape[0]
    T = B * TOK
    full = images(B, D, TOK)
    rest = [images(B, 3 * D, TOK), images(B, 8, TOK), full, full, MODS, whole(D, 3 * D)]
    tail = [(whole(2 * D, 128), (2 * D, 128), F32), (whole(*pack), pack, BF)]
    if bottom:
        ins = [images(B, PATCH_IN, TOK), whole(D, PATCH_IN), whole(D, TOK)] + rest
        outs = tail
        scratch = [((D, T), BF), ((3 * D, T), BF), ((D, T), BF), ((PATCH_IN, T), BF), ((D, 3 * D), F32),
                   ((PATCH_IN, D), F32)]
    else:
        ins = [full] + rest
        outs = [(full, (n, D, TOK), F32)] + tail
        scratch = [((D, T), BF), ((3 * D, T), BF), ((D, 3 * D), F32)]
    return run_kernel(
        functools.partial(att_bwd_kernel, B, bottom), n, B, ins, outs, scratch,
        2 * n * TOK * (6 * D * D + 5 * D * TOK), tuple(source) + (qkv, lse, go, gmid, mods, wqkv))

FREQ = 256
CLASSES = 1000
GRID = 16
LAYERS = 2
MOMENTUM = 0.9
LEARN = 30.0
DECAY = 0.7
IMAGES_PER_STEP = 2


def plan(steps_in):
    anchor = math.cos(0.5 * math.pi * 0.008 / 1.008)
    fraction = (steps_in.astype(F32) / 1000.0 + 0.008) / 1.008
    levels = jnp.cos(0.5 * math.pi * fraction)
    return levels * levels / (anchor * anchor)


def time_features(steps_in):
    half_width = FREQ // 2
    frequencies = jnp.exp(-math.log(10000.0) * jnp.arange(half_width, dtype=F32) / half_width)
    angles = steps_in.astype(F32)[:, None] * frequencies[None, :]
    return jnp.concatenate([jnp.cos(angles), jnp.sin(angles)], axis=1)


def positions():
    quarter = D // 4
    omegas = jnp.exp(-math.log(10000.0) * jnp.arange(quarter, dtype=F32) / quarter)
    places = jnp.arange(GRID * GRID, dtype=jnp.int32)
    column = omegas[:, None] * (places % GRID).astype(F32)[None, :]
    row_pos = omegas[:, None] * (places // GRID).astype(F32)[None, :]
    return jnp.concatenate(
        [jnp.sin(column), jnp.cos(column), jnp.sin(row_pos), jnp.cos(row_pos)], axis=0
    )


def swish_act(values):
    return values / (1.0 + jnp.exp(-values))


def swish_slope(values):
    s = 1.0 / (1.0 + jnp.exp(-values))
    return s * (1.0 + values * (1.0 - s))


def advance(weight, moment, average, gradient):
    new_moment = MOMENTUM * moment + gradient
    new_weight = weight - LEARN * (gradient + MOMENTUM * new_moment)
    new_average = DECAY * average + (1.0 - DECAY) * new_weight
    return (new_weight, new_moment, new_average)


def swap(x, axis, mask):
    pairs = [(i, i ^ mask) for i in range(lax.axis_size(axis))]
    return lax.ppermute(x, axis, pairs)


def digit_list(n):
    found, shift = [], 0
    while (1 << shift) < n:
        left = n >> shift
        size = 2 if shift == 0 or left == 2 else 4
        found.append((shift, size))
        shift += size.bit_length() - 1
    return found


def place_of(index, n):
    place = 0
    for shift, size in digit_list(n):
        place = place * size + ((index >> shift) & (size - 1))
    return place


def pick(x, index, axis=0):
    return lax.dynamic_index_in_dim(x, index, axis, keepdims=False)


def add_low(parts):
    total = parts[0].astype(F32)
    for part in parts[1:]:
        total = total + part.astype(F32)
    return total.astype(BF)


def spread(piece, n):
    pieces = {0: piece}
    digits = digit_list(n)
    for shift, size in digits[1:] + digits[:1]:
        known = dict(pieces)
        for j in range(1, size):
            for mask, value in known.items():
                pieces[mask ^ (j << shift)] = swap(value, "rep", j << shift)
    return pieces


def gather_rows(rows):
    nr, ng = lax.axis_size("rep"), lax.axis_size("grp")
    cur = jnp.concatenate([rows] + [swap(rows, "grp", k) for k in range(1, ng)], axis=0)
    digits = digit_list(nr)
    for shift, size in digits[1:] + digits[:1]:
        cur = jnp.concatenate([cur] + [swap(cur, "rep", j << shift) for j in range(1, size)], axis=0)
    return cur


def gather_start(shard):
    nr, ng = lax.axis_size("rep"), lax.axis_size("grp")
    rows = shard.shape[0] // nr
    me = lax.axis_index("rep")
    mine = lax.dynamic_slice_in_dim(shard, place_of(me, nr) * rows, rows, 0)
    got = [swap(mine, "grp", k) for k in range(1, ng)]
    if not got:
        return {}
    return spread(jnp.stack(got), nr)


def place_table():
    nr, ng = lax.axis_size("rep"), lax.axis_size("grp")
    me, member = lax.axis_index("rep"), lax.axis_index("grp")
    entries = [place_of(me ^ mask, nr) for mask in range(nr)] + [member ^ k for k in range(ng)]
    return jnp.stack([jnp.asarray(e, jnp.int32) for e in entries])


def reduce_rows(packed):
    nr, ng = lax.axis_size("rep"), lax.axis_size("grp")
    me, member = lax.axis_index("rep"), lax.axis_index("grp")
    cur = packed
    for shift, size in digit_list(nr):
        digit = (me >> shift) & (size - 1)
        cut = cur.reshape(ng, size, cur.shape[1] // size, D)
        got = [swap(pick(cut, digit ^ j, 1), "rep", j << shift) for j in range(1, size)]
        cur = add_low([pick(cut, digit, 1)] + got)
    got = [swap(pick(cur, member ^ k), "grp", k) for k in range(1, ng)]
    return add_low([pick(cur, member)] + got)


def assemble_shard_kernel(masks, table_ref, *refs):
    out_ref = refs[-1]
    for mask, ref in zip(masks, refs[:-1]):
        rows = ref.shape[0]
        out_ref[pl.ds(pl.multiple_of(table_ref[mask] * rows, rows), rows), :] = ref[...]


def in_vmem():
    return pl.BlockSpec(memory_space=pltpu.VMEM)


def assemble_shard(piece, table):
    nr = lax.axis_size("rep")
    pieces = spread(piece, nr)
    masks = tuple(sorted(pieces))
    return pl.pallas_call(
        functools.partial(assemble_shard_kernel, masks),
        in_specs=[pl.BlockSpec(memory_space=pltpu.SMEM)] + [in_vmem()] * len(masks),
        out_specs=in_vmem(),
        out_shape=sds((piece.shape[0] * nr, D), BF),
    )(table, *[pieces[m] for m in masks])


def assemble_kernel(masks, nr, layout, table_ref, shard_ref, *refs):
    pieces, rest = refs[: len(masks)], refs[len(masks) :]
    outs, full_ref = list(rest[:-1]), rest[-1]
    ng = full_ref.shape[0]
    full_ref[table_ref[nr]] = shard_ref[...]
    for mask, ref in zip(masks, pieces):
        rows = ref.shape[1]
        at = pl.ds(pl.multiple_of(table_ref[mask] * rows, rows), rows)
        for k in range(1, ng):
            full_ref[table_ref[nr + k], at, :] = ref[k - 1]
    step = D // ng
    for kind, start, size in layout:
        if kind == "rows":
            outs.pop(0)[...] = full_ref[:, start : start + size, :]
        elif kind == "blocks":
            out_ref = outs.pop(0)
            for g in range(ng):
                for c in range(size):
                    out_ref[step * g : step * (g + 1), D * c : D * (c + 1)] = full_ref[
                        g, start + step * c : start + step * (c + 1), :
                    ]
            flip_ref = outs.pop(0)
            flip_ref[...] = out_ref[...].T
        else:
            wo_ref, wg_ref = outs.pop(0), outs.pop(0)
            wide = (D + FF) // ng
            for g in range(ng):
                low, high = wide * g, wide * (g + 1)
                if low < D:
                    cut = min(high, D)
                    wo_ref[low:cut, :] = full_ref[g, start : start + cut - low, :]
                if high > D:
                    cut = max(low, D)
                    wg_ref[cut - D : high - D, :] = full_ref[g, start + cut - low : start + wide, :]
            outs.pop(0)[...] = wo_ref[...].T
            outs.pop(0)[...] = wg_ref[...].T


def assemble(shard, pieces, table, layout):
    nr, ng = lax.axis_size("rep"), lax.axis_size("grp")
    masks = tuple(sorted(pieces))
    out_shape = []
    for kind, _, size in layout:
        if kind == "rows":
            out_shape.append(sds((ng, size, D), BF))
        elif kind == "blocks":
            out_shape += [sds((D, size * D), BF), sds((size * D, D), BF)]
        else:
            out_shape += [sds(s, BF) for s in ((D, D), (FF, D), (D, D), (D, FF))]
    return pl.pallas_call(
        functools.partial(assemble_kernel, masks, nr, layout),
        in_specs=[pl.BlockSpec(memory_space=pltpu.SMEM)] + [in_vmem()] * (1 + len(masks)),
        out_specs=[in_vmem()] * len(out_shape),
        out_shape=out_shape,
        scratch_shapes=[pltpu.VMEM((ng,) + shard.shape, BF)],
        compiler_params=pltpu.CompilerParams(vmem_limit_bytes=VMEM_LIMIT),
    )(table, shard, *[pieces[m] for m in masks])


def pad_rows(x, multiple):
    short = -x.shape[0] % multiple
    return jnp.pad(x, ((0, short), (0, 0))) if short else x


def column_blocks(low, first, count):
    return [low[:, D * c : D * (c + 1)] for c in range(first, first + count)]


def local(
    latents, noise, timesteps, labels, emb_table, emb_mom, emb_ema, w_in, in_mom, in_ema,
    w_out, out_mom, out_ema, head, head_mom, head_ema,
):
    nr, ng = lax.axis_size("rep"), lax.axis_size("grp")
    member = lax.axis_index("grp")
    n = latents.shape[0]
    B = IMAGES_PER_STEP
    unit = 16 * nr
    rows_d = D // ng
    rows_out = (D + FF) // ng
    emb_rows = emb_table.shape[0]
    emb_pad = -(-emb_rows // 16) * 16
    low_emb, low_in, low_out, low_head = (a.astype(BF) for a in (emb_table, w_in, w_out, head))
    table = place_table()
    shard1 = pad_rows(
        jnp.concatenate([pad_rows(low_emb, 16)] + column_blocks(low_in[0], 0, 9), axis=0), unit
    )
    shard2 = pad_rows(jnp.concatenate([low_out[0]] + column_blocks(low_in[0], 9, 4), axis=0), unit)
    wy_block = jnp.pad(low_head[:, 2 * D :], ((0, 0), (0, D - PATCH_IN)))
    shard3 = pad_rows(
        jnp.concatenate(
            column_blocks(low_in[1], 0, 9) + column_blocks(low_head, 0, 2) + [wy_block], axis=0
        ),
        unit,
    )
    shard4 = pad_rows(jnp.concatenate([low_out[1]] + column_blocks(low_in[1], 9, 4), axis=0), unit)
    pieces1, pieces2, pieces3, pieces4 = (gather_start(s) for s in (shard1, shard2, shard3, shard4))

    levels = plan(timesteps)
    noise_level = jnp.sqrt(jnp.maximum(1.0 - levels, 0.0))
    noisy = (
        jnp.sqrt(levels)[:, None, None] * latents.astype(F32)
        + noise_level[:, None, None] * noise.astype(F32)
    ).astype(BF)
    time_feats = time_features(timesteps).astype(BF)
    one_hot = (labels[:, None] == jnp.arange(CLASSES, dtype=jnp.int32)[None, :]).astype(BF)
    pos = positions()

    emb3, wa0, wa0_t, wqkv0, wqkv0_t = assemble(
        shard1, pieces1, table,
        (("rows", 0, emb_pad), ("blocks", emb_pad, 6), ("blocks", emb_pad + 6 * rows_d, 3)),
    )
    emb_full = emb3[:, :emb_rows].reshape(ng * emb_rows, D)
    w_patch = emb_full[:PATCH_IN]
    w_time1 = emb_full[PATCH_IN : PATCH_IN + FREQ]
    w_time2 = emb_full[PATCH_IN + FREQ : PATCH_IN + FREQ + D]
    w_class = emb_full[PATCH_IN + FREQ + D :]
    pre_time = jnp.dot(time_feats, w_time1, preferred_element_type=F32)
    time_act = swish_act(pre_time).astype(BF)
    condition = jnp.dot(time_act, w_time2, preferred_element_type=F32) + jnp.dot(
        one_hot, w_class, preferred_element_type=F32
    )
    cond_act = swish_act(condition).astype(BF)

    def mods_of(weights_t):
        columns = lax.dot_general(
            weights_t, cond_act, (((1,), (1,)), ((), ())), preferred_element_type=F32
        )
        return jnp.pad(columns, ((0, 0), (0, 128 - n)))

    mods0 = mods_of(wa0_t)
    wp_t = w_patch.T
    wo0, wg0, wo0_t, wg0_t, wf0, wf0_t = assemble(
        shard2, pieces2, table, (("outer", 0, 0), ("blocks", rows_out, 4))
    )
    qkv0, lse0, att0, bra0, mid0 = att_forward(noisy, wp_t, pos, mods0, wqkv0_t, wo0_t, B)
    brb0, hid1 = ffn_forward(mid0, mods0, wf0_t, wg0_t, B)
    wa1, wa1_t, wqkv1, wqkv1_t, wm, wm_t, wy_wide, wy_wide_t = assemble(
        shard3, pieces3, table,
        (("blocks", 0, 6), ("blocks", 6 * rows_d, 3), ("blocks", 9 * rows_d, 2),
         ("blocks", 11 * rows_d, 1)),
    )
    wo1, wg1, wo1_t, wg1_t, wf1, wf1_t = assemble(
        shard4, pieces4, table, (("outer", 0, 0), ("blocks", rows_out, 4))
    )
    mods1 = mods_of(wa1_t)
    modf = mods_of(wm_t)
    wy = wy_wide[:, :PATCH_IN]
    wy_t = wy_wide_t[:PATCH_IN]
    entries = n * nr * ng * TOK * PATCH_IN
    outer_rows = -(-(rows_out + FF // ng + PATCH_IN) // unit) * unit
    qkv_rows = -(-(3 * rows_d + PATCH_IN) // unit) * unit
    outer_pack = (ng, outer_rows, D)
    qkv_pack = (ng, qkv_rows, D)
    qkv1, lse1, go1, gmid1, gm1, gmf, squares, pack_f1 = block_step(
        hid1, noise, mods1, modf, wqkv1_t, wo1_t, wf1_t, wg1_t, wo1, wf1, wg1, wy_t, wy,
        float(entries), B, outer_pack,
    )
    ghid1, gma1, pack_a1 = att_backward((hid1,), qkv1, lse1, go1, gmid1, mods1, wqkv1, B, False, qkv_pack)
    piece_f1 = reduce_rows(pack_f1)
    gm_rows1 = jnp.concatenate([gma1, gm1], axis=0)[:, :n].T
    gf_rows = gmf[:, :n].T
    loss_sum = jnp.sum(squares)
    loss_parts = []
    for _ in range(3):
        part = loss_sum.astype(BF)
        loss_parts.append(part)
        loss_sum = loss_sum - part.astype(F32)
    loss_row = jnp.stack(loss_parts)[None, :] * jnp.where(jnp.arange(n) == 0, 1.0, 0.0).astype(BF)[:, None]
    rows1 = gather_rows(
        jnp.concatenate([cond_act, gm_rows1.astype(BF), gf_rows.astype(BF), loss_row], axis=1)
    )
    go0, gmid0, gm0, pack_f0 = ffn_backward(
        ghid1, mid0, att0, bra0, brb0, mods0, wf0_t, wo0, wf0, wg0, B, outer_pack
    )
    piece_a1 = reduce_rows(pack_a1)
    gma0, pack_a0 = att_backward(
        (noisy, wp_t, pos), qkv0, lse0, go0, gmid0, mods0, wqkv0, B, True, qkv_pack
    )
    piece_f0 = reduce_rows(pack_f0)
    piece_a0 = reduce_rows(pack_a0)

    gm_rows0 = jnp.concatenate([gma0, gm0], axis=0)[:, :n].T

    def low_dot(left, right):
        return jnp.dot(left.astype(BF), right, preferred_element_type=F32)

    gcond_act = low_dot(gf_rows, wm_t) + low_dot(gm_rows1, wa1_t) + low_dot(gm_rows0, wa0_t)
    gcond = gcond_act * swish_slope(condition)
    gpre_time = low_dot(gcond, w_time2.T) * swish_slope(pre_time)
    label_parts = jnp.stack([labels >> 5, labels & 31], axis=1).astype(BF)
    rows0 = gather_rows(
        jnp.concatenate(
            [time_act, gcond.astype(BF), gpre_time.astype(BF), time_feats, gm_rows0.astype(BF), label_parts],
            axis=1,
        )
    )
    shard_f1, shard_a1, shard_f0, shard_a0 = (
        assemble_shard(piece, table) for piece in (piece_f1, piece_a1, piece_f0, piece_a0)
    )

    cond_all = lax.dynamic_slice_in_dim(rows1[:, :D], member * rows_d, rows_d, 1)

    def tall_dot(left, right):
        return lax.dot_general(left, right, (((0,), (0,)), ((), ())), preferred_element_type=F32)

    ga1 = tall_dot(cond_all, rows1[:, D : 7 * D])
    gm_head = tall_dot(cond_all, rows1[:, 7 * D : 9 * D])
    loss_value = jnp.sum(rows1[:, 9 * D :].astype(F32)) / entries
    at = 3 * D + FREQ
    ga0 = tall_dot(cond_all, rows0[:, at : at + 6 * D])
    split_labels = rows0[:, at + 6 * D :].astype(jnp.int32)
    all_labels = split_labels[:, 0] * 32 + split_labels[:, 1]
    class_hot = (all_labels[:, None] == jnp.arange(CLASSES, dtype=jnp.int32)[None, :]).astype(BF)
    left = jnp.concatenate(
        [jnp.zeros((rows0.shape[0], PATCH_IN), BF), rows0[:, 3 * D : at], rows0[:, :D], class_hot], axis=1
    )
    left = lax.dynamic_slice_in_dim(left, member * emb_rows, emb_rows, 1)
    row_id = member * emb_rows + jnp.arange(emb_rows, dtype=jnp.int32)
    emb_grad = jnp.where(
        (row_id < PATCH_IN + FREQ)[:, None],
        tall_dot(left, rows0[:, 2 * D : 3 * D]),
        tall_dot(left, rows0[:, D : 2 * D]),
    )
    patch_grad = shard_a0[3 * rows_d : 3 * rows_d + PATCH_IN].astype(F32)
    emb_grad = emb_grad + jnp.pad(patch_grad, ((0, emb_rows - PATCH_IN), (0, 0)))

    def wide(shard, start, count):
        blocks = shard[start : start + count * rows_d].reshape(count, rows_d, D)
        return blocks.transpose(1, 0, 2).reshape(rows_d, count * D).astype(F32)

    in_grad = jnp.stack(
        [
            jnp.concatenate([ga0, wide(shard_a0, 0, 3), wide(shard_f0, rows_out, 4)], axis=1),
            jnp.concatenate([ga1, wide(shard_a1, 0, 3), wide(shard_f1, rows_out, 4)], axis=1),
        ]
    )
    out_grad = jnp.stack([shard_f0[:rows_out], shard_f1[:rows_out]]).astype(F32)
    wy_rows = rows_out + FF // ng
    wy_grad = lax.dynamic_slice_in_dim(
        shard_f1[wy_rows : wy_rows + PATCH_IN], member * rows_d, rows_d, 1
    ).T.astype(F32)
    head_grad = jnp.concatenate([gm_head, wy_grad], axis=1)
    emb_new = advance(emb_table, emb_mom, emb_ema, emb_grad)
    in_new = advance(w_in, in_mom, in_ema, in_grad)
    out_new = advance(w_out, out_mom, out_ema, out_grad)
    head_new = advance(head, head_mom, head_ema, head_grad)
    return (loss_value, *emb_new, *in_new, *out_new, *head_new)


def solution(mesh):
    data = P(("rep", "grp"), None, None)
    vector = P(("rep", "grp"))
    flat = P("grp", None)
    deep = P(None, "grp", None)
    return jax.shard_map(
        local,
        mesh=mesh,
        in_specs=(data, data, vector, vector, flat, flat, flat, deep, deep, deep, deep, deep, deep,
                  flat, flat, flat),
        out_specs=(P(), flat, flat, flat, deep, deep, deep, deep, deep, deep, flat, flat, flat),
        check_vma=False,
    )
```

time: 1010 us -> 604 us (0.60)
  waiting for transfers between devices: 444 us -> 90.7 us
  Pallas kernels: 0 us -> 224 us
  matrix products: 239 us -> 19.1 us
  blocking collectives: 148 us -> 0 us
  starting transfers between devices: 7.43 us -> 106 us
  local copies, waits for them, and re-layouts: 39.6 us -> 116 us
  other arithmetic: 99.6 us -> 31.3 us
  between operations: 19.2 us -> 5.61 us
    pallas_call x0 -> x14, Pallas kernels: none -> 224 us  [the longest x6 195 us: run_kernel(): pl.pallas_call(kernel, grid=(n // B,), in_specs=in_specs, out_specs=out_s...]
    dot_general x57 -> x15, matrix products: 239 us -> 19.1 us  [the longest x5 8.46 us: tall_dot(): lax.dot_general(left, right, (((0,), (0,)), ((), ())), preferred_element_...]
    reduce_scatter x3 -> x0, waiting for transfers between devices: 208 us -> none  [the longest x1 208 us: local(): lax.psum_scatter(stacked_in, 'grp', scatter_dimension=1, tiled=True)]
    all_gather x3 -> x0, waiting for transfers between devices: 168 us -> none  [the longest x1 131 us: local(): lax.all_gather(low_in, 'grp', axis=1, tiled=True)]
    ppermute x0 -> x110, starting transfers between devices: none -> 106 us  [swap(): return lax.ppermute(x, axis, pairs)]
    ppermute x0 -> x110, waiting for transfers between devices: none -> 90.7 us  [swap(): return lax.ppermute(x, axis, pairs)]
    unnamed x1 -> x0, blocking collectives: 77.3 us -> none
    psum x1 -> x0, waiting for transfers between devices: 67.8 us -> none  [local(): lax.psum((shards[0], shards[1], shards[2], shards[3]), 'rep')]
  transfers between devices with their start and end apart: 8 -> 110, of which waited for: 6 -> 27; matrix products, arithmetic and copies ran while one was open for 27% -> 20% of each run, Pallas kernels for 0% -> 14%
where the time goes in v1:
time: 604 us; the launch traced here: 592 us
  Pallas kernels  224 us (37%)
  local copies, waits for them, and re-layouts  116 us (19%)
  starting transfers between devices  106 us (18%)
  waiting for transfers between devices  90.7 us (15%)
  other arithmetic  31.3 us (5%)
  matrix products  19.1 us (3%)
    pallas_call x6, Pallas kernels, run_kernel(): pl.pallas_call(kernel, grid=(n // B,), in_specs=in_specs, out_specs=out_s...  195 us
    ppermute x110, starting transfers between devices, swap(): return lax.ppermute(x, axis, pairs)  106 us
    ppermute x110, waiting for transfers between devices, swap(): return lax.ppermute(x, axis, pairs)  90.7 us
    unnamed x228, local copies, waits for them, and re-layouts  31.7 us
    concatenate x6, local copies, waits for them, and re-layouts, gather_rows(): jnp.concatenate([cur] + [swap(cur, 'rep', j << shift) for j in range(1, s...  23.8 us
    ppermute x12, local copies, waits for them, and re-layouts, swap(): return lax.ppermute(x, axis, pairs)  21.4 us
    pallas_call x4, Pallas kernels, assemble(): pl.pallas_call(functools.partial(assemble_kernel, masks, nr, layout), in_...  20.8 us
  transfers between devices with their start and end apart: 110, of which 27 were waited for; matrix products, arithmetic and copies ran while one was open for 20% of the time, Pallas kernels for 14%

profile of v1, /device:TPU:0, one launch (start us, length us, event | category | flops | bytes accessed | tf_op | source)
XLA Modules:
  0.0 592.0 jit_solution(9116576744572591088)
XLA Ops:
  11.0 3.1 collective-permute-start.30
  19.6 3.5 collective-permute-start.11
  28.5 3.8 collective-permute-start.22
  32.5 7.7 %collective-permute-done.12 = bf16[112,384]{1,0:T(8,128)(2,1)S(1)} collective-permute-done((bf16[112,384]{1,0:T(8,128)(2,1)S(1)}, bf16[112,384]{1,0:T(8,128)(2,1)S(1)}, u32[]{:S(2)}, u32[]{:S(2)}) %collective-permute-start.12) | collective-permute-done | bytes 86048 | tf_op jit(solution)/shard_map/ppermute | solution.py:544
  43.6 3.5 collective-permute-start.1
  49.6 5.4 collective-permute-done.1
  60.3 3.8 collective-permute-done.14.refs_2_
  65.5 4.9 collective-permute-done.16.refs_4_
  78.2 6.4 %collective-permute-done.26.refs_4_ = bf16[3,144,384]{2,1,0:T(8,128)(2,1)} collective-permute-done((bf16[3,144,384]{2,1,0:T(8,128)(2,1)S(1)}, bf16[3,144,384]{2,1,0:T(8,128)(2,1)}, u32[]{:S(2)}, u32[]{:S(2)}) %collective-permute-start.26) | collective-permute-done | bytes 331808 | tf_op jit(solution)/shard_map/ppermute | solution.py:544
  87.2 4.6 collective-permute-done.4.refs_2_
  91.8 8.6 %collective-permute-done.6.refs_4_ = bf16[3,160,384]{2,1,0:T(8,128)(2,1)S(1)} collective-permute-done((bf16[3,160,384]{2,1,0:T(8,128)(2,1)S(1)}, bf16[3,160,384]{2,1,0:T(8,128)(2,1)S(1)}, u32[]{:S(2)}, u32[]{:S(2)}) %collective-permute-start.6) | collective-permute-done | bytes 368672 | tf_op jit(solution)/shard_map/ppermute | solution.py:544
  108.9 4.8 shard_map.260
  113.7 4.8 shard_map.256
  119.2 5.7 shard_map.259
  127.7 5.6 shard_map.255
  143.9 21.7 %shard_map.257 = (bf16[8,1152,256]{2,1,0:T(8,128)(2,1)}, f32[8,8,256]{2,1,0:T(8,128)}, bf16[8,384,256]{2,1,0:T(8,128)(2,1)}, f32[8,384,256]{2,1,0:T(8,128)}, f32[8,384,256]{2,1,0:T(8,128)}) custom-call(bf16[8,16,256]{2,1,0:T(8,128)(2,1)} %add_convert_fusion.noisy_ref.refs_0_, bf16[384,16]{1,0:T(8,128)(2,1)} %bitcast.244, ...), custom_call_target="tpu_custom_call" | custom-call | flops 3221225472 | bytes 15478784 | tf_op jit(solution)/shard_map/pallas_call | solution.py:400
  165.7 12.6 %shard_map.258 = (f32[8,384,256]{2,1,0:T(8,128)}, f32[8,384,256]{2,1,0:T(8,128)}) custom-call(f32[8,384,256]{2,1,0:T(8,128)} %get-tuple-element.63.mid_ref, f32[2304,128]{1,0:T(8,128)} %pad.34.mods_ref.refs_7_, bf16[1536,384]{1,0:T(8,128)(2,1)} %get-tuple-element.64.wf_t_ref, bf16[384,1536]{1,0:T(8,128)(2,1)} %get-tuple-element.65.wg_t_ref), custom_call_target="tpu_custom_call" | custom-call | flops 4831838208 | bytes 12976128 | tf_op jit(solution)/shard_map/pallas_call | solution.py:400
  178.3 68.6 %shard_map.261 = (bf16[8,1152,256]{2,1,0:T(8,128)(2,1)}, f32[8,8,256]{2,1,0:T(8,128)}, bf16[8,384,256]{2,1,0:T(8,128)(2,1)}, f32[8,384,256]{2,1,0:T(8,128)}, f32...) custom-call(f32[8,384,256]{2,1,0:T(8,128)} %get-tuple-element.66.hid_ref.refs_0_, ...), custom_call_target="tpu_custom_call" | custom-call | flops 18924699648 | bytes 24453120 | tf_op jit(solution)/shard_map/pallas_call | solution.py:400
  246.9 27.2 %shard_map.262 = (f32[8,384,256]{2,1,0:T(8,128)}, f32[768,128]{1,0:T(8,128)}, bf16[4,384,384]{2,1,0:T(8,128)(2,1)}) custom-call(f32[8,384,256]{2,1,0:T(8,128)} %get-tuple-element.66.hid_ref.refs_0_, bf16[8,1152,256]{2,1,0:T(8,128)(2,1)} %get-tuple-element.78.refs_1_, f32[8,8,256]{2,1,0:T(8,128)} %get-tuple-element.79.refs_2_, ...), custom_call_target="tpu_custom_call" | custom-call | flops 5637144576 | bytes 19431424 | tf_op jit(solution)/shard_map/pallas_call | solution.py:400
  287.4 36.0 %shard_map.263 = (bf16[8,384,256]{2,1,0:T(8,128)(2,1)}, f32[8,384,256]{2,1,0:T(8,128)}, f32[1536,128]{1,0:T(8,128)}, bf16[4,896,384]{2,1,0:T(8,128)(2,1)}) custom-call(f32[8,384,256]{2,1,0:T(8,128)} %get-tuple-element.89.ghid_ref, f32[8,384,256]{2,1,0:T(8,128)} %get-tuple-element.63.mid_ref, bf16[8,384,256]{2,1,0:T(8,128)(2,1)} %get-tuple-element.90.att_ref, ...), custom_call_target="tpu_custom_call" | custom-call | flops 13287555072 | bytes 27426816 | tf_op jit(solution)/shard_map/pallas_call | solution.py:400
  323.4 29.2 %shard_map.264 = (f32[768,128]{1,0:T(8,128)}, bf16[4,384,384]{2,1,0:T(8,128)(2,1)}) custom-call(bf16[8,16,256]{2,1,0:T(8,128)(2,1)} %add_convert_fusion.noisy_ref.refs_0_, bf16[384,16]{1,0:T(8,128)(2,1)} %bitcast.245, f32[384,256]{1,0:T(8,128)} %pad_maximum_fusion.5.pos_ref.refs_2_, bf16[8,1152,256]{2,1,0:T(8,128)(2,1)} %get-tuple-element.87.refs_3_, ...), custom_call_target="tpu_custom_call" | custom-call | flops 5637144576 | bytes 13611008 | tf_op jit(solution)/shard_map/pallas_call | solution.py:400
  360.9 5.0 concatenate.80
  390.0 3.4 collective-permute-done.44
  400.7 4.4 collective-permute-done.51
  414.8 3.3 collective-permute-done.56
  484.6 8.4 %concatenate.78 = bf16[256,3459]{0,1:T(8,128)(2,1)} concatenate(bf16[8,3459]{0,1:T(8,128)(2,1)S(1)} %pad_maximum_fusion.1, bf16[8,3459]{0,1:T(8,128)(2,1)S(1)} %copy.233, bf16[8,3459]{0,1:T(8,128)(2,1)} %copy.234, bf16[8,3459]{0,1:T(8,128)(2,1)} %copy.235, bf16[32,3459]{0,1:T(8,128)(2,1)} %copy.236, bf16[32,3459]{0,1:T(8,128)(2,1)} %copy.237, bf16[32,3459]{0,1:T(8,128)(2,1)} %copy.238, ...), dimensions={0} | concatenate | bytes 3542016 | tf_op jit(solution)/shard_map/concatenate | solution.py:591
  500.7 8.2 %concatenate.83 = bf16[256,3714]{0,1:T(8,128)(2,1)S(1)} concatenate(bf16[8,3714]{0,1:T(8,128)(2,1)S(1)} %concatenate.80, bf16[8,3714]{0,1:T(8,128)(2,1)} %copy.258, bf16[8,3714]{0,1:T(8,128)(2,1)} %copy.259, bf16[8,3714]{0,1:T(8,128)(2,1)} %copy.260, bf16[32,3714]{0,1:T(8,128)(2,1)} %copy.261, bf16[32,3714]{0,1:T(8,128)(2,1)} %copy.262, bf16[32,3714]{0,1:T(8,128)(2,1)} %copy.263, ...), dimensions={0} | concatenate | bytes 3803136 | tf_op jit(solution)/shard_map/concatenate | solution.py:591
  522.3 3.4 collective-permute-done.97
  527.3 7.1 %collective-permute-done.98 = bf16[4,112,384]{2,1,0:T(8,128)(2,1)S(1)} collective-permute-done((bf16[4,112,384]{2,1,0:T(8,128)(2,1)S(1)}, bf16[4,112,384]{2,1,0:T(8,128)(2,1)S(1)}, u32[]{:S(2)}, u32[]{:S(2)}) %collective-permute-start.98) | collective-permute-done | bytes 344096 | tf_op jit(solution)/shard_map/ppermute | solution.py:544
  537.4 3.1 collective-permute-done.69
  542.6 5.4 collective-permute-done.70
  585.7 5.0 multiply_add_fusion
  (594 shorter events, 258.5 us)
Async XLA Ops:
  11.0 16.9 %collective-permute-start.30 = (bf16[112,384]{1,0:T(8,128)(2,1)S(1)}, bf16[112,384]{1,0:T(8,128)(2,1)S(1)}, u32[]{:S(2)}, u32[]{:S(2)}) collective-permute-start(bf16[112,384]{1,0:T(8,128)(2,1)S(1)} %constant_dynamic-slice_fusion.1), channel_id=1, source_target_pairs={{0,1},{1,0},{2,3},{3,2},{4,5},{5,4},{6,7},{7,6},{8,9},{9,8},{10,11... | collective-permute-start | bytes 258056 | tf_op jit(solution)/shard_map/ppermute | solution.py:544
  40.1 16.4 %collective-permute-start.34 = (bf16[3,112,384]{2,1,0:T(8,128)(2,1)S(1)}, bf16[3,112,384]{2,1,0:T(8,128)(2,1)S(1)}, u32[]{:S(2)}, u32[]{:S(2)}) collective-permute-start(bf16[3,112,384]{2,1,0:T(8,128)(2,1)S(1)} %pad_maximum_fusion.12.refs_0_), channel_id=1, source_target_pairs={{0,8},{4,12},{8,0},{12,4},{16,24},{20,28},{24,16},{28,20},{1,9},{5... | collective-permute-start | bytes 774152 | tf_op jit(solution)/shard_map/ppermute | solution.py:544
  41.6 16.4 %collective-permute-start.36 = (bf16[3,112,384]{2,1,0:T(8,128)(2,1)S(1)}, bf16[3,112,384]{2,1,0:T(8,128)(2,1)S(1)}, u32[]{:S(2)}, u32[]{:S(2)}) collective-permute-start(bf16[3,112,384]{2,1,0:T(8,128)(2,1)S(1)} %pad_maximum_fusion.12.refs_0_), channel_id=1, source_target_pairs={{0,16},{4,20},{8,24},{12,28},{16,0},{20,4},{24,8},{28,12},{1,17},{... | collective-permute-start | bytes 774152 | tf_op jit(solution)/shard_map/ppermute | solution.py:544
  58.7 18.0 %collective-permute-start.24 = (bf16[3,144,384]{2,1,0:T(8,128)(2,1)S(1)}, bf16[3,144,384]{2,1,0:T(8,128)(2,1)S(1)}, u32[]{:S(2)}, u32[]{:S(2)}) collective-permute-start(bf16[3,144,384]{2,1,0:T(8,128)(2,1)S(1)} %pad_maximum_fusion.10.refs_0_), channel_id=1, source_target_pairs={{0,8},{4,12},{8,0},{12,4},{16,24},{20,28},{24,16},{28,20},{1,9},{5... | collective-permute-start | bytes 995336 | tf_op jit(solution)/shard_map/ppermute | solution.py:544
  64.0 20.7 %collective-permute-start.26 = (bf16[3,144,384]{2,1,0:T(8,128)(2,1)S(1)}, bf16[3,144,384]{2,1,0:T(8,128)(2,1)}, u32[]{:S(2)}, u32[]{:S(2)}) collective-permute-start(bf16[3,144,384]{2,1,0:T(8,128)(2,1)S(1)} %pad_maximum_fusion.10.refs_0_), channel_id=1, source_target_pairs={{0,16},{4,20},{8,24},{12,28},{16,0},{20,4},{24,8},{28,12},{1,17},{... | collective-permute-start | bytes 995336 | tf_op jit(solution)/shard_map/ppermute | solution.py:544
  70.4 15.9 %collective-permute-start.28 = (bf16[3,144,384]{2,1,0:T(8,128)(2,1)S(1)}, bf16[3,144,384]{2,1,0:T(8,128)(2,1)S(1)}, u32[]{:S(2)}, u32[]{:S(2)}) collective-permute-start(bf16[3,144,384]{2,1,0:T(8,128)(2,1)S(1)} %pad_maximum_fusion.10.refs_0_), channel_id=1, source_target_pairs={{0,24},{4,28},{8,16},{12,20},{16,8},{20,12},{24,0},{28,4},{1,25},{... | collective-permute-start | bytes 995336 | tf_op jit(solution)/shard_map/ppermute | solution.py:544
  72.1 19.7 %collective-permute-start.4 = (bf16[3,160,384]{2,1,0:T(8,128)(2,1)S(1)}, bf16[3,160,384]{2,1,0:T(8,128)(2,1)S(1)}, u32[]{:S(2)}, u32[]{:S(2)}) collective-permute-start(bf16[3,160,384]{2,1,0:T(8,128)(2,1)S(1)} %pad_maximum_fusion.8.refs_0_), channel_id=1, source_target_pairs={{0,8},{4,12},{8,0},{12,4},{16,24},{20,28},{24,16},{28,20},{1,9},{5... | collective-permute-start | bytes 1105928 | tf_op jit(solution)/shard_map/ppermute | solution.py:544
  76.7 23.7 %collective-permute-start.6 = (bf16[3,160,384]{2,1,0:T(8,128)(2,1)S(1)}, bf16[3,160,384]{2,1,0:T(8,128)(2,1)S(1)}, u32[]{:S(2)}, u32[]{:S(2)}) collective-permute-start(bf16[3,160,384]{2,1,0:T(8,128)(2,1)S(1)} %pad_maximum_fusion.8.refs_0_), channel_id=1, source_target_pairs={{0,16},{4,20},{8,24},{12,28},{16,0},{20,4},{24,8},{28,12},{1,17},{... | collective-permute-start | bytes 1105928 | tf_op jit(solution)/shard_map/ppermute | solution.py:544
  102.7 25.0 %collective-permute-start.3 = (bf16[3,160,384]{2,1,0:T(8,128)(2,1)S(1)}, bf16[3,160,384]{2,1,0:T(8,128)(2,1)}, u32[]{:S(2)}, u32[]{:S(2)}) collective-permute-start(bf16[3,160,384]{2,1,0:T(8,128)(2,1)S(1)} %pad_maximum_fusion.8.refs_0_), channel_id=1, source_target_pairs={{0,4},{4,0},{8,12},{12,8},{16,20},{20,16},{24,28},{28,24},{1,5},{5... | collective-permute-start | bytes 1105928 | tf_op jit(solution)/shard_map/ppermute | solution.py:544
  102.8 24.9 %collective-permute-start.5 = (bf16[3,160,384]{2,1,0:T(8,128)(2,1)S(1)}, bf16[3,160,384]{2,1,0:T(8,128)(2,1)}, u32[]{:S(2)}, u32[]{:S(2)}) collective-permute-start(bf16[3,160,384]{2,1,0:T(8,128)(2,1)S(1)} %collective-permute-done.4.refs_2_), channel_id=1, source_target_pairs={{0,4},{4,0},{8,12},{12,8},{16,20},{20,16},{24,28},{28,24},{1,5},{5... | collective-permute-start | bytes 1105928 | tf_op jit(solution)/shard_map/ppermute | solution.py:544
  103.3 24.4 %collective-permute-start.7 = (bf16[3,160,384]{2,1,0:T(8,128)(2,1)S(1)}, bf16[3,160,384]{2,1,0:T(8,128)(2,1)}, u32[]{:S(2)}, u32[]{:S(2)}) collective-permute-start(bf16[3,160,384]{2,1,0:T(8,128)(2,1)S(1)} %collective-permute-done.6.refs_4_), channel_id=1, source_target_pairs={{0,4},{4,0},{8,12},{12,8},{16,20},{20,16},{24,28},{28,24},{1,5},{5... | collective-permute-start | bytes 1105928 | tf_op jit(solution)/shard_map/ppermute | solution.py:544
  103.4 24.3 %collective-permute-start.9 = (bf16[3,160,384]{2,1,0:T(8,128)(2,1)}, bf16[3,160,384]{2,1,0:T(8,128)(2,1)}, u32[]{:S(2)}, u32[]{:S(2)}) collective-permute-start(bf16[3,160,384]{2,1,0:T(8,128)(2,1)} %collective-permute-done.8.refs_6_), channel_id=1, source_target_pairs={{0,4},{4,0},{8,12},{12,8},{16,20},{20,16},{24,28},{28,24},{1,5},{5... | collective-permute-start | bytes 1105928 | tf_op jit(solution)/shard_map/ppermute | solution.py:544
  280.0 92.3 %collective-permute-start.40 = (bf16[8,3459]{1,0:T(8,128)(2,1)}, bf16[8,3459]{1,0:T(8,128)(2,1)}, u32[]{:S(2)}, u32[]{:S(2)}) collective-permute-start(bf16[8,3459]{1,0:T(8,128)(2,1)} %copy.227), channel_id=1, source_target_pairs={{0,1},{1,0},{2,3},{3,2},{4,5},{5,4},{6,7},{7,6},{8,9},{9,8},{10,11... | collective-permute-start | bytes 166040 | tf_op jit(solution)/shard_map/ppermute | solution.py:544
  280.0 95.4 %collective-permute-start.41 = (bf16[8,3459]{1,0:T(8,128)(2,1)}, bf16[8,3459]{1,0:T(8,128)(2,1)}, u32[]{:S(2)}, u32[]{:S(2)}) collective-permute-start(bf16[8,3459]{1,0:T(8,128)(2,1)} %copy.227), channel_id=1, source_target_pairs={{0,2},{1,3},{2,0},{3,1},{4,6},{5,7},{6,4},{7,5},{8,10},{9,11},{10,... | collective-permute-start | bytes 166040 | tf_op jit(solution)/shard_map/ppermute | solution.py:544
  282.7 94.3 %collective-permute-start.42 = (bf16[8,3459]{1,0:T(8,128)(2,1)}, bf16[8,3459]{1,0:T(8,128)(2,1)}, u32[]{:S(2)}, u32[]{:S(2)}) collective-permute-start(bf16[8,3459]{1,0:T(8,128)(2,1)} %copy.227), channel_id=1, source_target_pairs={{0,3},{1,2},{2,1},{3,0},{4,7},{5,6},{6,5},{7,4},{8,11},{9,10},{10,... | collective-permute-start | bytes 166040 | tf_op jit(solution)/shard_map/ppermute | solution.py:544
  375.5 30.3 %collective-permute-start.54 = (bf16[4,192,384]{2,1,0:T(8,128)(2,1)}, bf16[4,192,384]{2,1,0:T(8,128)(2,1)}, u32[]{:S(2)}, u32[]{:S(2)}) collective-permute-start(bf16[4,192,384]{2,1,0:T(8,128)(2,1)} %dynamic-slice_bitcast_fusion.3), channel_id=1, source_target_pairs={{0,4},{4,0},{8,12},{12,8},{16,20},{20,16},{24,28},{28,24},{1,5},{5... | collective-permute-start | bytes 1769480 | tf_op jit(solution)/shard_map/ppermute | solution.py:544
  376.9 32.9 %collective-permute-start.82 = (bf16[4,192,384]{2,1,0:T(8,128)(2,1)}, bf16[4,192,384]{2,1,0:T(8,128)(2,1)}, u32[]{:S(2)}, u32[]{:S(2)}) collective-permute-start(bf16[4,192,384]{2,1,0:T(8,128)(2,1)} %dynamic-slice_bitcast_fusion.2), channel_id=1, source_target_pairs={{0,4},{4,0},{8,12},{12,8},{16,20},{20,16},{24,28},{28,24},{1,5},{5... | collective-permute-start | bytes 1769480 | tf_op jit(solution)/shard_map/ppermute | solution.py:544
  396.1 42.1 %collective-permute-start.52 = (bf16[32,3714]{1,0:T(8,128)(2,1)}, bf16[32,3714]{1,0:T(8,128)(2,1)}, u32[]{:S(2)}, u32[]{:S(2)}) collective-permute-start(bf16[32,3714]{1,0:T(8,128)(2,1)} %pad_maximum_fusion.13), channel_id=1, source_target_pairs={{0,24},{4,28},{8,16},{12,20},{16,8},{20,12},{24,0},{28,4},{1,25},{... | collective-permute-start | bytes 713096 | tf_op jit(solution)/shard_map/ppermute | solution.py:544
  400.0 84.6 %collective-permute-start.46 = (bf16[128,3459]{0,1:T(8,128)(2,1)}, bf16[128,3459]{0,1:T(8,128)(2,1)}, u32[]{:S(2)}, u32[]{:S(2)}) collective-permute-start(bf16[128,3459]{0,1:T(8,128)(2,1)} %copy.232), channel_id=1, source_target_pairs={{0,4},{4,0},{8,12},{12,8},{16,20},{20,16},{24,28},{28,24},{1,5},{5... | collective-permute-start | bytes 2656520 | tf_op jit(solution)/shard_map/ppermute | solution.py:544
  443.6 57.1 %collective-permute-start.53 = (bf16[128,3714]{0,1:T(8,128)(2,1)}, bf16[128,3714]{0,1:T(8,128)(2,1)}, u32[]{:S(2)}, u32[]{:S(2)}) collective-permute-start(bf16[128,3714]{0,1:T(8,128)(2,1)} %copy.257), channel_id=1, source_target_pairs={{0,4},{4,0},{8,12},{12,8},{16,20},{20,16},{24,28},{28,24},{1,5},{5... | collective-permute-start | bytes 2852360 | tf_op jit(solution)/shard_map/ppermute | solution.py:544
  453.0 27.4 %collective-permute-start.91 = (bf16[48,384]{1,0:T(8,128)(2,1)}, bf16[48,384]{1,0:T(8,128)(2,1)S(1)}, u32[]{:S(2)}, u32[]{:S(2)}) collective-permute-start(bf16[48,384]{1,0:T(8,128)(2,1)} %collective-permute-done.90.refs_2_), channel_id=1, source_target_pairs={{0,4},{4,0},{8,12},{12,8},{16,20},{20,16},{24,28},{28,24},{1,5},{5... | collective-permute-start | bytes 110600 | tf_op jit(solution)/shard_map/ppermute | solution.py:544
  453.1 27.4 %collective-permute-start.93 = (bf16[48,384]{1,0:T(8,128)(2,1)}, bf16[48,384]{1,0:T(8,128)(2,1)}, u32[]{:S(2)}, u32[]{:S(2)}) collective-permute-start(bf16[48,384]{1,0:T(8,128)(2,1)} %collective-permute-done.92.refs_4_), channel_id=1, source_target_pairs={{0,4},{4,0},{8,12},{12,8},{16,20},{20,16},{24,28},{28,24},{1,5},{5... | collective-permute-start | bytes 110600 | tf_op jit(solution)/shard_map/ppermute | solution.py:544
  453.6 27.4 %collective-permute-start.95 = (bf16[48,384]{1,0:T(8,128)(2,1)}, bf16[48,384]{1,0:T(8,128)(2,1)}, u32[]{:S(2)}, u32[]{:S(2)}) collective-permute-start(bf16[48,384]{1,0:T(8,128)(2,1)} %collective-permute-done.94.refs_6_), channel_id=1, source_target_pairs={{0,4},{4,0},{8,12},{12,8},{16,20},{20,16},{24,28},{28,24},{1,5},{5... | collective-permute-start | bytes 110600 | tf_op jit(solution)/shard_map/ppermute | solution.py:544
  480.4 32.0 %collective-permute-start.96 = (bf16[4,448,384]{2,1,0:T(8,128)(2,1)}, bf16[4,448,384]{2,1,0:T(8,128)(2,1)}, u32[]{:S(2)}, u32[]{:S(2)}) collective-permute-start(bf16[4,448,384]{2,1,0:T(8,128)(2,1)} %dynamic-slice_bitcast_fusion), channel_id=1, source_target_pairs={{0,4},{4,0},{8,12},{12,8},{16,20},{20,16},{24,28},{28,24},{1,5},{5... | collective-permute-start | bytes 4128776 | tf_op jit(solution)/shard_map/ppermute | solution.py:544
  480.5 37.8 %collective-permute-start.68 = (bf16[4,448,384]{2,1,0:T(8,128)(2,1)}, bf16[4,448,384]{2,1,0:T(8,128)(2,1)}, u32[]{:S(2)}, u32[]{:S(2)}) collective-permute-start(bf16[4,448,384]{2,1,0:T(8,128)(2,1)} %dynamic-slice_bitcast_fusion.1), channel_id=1, source_target_pairs={{0,4},{4,0},{8,12},{12,8},{16,20},{20,16},{24,28},{28,24},{1,5},{5... | collective-permute-start | bytes 4128776 | tf_op jit(solution)/shard_map/ppermute | solution.py:544
  516.1 18.3 %collective-permute-start.98 = (bf16[4,112,384]{2,1,0:T(8,128)(2,1)S(1)}, bf16[4,112,384]{2,1,0:T(8,128)(2,1)S(1)}, u32[]{:S(2)}, u32[]{:S(2)}) collective-permute-start(bf16[4,112,384]{2,1,0:T(8,128)(2,1)S(1)} %get-tuple-element.126), channel_id=1, source_target_pairs={{0,16},{4,20},{8,24},{12,28},{16,0},{20,4},{24,8},{28,12},{1,17},{... | collective-permute-start | bytes 1032200 | tf_op jit(solution)/shard_map/ppermute | solution.py:544
  517.0 17.5 %collective-permute-start.99 = (bf16[4,112,384]{2,1,0:T(8,128)(2,1)S(1)}, bf16[4,112,384]{2,1,0:T(8,128)(2,1)S(1)}, u32[]{:S(2)}, u32[]{:S(2)}) collective-permute-start(bf16[4,112,384]{2,1,0:T(8,128)(2,1)S(1)} %get-tuple-element.125), channel_id=1, source_target_pairs={{0,24},{4,28},{8,16},{12,20},{16,8},{20,12},{24,0},{28,4},{1,25},{... | collective-permute-start | bytes 1032200 | tf_op jit(solution)/shard_map/ppermute | solution.py:544
  520.1 20.4 %collective-permute-start.69 = (bf16[4,112,384]{2,1,0:T(8,128)(2,1)S(1)}, bf16[4,112,384]{2,1,0:T(8,128)(2,1)S(1)}, u32[]{:S(2)}, u32[]{:S(2)}) collective-permute-start(bf16[4,112,384]{2,1,0:T(8,128)(2,1)S(1)} %get-tuple-element.121), channel_id=1, source_target_pairs={{0,8},{4,12},{8,0},{12,4},{16,24},{20,28},{24,16},{28,20},{1,9},{5... | collective-permute-start | bytes 1032200 | tf_op jit(solution)/shard_map/ppermute | solution.py:544
  521.5 26.5 %collective-permute-start.70 = (bf16[4,112,384]{2,1,0:T(8,128)(2,1)S(1)}, bf16[4,112,384]{2,1,0:T(8,128)(2,1)S(1)}, u32[]{:S(2)}, u32[]{:S(2)}) collective-permute-start(bf16[4,112,384]{2,1,0:T(8,128)(2,1)S(1)} %get-tuple-element.123), channel_id=1, source_target_pairs={{0,16},{4,20},{8,24},{12,28},{16,0},{20,4},{24,8},{28,12},{1,17},{... | collective-permute-start | bytes 1032200 | tf_op jit(solution)/shard_map/ppermute | solution.py:544
  525.7 22.2 %collective-permute-start.71 = (bf16[4,112,384]{2,1,0:T(8,128)(2,1)S(1)}, bf16[4,112,384]{2,1,0:T(8,128)(2,1)S(1)}, u32[]{:S(2)}, u32[]{:S(2)}) collective-permute-start(bf16[4,112,384]{2,1,0:T(8,128)(2,1)S(1)} %get-tuple-element.122), channel_id=1, source_target_pairs={{0,24},{4,28},{8,16},{12,20},{16,8},{20,12},{24,0},{28,4},{1,25},{... | collective-permute-start | bytes 1032200 | tf_op jit(solution)/shard_map/ppermute | solution.py:544
  534.7 16.3 %collective-permute-start.100 = (bf16[112,384]{1,0:T(8,128)(2,1)S(1)}, bf16[112,384]{1,0:T(8,128)(2,1)S(1)}, u32[]{:S(2)}, u32[]{:S(2)}) collective-permute-start(bf16[112,384]{1,0:T(8,128)(2,1)S(1)} %get-tuple-element.154), channel_id=1, source_target_pairs={{0,1},{1,0},{2,3},{3,2},{4,5},{5,4},{6,7},{7,6},{8,9},{9,8},{10,11... | collective-permute-start | bytes 258056 | tf_op jit(solution)/shard_map/ppermute | solution.py:544
  534.8 17.9 %collective-permute-start.101 = (bf16[112,384]{1,0:T(8,128)(2,1)S(1)}, bf16[112,384]{1,0:T(8,128)(2,1)S(1)}, u32[]{:S(2)}, u32[]{:S(2)}) collective-permute-start(bf16[112,384]{1,0:T(8,128)(2,1)S(1)} %get-tuple-element.156), channel_id=1, source_target_pairs={{0,2},{1,3},{2,0},{3,1},{4,6},{5,7},{6,4},{7,5},{8,10},{9,11},{10,... | collective-permute-start | bytes 258056 | tf_op jit(solution)/shard_map/ppermute | solution.py:544
  (180 other events, 1912.4 us)

commit v2 on v1

v2 whole, which is shorter than its diff:
```python
import functools
import math

import jax
import jax.numpy as jnp
from jax import lax
from jax.experimental import pallas as pl
from jax.experimental.pallas import tpu as pltpu
from jax.sharding import PartitionSpec as P

D = 384
HEADS = 6
HEAD_DIM = 64
FF = 1536
TOK = 256
PATCH_IN = 16
EPSILON = 1e-06
BF = jnp.bfloat16
F32 = jnp.float32
VMEM_LIMIT = 58 * 1024 * 1024


def mm(left, right):
    return lax.dot_general(left, right, (((1,), (0,)), ((), ())), preferred_element_type=F32)


def mm_nt(left, right):
    return lax.dot_general(left, right, (((1,), (1,)), ((), ())), preferred_element_type=F32)


def norm_parts(x):
    centered = x - jnp.mean(x, axis=0, keepdims=True)
    variance = jnp.mean(centered * centered, axis=0, keepdims=True)
    inv = lax.rsqrt(variance + EPSILON)
    return centered * inv, inv


def norm_back(d, normed, inv, scale1):
    dn = d * scale1
    m1 = jnp.mean(dn, axis=0, keepdims=True)
    m2 = jnp.mean(dn * normed, axis=0, keepdims=True)
    return (dn - m1 - normed * m2) * inv


def column(mods_ref, index, image):
    block = mods_ref[pl.ds(index * D, D), :]
    lane = lax.broadcasted_iota(jnp.int32, block.shape, 1)
    return jnp.sum(jnp.where(lane == image, block, 0.0), axis=1, keepdims=True)


def put_column(out_ref, index, image, values):
    total = jnp.sum(values, axis=1, keepdims=True)
    rows = pl.ds(index * D, D)
    old = out_ref[rows, :]
    lane = lax.broadcasted_iota(jnp.int32, old.shape, 1)
    out_ref[rows, :] = jnp.where(lane == image, total, old)


def half_zero(x, half):
    row = lax.broadcasted_iota(jnp.int32, x.shape, 0)
    keep = row < HEAD_DIM if half == 0 else row >= HEAD_DIM
    return jnp.where(keep, x, jnp.zeros_like(x))


def attention_forward(qkv_ref, b, lse_ref, att_ref, att_lanes):
    for pair in range(HEADS // 2):
        lo = 2 * HEAD_DIM * pair
        q2 = qkv_ref[b, lo : lo + 128, :]
        k2 = qkv_ref[b, D + lo : D + lo + 128, :].T
        for half in range(2):
            head = 2 * pair + half
            scores = mm(k2, half_zero(q2, half))
            peak = jnp.max(scores, axis=0, keepdims=True)
            exps = jnp.exp(scores - peak)
            total = jnp.sum(exps, axis=0, keepdims=True)
            vrow = 2 * D + HEAD_DIM * head
            out = mm(qkv_ref[b, vrow : vrow + HEAD_DIM, :], exps.astype(BF))
            att_ref[HEAD_DIM * head : HEAD_DIM * (head + 1), att_lanes] = (
                out * (1.0 / total)
            ).astype(BF)
            lse_ref[b, head : head + 1, :] = peak + jnp.log(total)


def attention_backward(qkv_ref, b, lse_ref, go_ref, gqkv_ref, lanes):
    for pair in range(HEADS // 2):
        lo = 2 * HEAD_DIM * pair
        q2 = qkv_ref[b, lo : lo + 128, :]
        k2 = qkv_ref[b, D + lo : D + lo + 128, :].T
        v2 = qkv_ref[b, 2 * D + lo : 2 * D + lo + 128, :].T
        g2 = go_ref[b, lo : lo + 128, :]
        for half in range(2):
            head = 2 * pair + half
            row = HEAD_DIM * head
            scores = mm(k2, half_zero(q2, half))
            probs = jnp.exp(scores - lse_ref[b, head : head + 1, :])
            gprobs = mm(v2, half_zero(g2, half))
            inner = jnp.sum(probs * gprobs, axis=0, keepdims=True)
            gscores = (probs * (gprobs - inner)).astype(BF)
            gq = mm(qkv_ref[b, D + row : D + row + HEAD_DIM, :], gscores)
            gk = mm_nt(qkv_ref[b, row : row + HEAD_DIM, :], gscores)
            gv = mm_nt(go_ref[b, row : row + HEAD_DIM, :], probs.astype(BF))
            gqkv_ref[row : row + HEAD_DIM, lanes] = (gq * (1.0 / math.sqrt(HEAD_DIM))).astype(BF)
            gqkv_ref[D + row : D + row + HEAD_DIM, lanes] = gk.astype(BF)
            gqkv_ref[2 * D + row : 2 * D + row + HEAD_DIM, lanes] = gv.astype(BF)


def project_qkv(wqkv_t_ref, normed_ref, lanes, qkv_ref, b):
    qkv = mm(wqkv_t_ref[...], normed_ref[:, lanes])
    qkv_ref[b, 0:D, :] = (qkv[0:D] * (1.0 / math.sqrt(HEAD_DIM))).astype(BF)
    qkv_ref[b, D:, :] = qkv[D:].astype(BF)


GELU_C = 0.7978845608
GELU_A = 0.044715


def gelu_both(v):
    square = v * v
    t = jnp.tanh(v * (GELU_C + (GELU_C * GELU_A) * square))
    half = 0.5 + 0.5 * t
    slope = half + 0.5 * v * (1.0 - t * t) * (GELU_C + (3.0 * GELU_C * GELU_A) * square)
    return v * half, slope


def gelu_one(v):
    t = jnp.tanh(v * (GELU_C + (GELU_C * GELU_A) * (v * v)))
    return v * (0.5 + 0.5 * t)


def accumulate(acc_ref, value, first):
    @pl.when(first)
    def _():
        acc_ref[...] = value

    @pl.when(jnp.logical_not(first))
    def _():
        acc_ref[...] += value


FF_CHUNK = 512


def pack_blocks(pack_ref, start, value):
    members = pack_ref.shape[0]
    rows = D // members
    count = value.shape[1] // D
    for g in range(members):
        for c in range(count):
            pack_ref[g, start + rows * c : start + rows * (c + 1), :] = value[
                rows * g : rows * (g + 1), D * c : D * (c + 1)
            ].astype(BF)
    return start + rows * count


def pack_outer(pack_ref, awo_ref, awf_ref, awg_ref):
    members = pack_ref.shape[0]
    rows = (D + FF) // members
    for g in range(members):
        low, high = rows * g, rows * (g + 1)
        if low < D:
            cut = min(high, D)
            pack_ref[g, 0 : cut - low, :] = awo_ref[low:cut, :].astype(BF)
        if high > D:
            cut = max(low, D)
            pack_ref[g, cut - low : rows, :] = awg_ref[cut - D : high - D, :].astype(BF)
    return pack_blocks(pack_ref, rows, awf_ref)


def pack_rest(pack_ref, used, extra):
    if extra is not None:
        for g in range(pack_ref.shape[0]):
            pack_ref[g, used : used + PATCH_IN, :] = extra.astype(BF)
        used += PATCH_IN
    if used < pack_ref.shape[1]:
        pack_ref[:, used:, :] = jnp.zeros_like(pack_ref[:, used:, :])


def split_pack(pack_ref, table_ref, offset, outs):
    for j, out_ref in enumerate(outs):
        rows = out_ref.shape[1]
        at = pl.multiple_of(table_ref[offset + j] * rows, rows)
        out_ref[...] = pack_ref[:, pl.ds(at, rows), :]


def att_fwd_kernel(B, offset, held, noisy_ref, wp_t_ref, pos_ref, mods_ref, wqkv_t_ref, *refs):
    qkv_ref, lse_ref, att_out_ref, normed_ref, att_ref = refs[held:]
    step = pl.program_id(0)
    for b in range(B):
        image = (offset + step) * B + b
        lanes = slice(TOK * b, TOK * (b + 1))
        hidden = mm(wp_t_ref[...], noisy_ref[b]) + pos_ref[...]
        normed, _ = norm_parts(hidden)
        normed_ref[:, lanes] = (
            normed * (1.0 + column(mods_ref, 1, image)) + column(mods_ref, 0, image)
        ).astype(BF)
        project_qkv(wqkv_t_ref, normed_ref, lanes, qkv_ref, b)
        attention_forward(qkv_ref, b, lse_ref, att_ref, lanes)
        att_out_ref[b] = att_ref[:, lanes]


def ffn_fwd_kernel(B, noisy_ref, wp_t_ref, pos_ref, att_ref, mods_a_ref, mods_b_ref, wo_t_ref, wf_t_ref,
                   wg_t_ref, mid_ref, bra_ref, brb_ref, hid_ref, normed_ref):
    step = pl.program_id(0)
    for b in range(B):
        image = step * B + b
        lanes = slice(TOK * b, TOK * (b + 1))
        hidden = mm(wp_t_ref[...], noisy_ref[b]) + pos_ref[...]
        branch_a = mm(wo_t_ref[...], att_ref[b])
        bra_ref[b] = branch_a
        mid = hidden + column(mods_a_ref, 2, image) * branch_a
        mid_ref[b] = mid
        normed, _ = norm_parts(mid)
        normed_ref[:, lanes] = (
            normed * (1.0 + column(mods_b_ref, 1, image)) + column(mods_b_ref, 0, image)
        ).astype(BF)
        branch = None
        for f in range(0, FF, FF_CHUNK):
            pre = mm(wf_t_ref[f : f + FF_CHUNK, :], normed_ref[:, lanes])
            part = mm(wg_t_ref[:, f : f + FF_CHUNK], gelu_one(pre).astype(BF))
            branch = part if branch is None else branch + part
        brb_ref[b] = branch
        hid_ref[b] = mid + column(mods_b_ref, 2, image) * branch


def out_bwd(b, image, lanes, gmid, branch, gate, wo_ref, gba_ref, go_ref, gm_ref, gm_base):
    put_column(gm_ref, gm_base, image, gmid * branch)
    gba_ref[:, lanes] = (gate * gmid).astype(BF)
    go_ref[b] = mm(wo_ref[...], gba_ref[:, lanes]).astype(BF)


def block_kernel(B, entries, table_ref, hid_ref, noise_ref, mods_ref, modf_ref, wqkv_t_ref, wo_t_ref, wf_t_ref,
                 wg_t_ref, wo_ref, wf_ref, wg_ref, wy_t_ref, wy_ref, cond_ref,
                 qkv_ref, lse_ref, go_ref, gmid_ref, gm_ref, gmf_ref, loss_ref,
                 keep_ref, send_ref,
                 pack_ref, normed_ref, att_ref, slope_ref, act_ref, gpre_ref, gba_ref, gbb_ref, normf_ref, gout_ref,
                 awo_ref, awf_ref, awg_ref, awy_ref):
    step = pl.program_id(0)
    first = step == 0

    @pl.when(first)
    def _():
        gm_ref[...] = jnp.zeros_like(gm_ref)
        gmf_ref[...] = jnp.zeros_like(gmf_ref)
        loss_ref[...] = jnp.zeros_like(loss_ref)

    for b in range(B):
        image = step * B + b
        lanes = slice(TOK * b, TOK * (b + 1))
        hidden = hid_ref[b]
        normed, _ = norm_parts(hidden)
        normed_ref[:, lanes] = (
            normed * (1.0 + column(mods_ref, 1, image)) + column(mods_ref, 0, image)
        ).astype(BF)
        project_qkv(wqkv_t_ref, normed_ref, lanes, qkv_ref, b)
        attention_forward(qkv_ref, b, lse_ref, att_ref, lanes)
        branch_a = mm(wo_t_ref[...], att_ref[:, lanes])
        gate_a = column(mods_ref, 2, image)
        mid = hidden + gate_a * branch_a
        normed_b, inv_b = norm_parts(mid)
        scale_b = 1.0 + column(mods_ref, 4, image)
        normed_ref[:, lanes] = (normed_b * scale_b + column(mods_ref, 3, image)).astype(BF)
        branch_b = None
        for f in range(0, FF, FF_CHUNK):
            rows = slice(f, f + FF_CHUNK)
            pre = mm(wf_t_ref[rows, :], normed_ref[:, lanes])
            act, slope = gelu_both(pre)
            slope_ref[rows, :] = slope
            act_ref[rows, lanes] = act.astype(BF)
            part = mm(wg_t_ref[:, rows], act_ref[rows, lanes])
            branch_b = part if branch_b is None else branch_b + part
        gate_b = column(mods_ref, 5, image)
        hidden2 = mid + gate_b * branch_b
        normed_f, inv_f = norm_parts(hidden2)
        scale_f = 1.0 + column(modf_ref, 1, image)
        normf_ref[:, lanes] = (normed_f * scale_f + column(modf_ref, 0, image)).astype(BF)
        residue = mm(wy_t_ref[...], normf_ref[:, lanes]) - noise_ref[b].astype(F32)
        loss_ref[...] += residue * residue
        gout_ref[:, lanes] = ((2.0 / entries) * residue).astype(BF)
        gnf = mm(wy_ref[...], gout_ref[:, lanes])
        put_column(gmf_ref, 0, image, gnf)
        put_column(gmf_ref, 1, image, gnf * normed_f)
        ghid = norm_back(gnf, normed_f, inv_f, scale_f)
        put_column(gm_ref, 3, image, ghid * branch_b)
        gbb_ref[:, lanes] = (gate_b * ghid).astype(BF)
        gnb = None
        for f in range(0, FF, FF_CHUNK):
            rows = slice(f, f + FF_CHUNK)
            gact = mm(wg_ref[rows, :], gbb_ref[:, lanes])
            gpre_ref[rows, lanes] = (gact * slope_ref[rows, :]).astype(BF)
            part = mm(wf_ref[:, rows], gpre_ref[rows, lanes])
            gnb = part if gnb is None else gnb + part
        put_column(gm_ref, 1, image, gnb)
        put_column(gm_ref, 2, image, gnb * normed_b)
        gmid = ghid + norm_back(gnb, normed_b, inv_b, scale_b)
        gmid_ref[b] = gmid
        out_bwd(b, image, lanes, gmid, branch_a, gate_a, wo_ref, gba_ref, go_ref, gm_ref, 0)
    accumulate(awo_ref, mm_nt(att_ref[...], gba_ref[...]), first)
    accumulate(awf_ref, mm_nt(normed_ref[...], gpre_ref[...]), first)
    accumulate(awg_ref, mm_nt(act_ref[...], gbb_ref[...]), first)
    accumulate(awy_ref, mm_nt(gout_ref[...], normf_ref[...]), first)

    @pl.when(step == pl.num_programs(0) - 1)
    def _():
        used = pack_outer(pack_ref, awo_ref, awf_ref, awg_ref)
        used = pack_blocks(pack_ref, used, mm_nt(cond_ref[...], gm_ref[...].astype(BF)))
        pack_rest(pack_ref, used, awy_ref[...])
        split_pack(pack_ref, table_ref, 0, (keep_ref, send_ref))


def ffn_bwd_kernel(B, table_ref, ghid_ref, mid_ref, att_ref, bra_ref, brb_ref, mods_a_ref, mods_b_ref, wf_t_ref, wo_ref, wf_ref,
                   wg_ref, cond_ref, go_ref, gmid_ref, gm_ref, keep_ref, send_ref, pack_ref,
                   normed_ref, act_ref, gpre_ref, gba_ref, gbb_ref, atts_ref, awo_ref, awf_ref, awg_ref):
    step = pl.program_id(0)
    first = step == 0

    @pl.when(first)
    def _():
        gm_ref[...] = jnp.zeros_like(gm_ref)

    for b in range(B):
        image = step * B + b
        lanes = slice(TOK * b, TOK * (b + 1))
        ghid = ghid_ref[b]
        put_column(gm_ref, 3, image, ghid * brb_ref[b])
        gbb_ref[:, lanes] = (column(mods_b_ref, 2, image) * ghid).astype(BF)
        normed_b, inv_b = norm_parts(mid_ref[b])
        scale_b = 1.0 + column(mods_b_ref, 1, image)
        normed_ref[:, lanes] = (normed_b * scale_b + column(mods_b_ref, 0, image)).astype(BF)
        atts_ref[:, lanes] = att_ref[b]
        gnb = None
        for f in range(0, FF, FF_CHUNK):
            rows = slice(f, f + FF_CHUNK)
            act, slope = gelu_both(mm(wf_t_ref[rows, :], normed_ref[:, lanes]))
            act_ref[rows, lanes] = act.astype(BF)
            gact = mm(wg_ref[rows, :], gbb_ref[:, lanes])
            gpre_ref[rows, lanes] = (gact * slope).astype(BF)
            part = mm(wf_ref[:, rows], gpre_ref[rows, lanes])
            gnb = part if gnb is None else gnb + part
        put_column(gm_ref, 1, image, gnb)
        put_column(gm_ref, 2, image, gnb * normed_b)
        gmid = ghid + norm_back(gnb, normed_b, inv_b, scale_b)
        gmid_ref[b] = gmid
        out_bwd(b, image, lanes, gmid, bra_ref[b], column(mods_a_ref, 2, image), wo_ref, gba_ref, go_ref,
                gm_ref, 0)
    accumulate(awo_ref, mm_nt(atts_ref[...], gba_ref[...]), first)
    accumulate(awf_ref, mm_nt(normed_ref[...], gpre_ref[...]), first)
    accumulate(awg_ref, mm_nt(act_ref[...], gbb_ref[...]), first)

    @pl.when(step == pl.num_programs(0) - 1)
    def _():
        used = pack_outer(pack_ref, awo_ref, awf_ref, awg_ref)
        used = pack_blocks(pack_ref, used, mm_nt(cond_ref[...], gm_ref[...].astype(BF)))
        pack_rest(pack_ref, used, None)
        split_pack(pack_ref, table_ref, 0, (keep_ref, send_ref))


def att_bwd_kernel(B, offset, bottom, opens, closes, *refs):
    refs = list(refs)
    take = lambda count: [refs.pop(0) for _ in range(count)]
    (table_ref,) = take(1)
    noisy_ref, wp_t_ref, pos_ref = take(3) if bottom else (None, None, None)
    (hid_ref,) = (None,) if bottom else take(1)
    qkv_ref, lse_ref, go_ref, gmid_ref, mods_ref, wqkv_ref, cond_ref = take(7)
    (gmf_ref,) = (None,) if bottom else take(1)
    before = take(3 if bottom else 2) if not opens else []
    (ghid_ref,) = (None,) if bottom else take(1)
    (gm_ref,) = take(1)
    sums = 2 if bottom else 1
    keep_ref, send_ref, pack_ref, accs = None, None, None, None
    if closes:
        keep_ref, send_ref = take(2)
    else:
        accs = take(sums)
    if closes:
        (pack_ref,) = take(1)
    normed_ref, gqkv_ref = take(2)
    tok_ref, noi_ref = take(2) if bottom else (None, None)
    if closes:
        accs = take(sums)
    step = pl.program_id(0)
    first = step == 0

    @pl.when(first)
    def _():
        if opens:
            gm_ref[...] = jnp.zeros_like(gm_ref)
            for acc_ref in accs:
                acc_ref[...] = jnp.zeros_like(acc_ref)
        else:
            for to_ref, from_ref in zip([gm_ref] + accs, before):
                to_ref[...] = from_ref[...]

    for b in range(B):
        image = (offset + step) * B + b
        lanes = slice(TOK * b, TOK * (b + 1))
        hidden = mm(wp_t_ref[...], noisy_ref[b]) + pos_ref[...] if bottom else hid_ref[b]
        normed, inv = norm_parts(hidden)
        scale = 1.0 + column(mods_ref, 1, image)
        normed_ref[:, lanes] = (normed * scale + column(mods_ref, 0, image)).astype(BF)
        attention_backward(qkv_ref, b, lse_ref, go_ref, gqkv_ref, lanes)
        gna = mm(wqkv_ref[...], gqkv_ref[:, lanes])
        put_column(gm_ref, 0, image, gna)
        put_column(gm_ref, 1, image, gna * normed)
        ghid = gmid_ref[b] + norm_back(gna, normed, inv, scale)
        if bottom:
            tok_ref[:, lanes] = ghid.astype(BF)
            noi_ref[:, lanes] = noisy_ref[b]
        else:
            ghid_ref[b] = ghid
    accs[0][...] += mm_nt(normed_ref[...], gqkv_ref[...])
    if bottom:
        accs[1][...] += mm_nt(noi_ref[...], tok_ref[...])

    if closes:
        @pl.when(step == pl.num_programs(0) - 1)
        def _():
            used = pack_blocks(pack_ref, 0, accs[0])
            used = pack_blocks(pack_ref, used, mm_nt(cond_ref[...], gm_ref[...].astype(BF)))
            if not bottom:
                used = pack_blocks(pack_ref, used, mm_nt(cond_ref[...], gmf_ref[...].astype(BF)))
            pack_rest(pack_ref, used, accs[1][...] if bottom else None)
            split_pack(pack_ref, table_ref, 0, (keep_ref, send_ref))


def whole(*shape):
    return pl.BlockSpec(shape, lambda i: (0,) * len(shape))


def images(B, *shape, offset=0):
    return pl.BlockSpec((B,) + shape, lambda i: (i + offset,) + (0,) * len(shape))


def sds(shape, dtype):
    return jax.ShapeDtypeStruct(shape, dtype)


def run_kernel(kernel, steps, in_specs, outs, scratch, flops, args, aliases=None):
    out_specs = [spec for spec, _, _ in outs]
    out_shape = [sds(shape, dtype) for _, shape, dtype in outs]
    moved = sum(a.size * a.dtype.itemsize for a in args) + sum(
        math.prod(o.shape) * o.dtype.itemsize for o in out_shape
    )
    return pl.pallas_call(
        kernel,
        grid=(steps,),
        in_specs=in_specs,
        out_specs=out_specs,
        out_shape=out_shape,
        scratch_shapes=[pltpu.VMEM(shape, dtype) for shape, dtype in scratch],
        input_output_aliases=aliases or {},
        compiler_params=pltpu.CompilerParams(vmem_limit_bytes=VMEM_LIMIT),
        cost_estimate=pl.CostEstimate(flops=8 * flops, bytes_accessed=moved, transcendentals=0),
    )(*args)


MODS = whole(6 * D, 128)
HALF_MODS = whole(3 * D, 128)
COND = whole(D, 128)
SCALARS = pl.BlockSpec(memory_space=pltpu.SMEM)


def halves(pack):
    ng, rows, _ = pack
    half = (ng, rows // 2, D)
    return [(whole(*half), half, BF)] * 2


def att_forward(noisy, wp_t, pos, mods, wqkv_t, B, part, parts, before):
    n = noisy.shape[0]
    T = B * TOK
    steps = n // B // parts
    here = functools.partial(images, B, offset=part * steps)
    return run_kernel(
        functools.partial(att_fwd_kernel, B, part * steps, len(before)), steps,
        [here(PATCH_IN, TOK), whole(D, PATCH_IN), whole(D, TOK), HALF_MODS, whole(3 * D, D)]
        + [pl.BlockSpec(memory_space=pl.ANY)] * len(before),
        [(here(3 * D, TOK), (n, 3 * D, TOK), BF), (here(8, TOK), (n, 8, TOK), F32),
         (here(D, TOK), (n, D, TOK), BF)],
        [((D, T), BF), ((D, T), BF)],
        2 * n * TOK * (3 * D * D + 2 * D * TOK) // parts, (noisy, wp_t, pos, mods, wqkv_t) + tuple(before),
        aliases={5 + i: i for i in range(len(before))})


def ffn_forward(noisy, wp_t, pos, att, mods_a, mods_b, wo_t, wf_t, wg_t, B):
    n = noisy.shape[0]
    T = B * TOK
    full = images(B, D, TOK)
    return run_kernel(
        functools.partial(ffn_fwd_kernel, B), n // B,
        [images(B, PATCH_IN, TOK), whole(D, PATCH_IN), whole(D, TOK), full, HALF_MODS, HALF_MODS, whole(D, D),
         whole(FF, D), whole(D, FF)],
        [(full, (n, D, TOK), F32)] * 4,
        [((D, T), BF)],
        2 * n * TOK * (2 * D * FF + D * D), (noisy, wp_t, pos, att, mods_a, mods_b, wo_t, wf_t, wg_t))


def block_step(table, hid, noise, mods, modf, wqkv_t, wo_t, wf_t, wg_t, wo, wf, wg, wy_t, wy, cond, entries, B, pack):
    n = hid.shape[0]
    T = B * TOK
    full = images(B, D, TOK)
    return run_kernel(
        functools.partial(block_kernel, B, entries), n // B,
        [SCALARS, full, images(B, PATCH_IN, TOK), MODS, whole(2 * D, 128), whole(3 * D, D), whole(D, D),
         whole(FF, D), whole(D, FF), whole(D, D), whole(D, FF), whole(FF, D), whole(PATCH_IN, D),
         whole(D, PATCH_IN), COND],
        [(images(B, 3 * D, TOK), (n, 3 * D, TOK), BF), (images(B, 8, TOK), (n, 8, TOK), F32),
         (full, (n, D, TOK), BF), (full, (n, D, TOK), F32),
         (whole(4 * D, 128), (4 * D, 128), F32), (whole(2 * D, 128), (2 * D, 128), F32),
         (whole(PATCH_IN, TOK), (PATCH_IN, TOK), F32)] + halves(pack),
        [(pack, BF), ((D, T), BF), ((D, T), BF), ((FF, TOK), F32), ((FF, T), BF), ((FF, T), BF), ((D, T), BF),
         ((D, T), BF), ((D, T), BF), ((PATCH_IN, T), BF), ((D, D), F32), ((D, FF), F32), ((FF, D), F32),
         ((PATCH_IN, D), F32)],
        2 * n * TOK * (4 * D * D + 2 * D * TOK + 6 * D * FF + 2 * D * D),
        (table, hid, noise, mods, modf, wqkv_t, wo_t, wf_t, wg_t, wo, wf, wg, wy_t, wy, cond))


def ffn_backward(table, ghid, mid, att, bra, brb, mods_a, mods_b, wf_t, wo, wf, wg, cond, B, pack):
    n = mid.shape[0]
    T = B * TOK
    full = images(B, D, TOK)
    return run_kernel(
        functools.partial(ffn_bwd_kernel, B), n // B,
        [SCALARS, full, full, full, full, full, HALF_MODS, HALF_MODS, whole(FF, D), whole(D, D), whole(D, FF),
         whole(FF, D), COND],
        [(full, (n, D, TOK), BF), (full, (n, D, TOK), F32), (whole(4 * D, 128), (4 * D, 128), F32)] + halves(pack),
        [(pack, BF), ((D, T), BF), ((FF, T), BF), ((FF, T), BF), ((D, T), BF), ((D, T), BF), ((D, T), BF),
         ((D, D), F32), ((D, FF), F32), ((FF, D), F32)],
        2 * n * TOK * (5 * D * FF + 2 * D * D),
        (table, ghid, mid, att, bra, brb, mods_a, mods_b, wf_t, wo, wf, wg, cond))


def att_backward(table, source, qkv, lse, go, gmid, mods, wqkv, cond, gmf, B, bottom, pack, part=0, parts=1, before=()):
    n = qkv.shape[0]
    T = B * TOK
    steps = n // B // parts
    offset = part * steps
    opens, closes = part == 0, part == parts - 1
    here = functools.partial(images, B, offset=offset)
    full = here(D, TOK)
    gm = (whole(2 * D, 128), (2 * D, 128), F32)
    sums = [(whole(D, 3 * D), (D, 3 * D), F32)] + ([(whole(PATCH_IN, D), (PATCH_IN, D), F32)] if bottom else [])
    ins = [SCALARS] + ([here(PATCH_IN, TOK), whole(D, PATCH_IN), whole(D, TOK)] if bottom else [full])
    ins += [here(3 * D, TOK), here(8, TOK), full, full, HALF_MODS if bottom else MODS, whole(D, 3 * D), COND]
    ins += [] if bottom else [whole(2 * D, 128)]
    args = (table,) + tuple(source) + (qkv, lse, go, gmid, mods, wqkv, cond) + (() if bottom else (gmf,))
    if not opens:
        ins += [gm[0]] + [s[0] for s in sums]
        args += tuple(before)
    outs = ([] if bottom else [(full, (n, D, TOK), F32)]) + [gm] + (halves(pack) if closes else sums)
    scratch = ([(pack, BF)] if closes else []) + [((D, T), BF), ((3 * D, T), BF)]
    scratch += [((D, T), BF), ((PATCH_IN, T), BF)] if bottom else []
    scratch += [(s[1], F32) for s in sums] if closes else []
    return run_kernel(
        functools.partial(att_bwd_kernel, B, offset, bottom, opens, closes), steps, ins, outs, scratch,
        2 * n * TOK * (6 * D * D + 5 * D * TOK) // parts, args)


FREQ = 256
CLASSES = 1000
GRID = 16
LAYERS = 2
MOMENTUM = 0.9
LEARN = 30.0
DECAY = 0.7
IMAGES_PER_STEP = 2
SMALL_COST = 8 * 10**9


def plan(steps_in):
    anchor = math.cos(0.5 * math.pi * 0.008 / 1.008)
    fraction = (steps_in.astype(F32) / 1000.0 + 0.008) / 1.008
    levels = jnp.cos(0.5 * math.pi * fraction)
    return levels * levels / (anchor * anchor)


def time_features(steps_in):
    half_width = FREQ // 2
    frequencies = jnp.exp(-math.log(10000.0) * jnp.arange(half_width, dtype=F32) / half_width)
    angles = steps_in.astype(F32)[:, None] * frequencies[None, :]
    return jnp.concatenate([jnp.cos(angles), jnp.sin(angles)], axis=1)


def positions():
    quarter = D // 4
    omegas = jnp.exp(-math.log(10000.0) * jnp.arange(quarter, dtype=F32) / quarter)
    places = jnp.arange(GRID * GRID, dtype=jnp.int32)
    column = omegas[:, None] * (places % GRID).astype(F32)[None, :]
    row_pos = omegas[:, None] * (places // GRID).astype(F32)[None, :]
    return jnp.concatenate(
        [jnp.sin(column), jnp.cos(column), jnp.sin(row_pos), jnp.cos(row_pos)], axis=0
    )


def swish_parts(values):
    s = 1.0 / (1.0 + jnp.exp(-values))
    return values * s, s * (1.0 + values * (1.0 - s))


def advance(weight, moment, average, gradient):
    new_moment = MOMENTUM * moment + gradient
    new_weight = weight - LEARN * (gradient + MOMENTUM * new_moment)
    new_average = DECAY * average + (1.0 - DECAY) * new_weight
    return (new_weight, new_moment, new_average)


def after(x, *others):
    return lax.optimization_barrier((x,) + others)[0]


def swap(x, axis, mask):
    pairs = [(i, i ^ mask) for i in range(lax.axis_size(axis))]
    return lax.ppermute(x, axis, pairs)


def digit_list(n):
    found, shift = [], 0
    while (1 << shift) < n:
        left = n >> shift
        size = 2 if shift == 0 or left == 2 else 4
        found.append((shift, size))
        shift += size.bit_length() - 1
    return found


def place_of(index, n):
    place = 0
    for shift, size in digit_list(n):
        place = place * size + ((index >> shift) & (size - 1))
    return place


def place_table(emb_rows):
    nr, ng = lax.axis_size("rep"), lax.axis_size("grp")
    me, member = lax.axis_index("rep"), lax.axis_index("grp")
    entries, offsets = [], {}
    for shift, size in digit_list(nr):
        offsets[shift] = len(entries)
        entries += [((me >> shift) & (size - 1)) ^ j for j in range(size)]
    if not entries:
        entries = [0, 1]
    offsets["place"] = len(entries)
    entries += [place_of(me ^ mask, nr) for mask in range(nr)]
    offsets["member"] = len(entries)
    entries += [member ^ k for k in range(ng)]
    offsets["lead"] = len(entries)
    entries.append(emb_rows * member % 16)
    return jnp.stack([jnp.asarray(e, jnp.int32) for e in entries]), offsets


def in_vmem():
    return pl.BlockSpec(memory_space=pltpu.VMEM)


def small_kernel(kernel, outs, scratch, args, scalars=1):
    return pl.pallas_call(
        kernel,
        in_specs=[SCALARS] * scalars + [in_vmem()] * (len(args) - scalars),
        out_specs=[in_vmem()] * len(outs),
        out_shape=[sds(shape, dtype) for shape, dtype in outs],
        scratch_shapes=[pltpu.VMEM(shape, dtype) for shape, dtype in scratch],
        compiler_params=pltpu.CompilerParams(vmem_limit_bytes=VMEM_LIMIT),
        cost_estimate=pl.CostEstimate(flops=SMALL_COST, bytes_accessed=0, transcendentals=0),
    )(*args)


def spread_outer(piece, n):
    pieces = [((0,), piece)]
    digits = digit_list(n)[1:]
    for shift, size in digits:
        if len(pieces) > 1:
            pieces = [(sum((m for m, _ in pieces), ()), jnp.concatenate([v for _, v in pieces], axis=0))]
        masks, value = pieces[0]
        pieces = pieces + [
            (tuple(m ^ (j << shift) for m in masks), swap(value, "rep", j << shift)) for j in range(1, size)
        ]
    return pieces


def spread_core(pieces, n):
    if n == 1:
        return pieces
    return pieces + [(tuple(m ^ 1 for m in masks), swap(value, "rep", 1)) for masks, value in pieces]


def gather_members(mine):
    got = [swap(mine, "grp", k) for k in range(1, lax.axis_size("grp"))]
    return jnp.concatenate(got, axis=0) if got else None


def sum_parts(parts):
    total = parts[0][...].astype(F32)
    for part in parts[1:]:
        total = total + part[...].astype(F32)
    return total.astype(BF)


def rows_kernel(count, offset, table_ref, *refs):
    parts, outs, total_ref = refs[:count], refs[count:-1], refs[-1]
    total_ref[...] = sum_parts(parts)
    split_pack(total_ref, table_ref, offset, outs)


def members_kernel(counts, offset, has_extra, table_ref, *refs):
    refs = list(refs)
    groups = [[refs.pop(0) for _ in range(c)] for c in counts]
    extra_ref = refs.pop(0) if has_extra else None
    outs, totals = refs[: -len(counts)], refs[-len(counts) :]
    for parts, total_ref in zip(groups, totals):
        total_ref[...] = sum_parts(parts)
    for k, out_ref in enumerate(outs):
        at = 0
        for total_ref in totals:
            rows = total_ref.shape[1]
            out_ref[at : at + rows, :] = total_ref[table_ref[offset + k]]
            at += rows
        if has_extra:
            out_ref[at:, :] = extra_ref[...]


def last_kernel(count, extra, table_ref, *refs):
    parts, out_ref = refs[:count], refs[-1]
    rows = parts[0].shape[0] - extra
    total = parts[0][0:rows, :].astype(F32)
    for part in parts[1:]:
        total = total + part[0:rows, :].astype(F32)
    out_ref[0:rows, :] = total.astype(BF)
    if extra:
        for i, part in enumerate(parts):
            out_ref[rows + extra * i : rows + extra * (i + 1), :] = part[rows:, :]


def reduce_first(keep, send):
    return [keep, swap(send, "rep", 1)] if lax.axis_size("rep") > 1 else [keep]


def reduce_outer(parts, table, offsets, number):
    shift, size = digit_list(lax.axis_size("rep"))[number]
    ng, rows, _ = parts[0].shape
    one = lambda r: pl.BlockSpec((1, r, D), lambda i: (i, 0, 0))
    cut = pl.pallas_call(
        functools.partial(rows_kernel, len(parts), offsets[shift]),
        grid=(ng,),
        in_specs=[SCALARS] + [one(rows)] * len(parts),
        out_specs=[one(rows // size)] * size,
        out_shape=[sds((ng, rows // size, D), BF)] * size,
        scratch_shapes=[pltpu.VMEM((1, rows, D), BF)],
    )(table, *parts)
    return [cut[0]], cut[1:], shift


def exchange(own, sends, axis, shift):
    return own + [swap(x, axis, (j + 1) << shift) for j, x in enumerate(sends)]


def reduce_members(groups, extra, table, offsets):
    ng = groups[0][0].shape[0]
    rows = sum(g[0].shape[1] for g in groups) + (0 if extra is None else extra.shape[0])
    cut = small_kernel(
        functools.partial(members_kernel, tuple(len(g) for g in groups), offsets["member"], extra is not None),
        [((rows, D), BF)] * ng, [(g[0].shape, BF) for g in groups],
        (table, *sum(groups, []), *([] if extra is None else [extra])),
    )
    return [cut[0]], cut[1:], 0


def reduce_last(parts, extra, table):
    rows = parts[0].shape[0] + extra * (len(parts) - 1)
    return small_kernel(
        functools.partial(last_kernel, len(parts), extra), [((rows, D), BF)], [], (table, *parts)
    )[0]


def pack_first_kernel(lead_at, emb_real, shard_place, table_ref, emb_ref, wa_ref, wqkv_ref, shard_ref, mine_ref, wide_ref):
    wide_ref[...] = jnp.zeros_like(wide_ref)
    wide_ref[0:emb_real, :] = emb_ref[...]
    seg = wide_ref.shape[0]
    shard_ref[0:seg, :] = pltpu.roll(wide_ref[...], table_ref[lead_at], 0).astype(BF)
    at = seg
    for ref in (wa_ref, wqkv_ref):
        for c in range(3):
            rows = ref.shape[1]
            shard_ref[at : at + rows, :] = ref[0, :, D * c : D * (c + 1)].astype(BF)
            at += rows
    if at < shard_ref.shape[0]:
        shard_ref[at:, :] = jnp.zeros_like(shard_ref[at:, :])
    rows = mine_ref.shape[0]
    mine_ref[...] = shard_ref[pl.ds(pl.multiple_of(table_ref[shard_place] * rows, rows), rows), :]


def pack_first(table, offsets, emb_table, w_in, seg, unit):
    nr = lax.axis_size("rep")
    rows = w_in.shape[1]
    total = -(-(seg + 6 * rows) // unit) * unit
    part = lambda c: pl.BlockSpec((1, rows, 3 * D), lambda i: (0, 0, c))
    return pl.pallas_call(
        functools.partial(pack_first_kernel, offsets["lead"], emb_table.shape[0], offsets["place"]),
        grid=(1,),
        in_specs=[SCALARS, whole(*emb_table.shape), part(0), part(2)],
        out_specs=[whole(total, D), whole(total // nr, D)],
        out_shape=[sds((total, D), BF), sds((total // nr, D), BF)],
        scratch_shapes=[pltpu.VMEM((seg, D), F32)],
        compiler_params=pltpu.CompilerParams(vmem_limit_bytes=VMEM_LIMIT),
    )(table, emb_table, w_in, w_in)


def pack_other_kernel(layouts, shard_place, table_ref, *refs):
    refs = list(refs)
    inputs = [[refs.pop(0) for _ in layout] for layout in layouts]
    shard_refs, mine_ref = refs[:-1], refs[-1]
    put = 0
    for layout, ins, shard_ref in zip(layouts, inputs, shard_refs):
        at = 0
        for ref, count in zip(ins, layout):
            rows = ref.shape[-2]
            for c in range(count):
                cols = slice(D * c, D * (c + 1))
                value = ref[0, :, cols] if len(ref.shape) == 3 else ref[:, cols]
                shard_ref[at : at + rows, :] = value.astype(BF)
                at += rows
            if len(ref.shape) == 2:
                value = ref[:, D * count :]
                shard_ref[at : at + rows, :] = jnp.concatenate(
                    [value, jnp.zeros((rows, D - value.shape[1]), F32)], axis=1
                ).astype(BF)
                at += rows
        if at < shard_ref.shape[0]:
            shard_ref[at:, :] = jnp.zeros_like(shard_ref[at:, :])
        rows = shard_ref.shape[0] * mine_ref.shape[0] // sum(r.shape[0] for r in shard_refs)
        from_rows = pl.ds(pl.multiple_of(table_ref[shard_place] * rows, rows), rows)
        mine_ref[put : put + rows, :] = shard_ref[from_rows, :]
        put += rows


def pack_other(table, offsets, shards):
    nr = lax.axis_size("rep")
    spec = lambda shape, index: pl.BlockSpec(shape, lambda i: index)
    parts = sum((p for _, p in shards), [])
    shapes = [(rows, D) for rows, _ in shards] + [(sum(rows for rows, _ in shards) // nr, D)]
    return pl.pallas_call(
        functools.partial(
            pack_other_kernel, tuple(tuple(p[3] for p in ps) for _, ps in shards), offsets["place"]
        ),
        grid=(1,),
        in_specs=[SCALARS] + [spec(p[1], p[2]) for p in parts],
        out_specs=[whole(*shape) for shape in shapes],
        out_shape=[sds(shape, BF) for shape in shapes],
        compiler_params=pltpu.CompilerParams(vmem_limit_bytes=VMEM_LIMIT),
    )(table, *[p[0] for p in parts])


def fill_full(full_ref, masks, place, member, table_ref, shard_ref, pieces):
    ng = full_ref.shape[0]
    full_ref[table_ref[member]] = shard_ref[...]
    for group, ref in zip(masks, pieces):
        rows = ref.shape[0] // (len(group) * (ng - 1))
        for i, mask in enumerate(group):
            at = pl.ds(pl.multiple_of(table_ref[place + mask] * rows, rows), rows)
            for k in range(1, ng):
                start = (i * (ng - 1) + k - 1) * rows
                full_ref[table_ref[member + k], at, :] = ref[start : start + rows, :]


def take_blocks(full_ref, start, count, out_ref):
    ng = full_ref.shape[0]
    step = D // ng
    for g in range(ng):
        for c in range(count):
            out_ref[step * g : step * (g + 1), D * c : D * (c + 1)] = full_ref[
                g, start + step * c : start + step * (c + 1), :
            ]
    return start + step * count


def take_outer(full_ref, start, wo_ref, wg_ref):
    ng = full_ref.shape[0]
    wide = (D + FF) // ng
    for g in range(ng):
        low, high = wide * g, wide * (g + 1)
        if low < D:
            cut = min(high, D)
            wo_ref[low:cut, :] = full_ref[g, start : start + cut - low, :]
        if high > D:
            cut = max(low, D)
            wg_ref[cut - D : high - D, :] = full_ref[g, start + cut - low : start + wide, :]
    return start + wide


def first_kernel(emb_rows, seg, masks, place, member, table_ref, shard_ref, feats_ref, labels_ref, *refs):
    pieces, rest = refs[: len(masks)], refs[len(masks) :]
    (wp_t_ref, w2_ref, wa_ref, wqkv_ref, wqkv_t_ref, mods_ref, time_act_ref, pre_ref, cond_ref, act_t_ref,
     full_ref, emb_ref) = rest
    fill_full(full_ref, masks, place, member, table_ref, shard_ref, pieces)
    ng = full_ref.shape[0]
    emb_ref[...] = jnp.zeros_like(emb_ref)
    for g in range(ng):
        base = emb_rows * g // 16 * 16
        emb_ref[base : base + seg, :] = emb_ref[base : base + seg, :] + full_ref[g, 0:seg, :]
    at = take_blocks(full_ref, seg, 3, wa_ref)
    take_blocks(full_ref, at, 3, wqkv_ref)
    wqkv_t_ref[...] = wqkv_ref[...].T
    wp_t_ref[...] = emb_ref[0:128, :].T[:, 0:PATCH_IN]
    w1 = emb_ref[PATCH_IN : PATCH_IN + FREQ, :]
    w2_ref[...] = emb_ref[PATCH_IN + FREQ : PATCH_IN + FREQ + D, :]
    classes = emb_ref[PATCH_IN + FREQ + D : PATCH_IN + FREQ + D + CLASSES + 8, :]
    pre = mm(feats_ref[...], w1)
    pre_ref[...] = pre
    time_act = swish_parts(pre)[0].astype(BF)
    time_act_ref[...] = time_act
    hot = labels_ref[...] == lax.broadcasted_iota(jnp.int32, (labels_ref.shape[0], CLASSES + 8), 1)
    cond = mm(time_act, w2_ref[...]) + mm(jnp.where(hot, 1.0, 0.0).astype(BF), classes)
    cond_ref[...] = cond
    act = swish_parts(cond)[0]
    act_t_ref[...] = act.T.astype(BF)
    mods_ref[...] = mm(wa_ref[...].T, act_t_ref[...])


def second_kernel(masks, place, member, table_ref, shard_ref, act_t_ref, *refs):
    pieces, rest = refs[: len(masks)], refs[len(masks) :]
    wo_ref, wg_ref, wo_t_ref, wg_t_ref, wf_ref, wf_t_ref, wa_ref, mods_ref, full_ref = rest
    fill_full(full_ref, masks, place, member, table_ref, shard_ref, pieces)
    at = take_outer(full_ref, 0, wo_ref, wg_ref)
    at = take_blocks(full_ref, at, 4, wf_ref)
    take_blocks(full_ref, at, 3, wa_ref)
    wo_t_ref[...] = wo_ref[...].T
    wg_t_ref[...] = wg_ref[...].T
    wf_t_ref[...] = wf_ref[...].T
    mods_ref[...] = mm(wa_ref[...].T, act_t_ref[...])


def third_kernel(masks, place, member, table_ref, shard_ref, act_t_ref, *refs):
    pieces, rest = refs[: len(masks)], refs[len(masks) :]
    (wo_ref, wg_ref, wo_t_ref, wg_t_ref, wf_ref, wf_t_ref, wqkv_ref, wqkv_t_ref, wa_ref, wm_ref, wy_ref, wy_t_ref,
     mods_ref, modf_ref, full_ref, wide_ref) = rest
    fill_full(full_ref, masks, place, member, table_ref, shard_ref, pieces)
    at = take_outer(full_ref, 0, wo_ref, wg_ref)
    at = take_blocks(full_ref, at, 6, wa_ref)
    at = take_blocks(full_ref, at, 3, wqkv_ref)
    at = take_blocks(full_ref, at, 4, wf_ref)
    at = take_blocks(full_ref, at, 2, wm_ref)
    take_blocks(full_ref, at, 1, wide_ref)
    wo_t_ref[...] = wo_ref[...].T
    wg_t_ref[...] = wg_ref[...].T
    wf_t_ref[...] = wf_ref[...].T
    wqkv_t_ref[...] = wqkv_ref[...].T
    wy_ref[...] = wide_ref[:, 0:PATCH_IN]
    wy_t_ref[...] = wide_ref[...].T[0:PATCH_IN, :]
    mods_ref[...] = mm(wa_ref[...].T, act_t_ref[...])
    modf_ref[...] = mm(wm_ref[...].T, act_t_ref[...])


def assemble(kernel, table, offsets, shard, pieces, extra, outs, scratch):
    ng = lax.axis_size("grp")
    masks = tuple(m for m, v in pieces if v is not None)
    arrays = [v for _, v in pieces if v is not None]
    return small_kernel(
        functools.partial(kernel, masks, offsets["place"], offsets["member"]), outs,
        [((ng,) + shard.shape, BF)] + scratch, (table, shard, *extra, *arrays),
    )


def cond_back_kernel(n, table_ref, gma0_ref, gmb0_ref, gma1_ref, gmb1_ref, gmf_ref, wa0a_ref, wa0b_ref, wa1_ref, wm_ref,
                     w2_ref, cond_ref, pre_ref, time_act_ref, feats_ref, label_ref, squares_ref, rows_ref):
    low = lambda ref: ref[...].astype(BF)
    gact = mm(wm_ref[...], low(gmf_ref))
    gact += mm(wa1_ref[:, 0 : 2 * D], low(gma1_ref)) + mm(wa1_ref[:, 2 * D :], low(gmb1_ref))
    gact += mm(wa0a_ref[:, 0 : 2 * D], low(gma0_ref)) + mm(wa0a_ref[:, 2 * D :], gmb0_ref[0:D, :].astype(BF))
    gact += mm(wa0b_ref[...], gmb0_ref[D:, :].astype(BF))
    gcond = gact.T * swish_parts(cond_ref[...])[1]
    gpre = mm_nt(gcond.astype(BF), w2_ref[...]) * swish_parts(pre_ref[...])[1]
    total = jnp.sum(squares_ref[...]).reshape(1, 1)
    high = total.astype(BF).astype(F32)
    middle = (total - high).astype(BF).astype(F32)
    last = total - high - middle
    lane = lax.broadcasted_iota(jnp.int32, (n, 128), 1)
    row = lax.broadcasted_iota(jnp.int32, (n, 128), 0)
    loss = jnp.where(lane == 0, high, jnp.where(lane == 1, middle, jnp.where(lane == 2, last, 0.0)))
    loss = jnp.where(row == 0, loss, 0.0)
    loss = jnp.where(lane == 3, label_ref[:, 0:1], jnp.where(lane == 4, label_ref[:, 1:2], loss))
    top = jnp.concatenate([time_act_ref[...].astype(F32)[0:n], gpre[0:n]], axis=0)
    feats = jnp.concatenate([feats_ref[...].astype(F32)[0:n], loss], axis=1)
    rows_ref[0 : 2 * n, :] = top.astype(BF)
    rows_ref[2 * n : 4 * n, :] = jnp.concatenate([gcond[0:n], feats], axis=0).astype(BF)


def emb_grad_kernel(n, inv_entries, counts, extra, table_ref, *refs):
    pieces, (grad_ref, loss_ref, left_ref, right_ref) = refs[: len(counts)], refs[len(counts) :]
    at = 0
    for ref, count in zip(pieces, counts):
        each = ref.shape[0] // count
        for i in range(count):
            for base in range(each * (i + 1) - extra, each * (i + 1), 4 * n):
                left_ref[at : at + 2 * n, :] = ref[base : base + 2 * n, :]
                right_ref[at : at + 2 * n, :] = ref[base + 2 * n : base + 4 * n, :]
                at += 2 * n
    total = left_ref.shape[0]
    row = lax.broadcasted_iota(jnp.int32, (total, D), 0)
    top = (row % (2 * n)) < n
    zero = jnp.zeros((total, D), BF)
    act = jnp.where(top, left_ref[...], zero)
    gcond = jnp.where(top, right_ref[...], zero)
    gpre = jnp.where(top, zero, left_ref[...])
    feats = right_ref[:, 0:FREQ]
    tags = right_ref[:, FREQ:].astype(F32).T
    label = (tags[3:4, :] * 32.0 + tags[4:5, :]).astype(jnp.int32)
    label = pltpu.roll(jnp.broadcast_to(label, (8, total)), total - n, 1)[0:1, :]
    hot = label == lax.broadcasted_iota(jnp.int32, (CLASSES + 8, total), 0)
    grad_ref[0:PATCH_IN, :] = jnp.zeros((PATCH_IN, D), F32)
    grad_ref[PATCH_IN : PATCH_IN + FREQ, :] = mm(feats.T, gpre)
    grad_ref[PATCH_IN + FREQ : PATCH_IN + FREQ + D, :] = mm(act.T, gcond)
    grad_ref[PATCH_IN + FREQ + D :, :] = mm(jnp.where(hot, 1.0, 0.0).astype(BF), gcond)
    spot = lax.broadcasted_iota(jnp.int32, tags.shape, 1) % (2 * n) >= n
    spot &= lax.broadcasted_iota(jnp.int32, tags.shape, 0) < 3
    loss_ref[...] = jnp.sum(jnp.where(spot, tags, 0.0)).reshape(1, 1) * inv_entries


def update_kernel(masks, place, sizes, step_rows, layout, extra, n_chain, table_ref, *refs):
    pieces, refs = refs[: len(masks)], refs[len(masks) :]
    states, refs = refs[:6], refs[6 + n_chain :]
    news, rest_refs, shard_refs = refs[:6], refs[6 : 6 + len(sizes)], refs[6 + len(sizes) :]
    step = pl.program_id(0)

    @pl.when(step == 0)
    def _():
        for group, ref in zip(masks, pieces):
            each = ref.shape[0] // len(group)
            for i, mask in enumerate(group):
                start = each * i
                for rows, shard_ref in zip(sizes, shard_refs):
                    at = pl.ds(pl.multiple_of(table_ref[place + mask] * rows, rows), rows)
                    shard_ref[at, :] = ref[start : start + rows, :]
                    start += rows
        for rest_ref, shard_ref in zip(rest_refs, shard_refs):
            rest_ref[...] = shard_ref[shard_ref.shape[0] - rest_ref.shape[0] :, :].astype(F32)

    out_rows = states[0].shape[1]
    at = pl.multiple_of(step * out_rows, 16)
    grad = shard_refs[0][pl.ds(at, out_rows), :].astype(F32)
    for ref, value in zip(news[:3], advance(*(r[0] for r in states[:3]), grad)):
        ref[0] = value
    for group, row, block in layout:
        cols = slice(D * block, D * (block + 1))
        at = pl.multiple_of(row + step * step_rows, 16)
        grad = shard_refs[group][pl.ds(at, step_rows), :].astype(F32)
        for ref, value in zip(news[3:], advance(*(r[0, :, cols] for r in states[3:]), grad)):
            ref[0, :, cols] = value


def update(table, offsets, pieces, layer, packs, extra, outer, inner, chain):
    nr = lax.axis_size("rep")
    rows, wide = inner[0].shape[1], inner[0].shape[2]
    rows_out = outer[0].shape[1]
    step_rows = 16
    steps = rows // step_rows
    masks = tuple(m for m, _ in pieces)
    arrays = [v for _, v in pieces]
    sizes = tuple(p[1] // nr for p in packs)
    layout = [(0, rows_out + rows * i, 9 + i) for i in range(4)]
    layout += [(0, rows_out + rows * (4 + i), 2 + i) for i in range(4)]
    layout += [(1, rows * i, 6 + i) for i in range(3)] + [(1, rows * (3 + i), i) for i in range(2)]
    rests = [packs[0][1] - rows_out - 8 * rows, packs[1][1] - 5 * rows]
    in_spec = pl.BlockSpec((1, step_rows, wide), lambda i: (layer, i, 0))
    out_spec = pl.BlockSpec((1, rows_out // steps, D), lambda i: (layer, i, 0))
    states = list(outer) + list(inner)
    specs = [out_spec] * 3 + [in_spec] * 3
    chain = list(chain) if chain else []
    first = 1 + len(arrays) + len(states)
    return pl.pallas_call(
        functools.partial(
            update_kernel, masks, offsets["place"], sizes, step_rows, tuple(layout), extra, len(chain)
        ),
        grid=(steps,),
        in_specs=[SCALARS] + [whole(*a.shape) for a in arrays] + specs
        + [pl.BlockSpec(memory_space=pl.ANY)] * len(chain),
        out_specs=specs + [whole(r, D) for r in rests],
        out_shape=[sds(s.shape, F32) for s in states] + [sds((r, D), F32) for r in rests],
        scratch_shapes=[pltpu.VMEM((p[1], D), BF) for p in packs],
        input_output_aliases={first + i: i for i in range(len(chain))},
        compiler_params=pltpu.CompilerParams(vmem_limit_bytes=VMEM_LIMIT),
    )(table, *arrays, *states, *chain)


def local(
    latents, noise, timesteps, labels, emb_table, emb_mom, emb_ema, w_in, in_mom, in_ema,
    w_out, out_mom, out_ema, head, head_mom, head_ema,
):
    nr, ng = lax.axis_size("rep"), lax.axis_size("grp")
    member = lax.axis_index("grp")
    n = latents.shape[0]
    B = IMAGES_PER_STEP
    unit = 16 * nr
    digits = digit_list(nr)
    rows_d = D // ng
    rows_out = (D + FF) // ng
    emb_rows = emb_table.shape[0]
    seg = -(-(emb_rows + 15) // 16) * 16
    emb_full = emb_rows * (ng - 1) // 16 * 16 + seg
    full_rows = lambda rows: -(-rows // unit) * unit
    table, offsets = place_table(emb_rows)

    shard1, mine1 = pack_first(table, offsets, emb_table, w_in, seg, unit)
    got1 = gather_members(mine1)
    three, one = (1, rows_d, 3 * D), (1, rows_d, D)
    shard2, shard3, mine23 = pack_other(
        table, offsets,
        [
            (full_rows(rows_out + 7 * rows_d),
             [(w_out, (1, rows_out, D), (0, 0, 0), 1), (w_in, three, (0, 0, 3), 3), (w_in, one, (0, 0, 12), 1),
              (w_in, three, (0, 0, 1), 3)]),
            (full_rows(rows_out + 16 * rows_d),
             [(w_out, (1, rows_out, D), (1, 0, 0), 1), (w_in, (1, rows_d, 13 * D), (1, 0, 0), 13),
              (head, head.shape, (0, 0), 2)]),
        ],
    )
    around1 = spread_outer(after(got1, mine23), nr)
    cut2 = shard2.shape[0] // nr
    came1 = [v for m, v in around1 if m != (0,)]
    got2 = gather_members(after(mine23[:cut2], came1[0]))
    around2 = spread_outer(got2, nr)
    mine3 = after(mine23[cut2:], *came1, got2)
    got3 = [swap(mine3, "grp", k) for k in range(1, ng)]

    levels = plan(timesteps)
    noise_level = jnp.sqrt(jnp.maximum(1.0 - levels, 0.0))
    noisy = (
        jnp.sqrt(levels)[:, None, None] * latents.astype(F32)
        + noise_level[:, None, None] * noise.astype(F32)
    ).astype(BF)
    feats = jnp.pad(time_features(timesteps).astype(BF), ((0, 128 - n), (0, 0)))
    label_column = jnp.pad(labels, (0, 128 - n), constant_values=-1)[:, None]
    label_parts = jnp.pad(
        jnp.stack([labels >> 5, labels & 31], axis=1).astype(F32), ((0, 0), (0, 126))
    )
    pos = positions()

    pieces1 = spread_core(
        [(sum((m for m, _ in around1), ()), jnp.concatenate([v for _, v in around1], axis=0))], nr
    )
    wp_t, w2, wa0a, wqkv0, wqkv0_t, mods0a, time_act, pre_time, cond, act_t = assemble(
        functools.partial(first_kernel, emb_rows, seg), table, offsets, shard1, pieces1,
        (feats, label_column),
        [((D, PATCH_IN), BF), ((D, D), BF), ((D, 3 * D), BF), ((D, 3 * D), BF), ((3 * D, D), BF),
         ((3 * D, 128), F32), ((128, D), BF), ((128, D), F32), ((128, D), F32), ((D, 128), BF)],
        [((emb_full, D), BF)],
    )
    early = att_forward(noisy, wp_t, pos, after(mods0a, got2), wqkv0_t, B, 0, 2, ())
    got3 = [after(g, early[0]) for g in got3]
    got3 = jnp.concatenate(got3, axis=0)
    around3 = spread_outer(got3, nr)
    qkv0, lse0, att0 = att_forward(noisy, wp_t, pos, after(mods0a, got3), wqkv0_t, B, 1, 2, early)
    pieces2 = spread_core([(m, after(v, att0)) for m, v in around2], nr)
    wo0, wg0, wo0_t, wg0_t, wf0, wf0_t, wa0b, mods0b = assemble(
        second_kernel, table, offsets, shard2, pieces2, (act_t,),
        [((D, D), BF), ((FF, D), BF), ((D, D), BF), ((D, FF), BF), ((D, FF), BF), ((FF, D), BF),
         ((D, 3 * D), BF), ((3 * D, 128), F32)],
        [],
    )
    mid0, bra0, brb0, hid1 = ffn_forward(noisy, wp_t, pos, att0, mods0a, mods0b, wo0_t, wf0_t, wg0_t, B)
    pieces3 = spread_core([(m, after(v, hid1)) for m, v in around3], nr)
    (wo1, wg1, wo1_t, wg1_t, wf1, wf1_t, wqkv1, wqkv1_t, wa1, wm, wy, wy_t, mods1, modf) = assemble(
        third_kernel, table, offsets, shard3, pieces3, (act_t,),
        [((D, D), BF), ((FF, D), BF), ((D, D), BF), ((D, FF), BF), ((D, FF), BF), ((FF, D), BF),
         ((D, 3 * D), BF), ((3 * D, D), BF), ((D, 6 * D), BF), ((D, 2 * D), BF), ((D, PATCH_IN), BF),
         ((PATCH_IN, D), BF), ((6 * D, 128), F32), ((2 * D, 128), F32)],
        [((D, D), BF)],
    )
    entries = n * nr * ng * TOK * PATCH_IN
    outer_pack = (ng, full_rows(rows_out + 8 * rows_d + PATCH_IN), D)
    qkv_pack1 = (ng, full_rows(7 * rows_d), D)
    qkv_pack0 = (ng, full_rows(5 * rows_d + PATCH_IN), D)
    qkv1, lse1, go1, gmid1, gmb1, gmf, squares, keep_f1, send_f1 = block_step(
        table, hid1, noise, mods1, modf, wqkv1_t, wo1_t, wf1_t, wg1_t, wo1, wf1, wg1, wy_t, wy, act_t,
        float(entries), B, outer_pack,
    )
    parts_f1 = reduce_first(keep_f1, send_f1)
    ghid1, gma1, keep_a1, send_a1 = att_backward(
        table, (hid1,), qkv1, lse1, go1, gmid1, mods1, wqkv1, act_t, gmf, B, False, qkv_pack1
    )
    parts_a1 = reduce_first(keep_a1, send_a1)

    def outer_stage(parts):
        sends = []
        for number in range(1, len(digits)):
            own, sends, shift = reduce_outer(parts, table, offsets, number)
            parts = exchange(own, sends, "rep", shift)
        return parts, sends

    def member_stage(groups, extra):
        own, sends, shift = reduce_members(groups, extra, table, offsets)
        return exchange(own, sends, "grp", shift), sends

    def held(parts, *marks):
        return [parts[0]] + [after(p, *marks) for p in parts[1:]]

    parts_f1, sends_f1 = outer_stage(held(parts_f1, ghid1))
    go0, gmid0, gmb0, keep_f0, send_f0 = ffn_backward(
        table, after(ghid1, *sends_f1), mid0, att0, bra0, brb0, mods0a, mods0b, wf0_t, wo0, wf0, wg0, act_t,
        B, outer_pack,
    )
    parts_f0 = reduce_first(keep_f0, send_f0)
    parts_f1 = held(parts_f1, gmid0)
    parts_a1, sends_a1 = outer_stage(held(parts_a1, gmid0, *parts_f1[1:]))
    back0 = functools.partial(
        att_backward, table, (noisy, wp_t, pos), qkv0, lse0, go0, mods=mods0a, wqkv=wqkv0, cond=act_t, gmf=None,
        B=B, bottom=True, pack=qkv_pack0, parts=2,
    )
    half = back0(gmid=after(gmid0, *sends_a1), part=0)
    mark = half[0]
    parts_1, sends_1 = member_stage([parts_f1, held(parts_a1, mark)], None)
    parts_f0, sends_f0 = outer_stage([after(p, *sends_1) for p in held(parts_f0, mark)])
    gma0, keep_a0, send_a0 = back0(gmid=after(gmid0, *sends_f0), part=1, before=half)
    parts_a0 = reduce_first(keep_a0, send_a0)
    parts_f0 = held(parts_f0, gma0)
    piece_1 = reduce_last(held(parts_1, gma0), 0, table)
    rows0 = small_kernel(
        functools.partial(cond_back_kernel, n), [((4 * n, D), BF)], [],
        (table, after(gma0, piece_1), gmb0, gma1, gmb1, gmf, wa0a, wa0b, wa1, wm, w2, cond, pre_time,
         time_act, feats, label_parts, squares),
    )[0]
    parts_a0, sends_a0 = outer_stage(held(parts_a0, rows0, *parts_f0[1:]))
    pieces_1 = spread_core(spread_outer(piece_1, nr), nr)
    outer_state, inner_state = (w_out, out_mom, out_ema), (w_in, in_mom, in_ema)
    new_1 = update(table, offsets, pieces_1, 1, (outer_pack, qkv_pack1), 0, outer_state, inner_state, None)
    parts_0, sends_0 = member_stage([parts_f0, parts_a0], rows0)
    piece_0 = reduce_last(parts_0, 4 * n, table)
    pieces_0 = spread_core(spread_outer(piece_0, nr), nr)
    extra = ng * 4 * n
    new_0 = update(table, offsets, pieces_0, 0, (outer_pack, qkv_pack0), extra, outer_state, inner_state, new_1[:6])
    emb_grad, loss_value = small_kernel(
        functools.partial(emb_grad_kernel, n, 1.0 / entries, tuple(len(m) for m, _ in pieces_0), extra),
        [((emb_full, D), F32), ((1, 1), F32)], [((2 * n * nr * ng, D), BF)] * 2,
        (table, *[v for _, v in pieces_0]),
    )
    emb_grad = lax.dynamic_slice_in_dim(emb_grad, member * emb_rows, emb_rows, 0)
    patch_grad = jnp.where(member == 0, new_0[7][:PATCH_IN], 0.0)
    emb_new = advance(
        emb_table, emb_mom, emb_ema, emb_grad + jnp.pad(patch_grad, ((0, emb_rows - PATCH_IN), (0, 0)))
    )
    wm_grad = new_1[7][: 2 * rows_d].reshape(2, rows_d, D).transpose(1, 0, 2).reshape(rows_d, 2 * D)
    wy_grad = lax.dynamic_slice_in_dim(new_1[6][:PATCH_IN], member * rows_d, rows_d, 1).T
    head_new = advance(head, head_mom, head_ema, jnp.concatenate([wm_grad, wy_grad], axis=1))
    return (loss_value.reshape(()), *emb_new, *new_0[3:6], *new_0[:3], *head_new)


def solution(mesh):
    data = P(("rep", "grp"), None, None)
    vector = P(("rep", "grp"))
    flat = P("grp", None)
    deep = P(None, "grp", None)
    return jax.shard_map(
        local,
        mesh=mesh,
        in_specs=(data, data, vector, vector, flat, flat, flat, deep, deep, deep, deep, deep, deep,
                  flat, flat, flat),
        out_specs=(P(), flat, flat, flat, deep, deep, deep, deep, deep, deep, flat, flat, flat),
        check_vma=False,
    )
```

time: 604 us -> 420 us (0.70); the launches traced: 592 us -> 415 us
  local copies, waits for them, and re-layouts: 116 us -> 15.2 us
  Pallas kernels: 224 us -> 287 us
  waiting for transfers between devices: 90.7 us -> 43.2 us
  starting transfers between devices: 106 us -> 59.9 us
  other arithmetic: 31.3 us -> 7.41 us
  matrix products: 19.1 us -> 0 us
    pallas_call x14 -> x25, Pallas kernels: 224 us -> 287 us  [the longest x8 208 us: run_kernel(): pl.pallas_call(kernel, grid=(steps,), in_specs=in_specs, out_specs=out_sp...]
    ppermute x110 -> x63, waiting for transfers between devices: 90.7 us -> 43.2 us  [swap(): return lax.ppermute(x, axis, pairs)]
    ppermute x110 -> x63, starting transfers between devices: 106 us -> 59.9 us  [swap(): return lax.ppermute(x, axis, pairs)]
    concatenate x13 -> x3, local copies, waits for them, and re-layouts: 33.8 us -> 0.1 us  [the longest x1 0.05 us: local(): jnp.concatenate([v for _, v in around1], axis=0)]
    ppermute x12 -> x0, local copies, waits for them, and re-layouts: 21.4 us -> none  [swap(): return lax.ppermute(x, axis, pairs)]
    unnamed x228 -> x135, local copies, waits for them, and re-layouts: 31.7 us -> 10.9 us
    dot_general x15 -> x0, matrix products: 19.1 us -> none  [the longest x5 8.46 us: tall_dot(): lax.dot_general(left, right, (((0,), (0,)), ((), ())), preferred_element_...]
    convert_element_type x23 -> x2, other arithmetic: 11.8 us -> 0.01 us  [the longest x1 0.01 us: local(): jnp.stack([labels >> 5, labels & 31], axis=1).astype(F32)]
  transfers between devices with their start and end apart: 110 -> 63, of which waited for: 27 -> 17; matrix products, arithmetic and copies ran while one was open for 20% -> 2% of each run, Pallas kernels for 14% -> 46%
where the time goes in v2:
time: 420 us; the launch traced here: 415 us
  Pallas kernels  287 us (68%)
  starting transfers between devices  59.9 us (14%)
  waiting for transfers between devices  43.2 us (10%)
  local copies, waits for them, and re-layouts  15.2 us (4%)
  other arithmetic  7.41 us (2%)
    pallas_call x8, Pallas kernels, run_kernel(): pl.pallas_call(kernel, grid=(steps,), in_specs=in_specs, out_specs=out_sp...  208 us
    ppermute x63, starting transfers between devices, swap(): return lax.ppermute(x, axis, pairs)  59.9 us
    ppermute x63, waiting for transfers between devices, swap(): return lax.ppermute(x, axis, pairs)  43.2 us
    pallas_call x9, Pallas kernels, small_kernel(): pl.pallas_call(kernel, in_specs=[SCALARS] * scalars + [in_vmem()] * (len(...  38.8 us
    pallas_call x2, Pallas kernels, update(): pl.pallas_call(functools.partial(update_kernel, masks, offsets['place'],...  17.5 us
    pallas_call x4, Pallas kernels, reduce_outer(): pl.pallas_call(functools.partial(rows_kernel, len(parts), offsets[shift])...  16.2 us
    unnamed x135, local copies, waits for them, and re-layouts  10.9 us
  transfers between devices with their start and end apart: 63, of which 17 were waited for; matrix products, arithmetic and copies ran while one was open for 2% of the time, Pallas kernels for 46%

profile of v2, /device:TPU:0, one launch (start us, length us, event | category | flops | bytes accessed | tf_op | source)
XLA Modules:
  0.0 415.1 jit_solution(11226566913849226952)
XLA Ops:
  1.4 2.7 shard_map.255
  4.0 3.0 collective-permute-start
  7.1 2.6 collective-permute-start.1
  10.5 4.0 shard_map.256
  14.5 3.2 collective-permute-done.1
  22.1 5.6 %collective-permute-done.3 = bf16[384,384]{1,0:T(8,128)(2,1)S(1)} collective-permute-done((bf16[384,384]{1,0:T(8,128)(2,1)S(1)}, bf16[384,384]{1,0:T(8,128)(2,1)S(1)}, u32[]{:S(2)}, u32[]{:S(2)}) %collective-permute-start.3) | collective-permute-done | bytes 294944 | tf_op jit(solution)/shard_map/ppermute | solution.py:612
  27.8 5.2 %collective-permute-done.4 = bf16[384,384]{1,0:T(8,128)(2,1)S(1)} collective-permute-done((bf16[384,384]{1,0:T(8,128)(2,1)S(1)}, bf16[384,384]{1,0:T(8,128)(2,1)S(1)}, u32[]{:S(2)}, u32[]{:S(2)}) %collective-permute-start.4) | collective-permute-done | bytes 294944 | tf_op jit(solution)/shard_map/ppermute | solution.py:612
  40.9 8.6 %collective-permute-done.8 = bf16[144,384]{1,0:T(8,128)(2,1)S(1)} collective-permute-done((bf16[144,384]{1,0:T(8,128)(2,1)S(1)}, bf16[144,384]{1,0:T(8,128)(2,1)S(1)}, u32[]{:S(2)}, u32[]{:S(2)}) %collective-permute-start.8) | collective-permute-done | bytes 110624 | tf_op jit(solution)/shard_map/ppermute | solution.py:612
  56.5 5.0 %shard_map.257 = (bf16[384,16]{1,0:T(8,128)(2,1)}, bf16[384,384]{1,0:T(8,128)(2,1)}, bf16[384,1152]{1,0:T(8,128)(2,1)}, bf16[384,1152]{1,0:T(8,128)(2,1)}, bf16[...) custom-call(s32[19]{0:T(128)} %stack.88.table_ref.refs_0_, ...), custom_call_target="tpu_custom_call" | custom-call | flops 8000000000 | tf_op jit(solution)/shard_map/pallas_call | solution.py:655
  61.6 13.0 %shard_map.258 = (bf16[8,1152,256]{2,1,0:T(8,128)(2,1)}, f32[8,8,256]{2,1,0:T(8,128)}, bf16[8,384,256]{2,1,0:T(8,128)(2,1)}) custom-call(bf16[8,16,256]{2,1,0:T(8,128)(2,1)} %add_convert_fusion.noisy_ref.refs_1_, bf16[384,16]{1,0:T(8,128)(2,1)} %get-tuple-element.167.wp_t_ref.refs_2_, f32[384,256]{1,0:T(8,128)} %pad_maximum_fusion.pos_ref.refs_3_, ...), custom_call_target="tpu_custom_call" | custom-call | flops 10468982784 | bytes 8302592 | tf_op jit(solution)/shard_map/pallas_call | solution.py:443
  76.2 13.3 %shard_map.259 = (bf16[8,1152,256]{2,1,0:T(8,128)(2,1)}, f32[8,8,256]{2,1,0:T(8,128)}, bf16[8,384,256]{2,1,0:T(8,128)(2,1)}) custom-call(bf16[8,16,256]{2,1,0:T(8,128)(2,1)} %add_convert_fusion.noisy_ref.refs_1_, bf16[384,16]{1,0:T(8,128)(2,1)} %get-tuple-element.167.wp_t_ref.refs_2_, ...), custom_call_target="tpu_custom_call", output_to_operand_aliasing={{0}: (5, {}), {1}: (6, {}), {2}: (7, {})} | custom-call | flops 10468982784 | bytes 14659584 | tf_op jit(solution)/shard_map/pallas_call | solution.py:443
  95.0 5.4 %shard_map.260 = (bf16[384,384]{1,0:T(8,128)(2,1)}, bf16[1536,384]{1,0:T(8,128)(2,1)}, bf16[384,384]{1,0:T(8,128)(2,1)}, bf16[384,1536]{1,0:T(8,128)(2,1)}, bf16...) custom-call(s32[19]{0:T(128)} %stack.88.table_ref.refs_0_, ...), custom_call_target="tpu_custom_call" | custom-call | flops 8000000000 | tf_op jit(solution)/shard_map/pallas_call | solution.py:655
  100.4 15.4 %shard_map.261 = (f32[8,384,256]{2,1,0:T(8,128)}, f32[8,384,256]{2,1,0:T(8,128)}, f32[8,384,256]{2,1,0:T(8,128)}, f32[8,384,256]{2,1,0:T(8,128)}) custom-call(bf16[8,16,256]{2,1,0:T(8,128)(2,1)} %add_convert_fusion.noisy_ref.refs_1_, bf16[384,16]{1,0:T(8,128)(2,1)} %get-tuple-element.167.wp_t_ref.refs_2_, f32[384,256]{1,0:T(8,128)} %pad_maximum_fusion.pos_ref.refs_3_, ...), custom_call_target="tpu_custom_call" | custom-call | flops 43486543872 | bytes 18460672 | tf_op jit(solution)/shard_map/pallas_call | solution.py:443
  116.4 2.9 collective-permute-done.21.refs_2_
  122.3 7.9 %shard_map.262 = (bf16[384,384]{1,0:T(8,128)(2,1)}, bf16[1536,384]{1,0:T(8,128)(2,1)}, bf16[384,384]{1,0:T(8,128)(2,1)}, bf16[384,1536]{1,0:T(8,128)(2,1)}, bf16...) custom-call(s32[19]{0:T(128)} %stack.88.table_ref.refs_0_, ...), custom_call_target="tpu_custom_call" | custom-call | flops 8000000000 | tf_op jit(solution)/shard_map/pallas_call | solution.py:655
  130.3 69.9 %shard_map.263 = (bf16[8,1152,256]{2,1,0:T(8,128)(2,1)}, f32[8,8,256]{2,1,0:T(8,128)}, bf16[8,384,256]{2,1,0:T(8,128)(2,1)}, f32[8,384,256]{2,1,0:T(8,128)}, f32...) custom-call(s32[19]{0:T(128)} %stack.88.table_ref.refs_0_, ...), custom_call_target="tpu_custom_call" | custom-call | flops 151397597184 | bytes 25731148 | tf_op jit(solution)/shard_map/pallas_call | solution.py:443
  200.3 28.0 %shard_map.264 = (f32[8,384,256]{2,1,0:T(8,128)}, f32[768,128]{1,0:T(8,128)}, bf16[4,384,384]{2,1,0:T(8,128)(2,1)}, bf16[4,384,384]{2,1,0:T(8,128)(2,1)}) custom-call(s32[19]{0:T(128)} %stack.88.table_ref.refs_0_, f32[8,384,256]{2,1,0:T(8,128)} %get-tuple-element.191.hid_ref.refs_1_, bf16[8,1152,256]{2,1,0:T(8,128)(2,1)} %get-tuple-element.208.refs_2_, ...), custom_call_target="tpu_custom_call" | custom-call | flops 45097156608 | bytes 21102668 | tf_op jit(solution)/shard_map/pallas_call | solution.py:443
  230.1 4.4 %shard_map.265 = (bf16[4,160,384]{2,1,0:T(8,128)(2,1)}, bf16[4,160,384]{2,1,0:T(8,128)(2,1)}, bf16[4,160,384]{2,1,0:T(8,128)(2,1)}, bf16[4,160,384]{2,1,0:T(8,128)(2,1)}) custom-call(s32[19]{0:T(128)} %stack.88.table_ref.refs_0_, bf16[4,640,384]{2,1,0:T(8,128)(2,1)} %get-tuple-element.215.refs_0_, bf16[4,640,384]{2,1,0:T(8,128)(2,1)} %copy-done.2), custom_call_target="tpu_custom_call" | custom-call | tf_op jit(solution)/shard_map/pallas_call | solution.py:740
  238.0 37.1 %shard_map.266 = (bf16[8,384,256]{2,1,0:T(8,128)(2,1)}, f32[8,384,256]{2,1,0:T(8,128)}, f32[1536,128]{1,0:T(8,128)}, bf16[4,640,384]{2,1,0:T(8,128)(2,1)}, bf16[4,640,384]{2,1,0:T(8,128)(2,1)}) custom-call(s32[19]{0:T(128)} %stack.88.table_ref.refs_0_, f32[8,384,256]{2,1,0:T(8,128)} %get-tuple-element.221.ghid_ref, ...), custom_call_target="tpu_custom_call" | custom-call | flops 106300440576 | bytes 28704844 | tf_op jit(solution)/shard_map/pallas_call | solution.py:443
  277.4 3.8 shard_map.267
  284.7 15.1 %shard_map.268 = (f32[768,128]{1,0:T(8,128)}, f32[384,1152]{1,0:T(8,128)}, f32[16,384]{1,0:T(8,128)}) custom-call(s32[19]{0:T(128)} %stack.88.table_ref.refs_0_, bf16[8,16,256]{2,1,0:T(8,128)(2,1)} %add_convert_fusion.noisy_ref.refs_1_, bf16[384,16]{1,0:T(8,128)(2,1)} %get-tuple-element.167.wp_t_ref.refs_2_, f32[384,256]{1,0:T(8,128)} %pad_maximum_fusion.pos_ref.refs_3_, ...), custom_call_target="tpu_custom_call" | custom-call | flops 22548578304 | bytes 13733964 | tf_op jit(solution)/shard_map/pallas_call | solution.py:443
  300.8 3.4 shard_map.269
  309.9 4.4 %shard_map.270 = (bf16[4,160,384]{2,1,0:T(8,128)(2,1)}, bf16[4,160,384]{2,1,0:T(8,128)(2,1)}, bf16[4,160,384]{2,1,0:T(8,128)(2,1)}, bf16[4,160,384]{2,1,0:T(8,128)(2,1)}) custom-call(s32[19]{0:T(128)} %stack.88.table_ref.refs_0_, bf16[4,640,384]{2,1,0:T(8,128)(2,1)} %get-tuple-element.253.refs_0_, bf16[4,640,384]{2,1,0:T(8,128)(2,1)} %copy-done.1), custom_call_target="tpu_custom_call" | custom-call | tf_op jit(solution)/shard_map/pallas_call | solution.py:740
  316.5 16.5 %shard_map.271 = (f32[768,128]{1,0:T(8,128)}, bf16[4,256,384]{2,1,0:T(8,128)(2,1)}, bf16[4,256,384]{2,1,0:T(8,128)(2,1)}) custom-call(s32[19]{0:T(128)} %stack.88.table_ref.refs_0_, bf16[8,16,256]{2,1,0:T(8,128)(2,1)} %add_convert_fusion.noisy_ref.refs_1_, bf16[384,16]{1,0:T(8,128)(2,1)} %get-tuple-element.167.wp_t_ref.refs_2_, ...), custom_call_target="tpu_custom_call" | custom-call | flops 22548578304 | bytes 15700044 | tf_op jit(solution)/shard_map/pallas_call | solution.py:443
  337.1 5.4 %shard_map.273.refs_8_ = bf16[32,384]{1,0:T(8,128)(2,1)} custom-call(s32[19]{0:T(128)} %stack.88.table_ref.refs_0_, f32[768,128]{1,0:T(8,128)} %get-tuple-element.274.gma0_ref, f32[1536,128]{1,0:T(8,128)} %get-tuple-element.275.gmb0_ref, f32[768,128]{1,0:T(8,128)} %get-tuple-element.276.gma1_ref, f32[1536,128]{1,0:T(8,128)} %get-tuple-element.277.gmb1_ref, ...), custom_call_target="tpu_custom_call" | custom-call | flops 8000000000 | tf_op jit(solution)/shard_map/pallas_call | solution.py:655
  345.4 3.6 shard_map.274
  362.5 3.2 shard_map.275
  372.5 5.3 %collective-permute-done.47.refs_2_ = bf16[256,384]{1,0:T(8,128)(2,1)S(1)} collective-permute-done((bf16[256,384]{1,0:T(8,128)(2,1)}, bf16[256,384]{1,0:T(8,128)(2,1)S(1)}, u32[]{:S(2)}, u32[]{:S(2)}) %collective-permute-start.47) | collective-permute-done | bytes 196640 | tf_op jit(solution)/shard_map/ppermute | solution.py:612
  384.2 8.8 %shard_map.278 = (f32[2,480,384]{2,1,0:T(8,128)}, f32[2,480,384]{2,1,0:T(8,128)}, f32[2,480,384]{2,1,0:T(8,128)}, f32[2,96,4992]{2,1,0:T(8,128)}, f32[2,96,4992]...) custom-call(s32[19]{0:T(128)} %stack.88.table_ref.refs_0_, ...), custom_call_target="tpu_custom_call" | custom-call | tf_op jit(solution)/shard_map/pallas_call | solution.py:1067
  398.4 8.7 %shard_map.279 = (f32[2,480,384]{2,1,0:T(8,128)}, f32[2,480,384]{2,1,0:T(8,128)}, f32[2,480,384]{2,1,0:T(8,128)}, f32[2,96,4992]{2,1,0:T(8,128)}, f32[2,96,4992]...) custom-call(s32[19]{0:T(128)} %stack.88.table_ref.refs_0_, ...), custom_call_target="tpu_custom_call", output_to_operand_aliasing={{0}: (15, {}), {1}: (16, {}), {2}: (17, {}), {3}: (18, {}),... | custom-call | tf_op jit(solution)/shard_map/pallas_call | solution.py:1067
  407.8 4.3 %shard_map.277 = (f32[1664,384]{1,0:T(8,128)}, f32[1,1]{1,0:T(1,128)}) custom-call(s32[19]{0:T(128)} %stack.88.table_ref.refs_0_, bf16[352,384]{1,0:T(8,128)(2,1)} %shard_map.276.refs_0_, bf16[352,384]{1,0:T(8,128)(2,1)} %copy-done.12, bf16[352,384]{1,0:T(8,128)(2,1)} %copy-done.13, bf16[352,384]{1,0:T(8,128)(2,1)} %copy-done.14, ...), custom_call_target="tpu_custom_call" | custom-call | flops 8000000000 | tf_op jit(solution)/shard_map/pallas_call | solution.py:655
  412.1 2.5 multiply_add_fusion
  (287 shorter events, 90.8 us)
Async XLA Ops:
  20.1 12.9 %collective-permute-start.4 = (bf16[384,384]{1,0:T(8,128)(2,1)S(1)}, bf16[384,384]{1,0:T(8,128)(2,1)S(1)}, u32[]{:S(2)}, u32[]{:S(2)}) collective-permute-start(bf16[384,384]{1,0:T(8,128)(2,1)S(1)} %pad_maximum_fusion.2), channel_id=1, source_target_pairs={{0,16},{4,20},{8,24},{12,28},{16,0},{20,4},{24,8},{28,12},{1,17},{... | collective-permute-start | bytes 884744 | tf_op jit(solution)/shard_map/ppermute | solution.py:612
  33.1 22.4 %collective-permute-start.6 = (bf16[1536,384]{1,0:T(8,128)(2,1)S(1)}, bf16[1536,384]{1,0:T(8,128)(2,1)S(1)}, u32[]{:S(2)}, u32[]{:S(2)}) collective-permute-start(bf16[1536,384]{1,0:T(8,128)(2,1)S(1)} %constant_dynamic-update-slice_fusion.refs_0_), channel_id=1, source_target_pairs={{0,4},{4,0},{8,12},{12,8},{16,20},{20,16},{24,28},{28,24},{1,5},{5... | collective-permute-start | bytes 3538952 | tf_op jit(solution)/shard_map/ppermute | solution.py:612
  49.6 25.0 %collective-permute-start.12 = (bf16[256,384]{1,0:T(8,128)(2,1)S(1)}, bf16[256,384]{1,0:T(8,128)(2,1)S(1)}, u32[]{:S(2)}, u32[]{:S(2)}) collective-permute-start(bf16[256,384]{1,0:T(8,128)(2,1)S(1)} %slice.15), channel_id=1, source_target_pairs={{0,3},{1,2},{2,1},{3,0},{4,7},{5,6},{6,5},{7,4},{8,11},{9,10},{10,... | collective-permute-start | bytes 589832 | tf_op jit(solution)/shard_map/ppermute | solution.py:612
  51.6 24.5 %collective-permute-start.11 = (bf16[256,384]{1,0:T(8,128)(2,1)S(1)}, bf16[256,384]{1,0:T(8,128)(2,1)S(1)}, u32[]{:S(2)}, u32[]{:S(2)}) collective-permute-start(bf16[256,384]{1,0:T(8,128)(2,1)S(1)} %slice.15), channel_id=1, source_target_pairs={{0,2},{1,3},{2,0},{3,1},{4,6},{5,7},{6,4},{7,5},{8,10},{9,11},{10,... | collective-permute-start | bytes 589832 | tf_op jit(solution)/shard_map/ppermute | solution.py:612
  53.1 23.0 %collective-permute-start.10 = (bf16[256,384]{1,0:T(8,128)(2,1)S(1)}, bf16[256,384]{1,0:T(8,128)(2,1)S(1)}, u32[]{:S(2)}, u32[]{:S(2)}) collective-permute-start(bf16[256,384]{1,0:T(8,128)(2,1)S(1)} %slice.15), channel_id=1, source_target_pairs={{0,1},{1,0},{2,3},{3,2},{4,5},{5,4},{6,7},{7,6},{8,9},{9,8},{10,11... | collective-permute-start | bytes 589832 | tf_op jit(solution)/shard_map/ppermute | solution.py:612
  54.0 35.5 %collective-permute-start.15 = (bf16[432,384]{1,0:T(8,128)(2,1)S(1)}, bf16[432,384]{1,0:T(8,128)(2,1)S(1)}, u32[]{:S(2)}, u32[]{:S(2)}) collective-permute-start(bf16[432,384]{1,0:T(8,128)(2,1)S(1)} %constant_dynamic-update-slice_fusion.4.refs_0_), channel_id=1, source_target_pairs={{0,24},{4,28},{8,16},{12,20},{16,8},{20,12},{24,0},{28,4},{1,25},{... | collective-permute-start | bytes 995336 | tf_op jit(solution)/shard_map/ppermute | solution.py:612
  55.5 34.1 %collective-permute-start.14 = (bf16[432,384]{1,0:T(8,128)(2,1)S(1)}, bf16[432,384]{1,0:T(8,128)(2,1)S(1)}, u32[]{:S(2)}, u32[]{:S(2)}) collective-permute-start(bf16[432,384]{1,0:T(8,128)(2,1)S(1)} %constant_dynamic-update-slice_fusion.4.refs_0_), channel_id=1, source_target_pairs={{0,16},{4,20},{8,24},{12,28},{16,0},{20,4},{24,8},{28,12},{1,17},{... | collective-permute-start | bytes 995336 | tf_op jit(solution)/shard_map/ppermute | solution.py:612
  74.6 15.5 %collective-permute-start.13 = (bf16[432,384]{1,0:T(8,128)(2,1)S(1)}, bf16[432,384]{1,0:T(8,128)(2,1)S(1)}, u32[]{:S(2)}, u32[]{:S(2)}) collective-permute-start(bf16[432,384]{1,0:T(8,128)(2,1)S(1)} %constant_dynamic-update-slice_fusion.4.refs_0_), channel_id=1, source_target_pairs={{0,8},{4,12},{8,0},{12,4},{16,24},{20,28},{24,16},{28,20},{1,9},{5... | collective-permute-start | bytes 995336 | tf_op jit(solution)/shard_map/ppermute | solution.py:612
  90.6 25.3 %collective-permute-start.22 = (bf16[768,384]{1,0:T(8,128)(2,1)S(1)}, bf16[768,384]{1,0:T(8,128)(2,1)S(1)}, u32[]{:S(2)}, u32[]{:S(2)}) collective-permute-start(bf16[768,384]{1,0:T(8,128)(2,1)S(1)} %constant_dynamic-update-slice_fusion.7.refs_0_), channel_id=1, source_target_pairs={{0,24},{4,28},{8,16},{12,20},{16,8},{20,12},{24,0},{28,4},{1,25},{... | collective-permute-start | bytes 1769480 | tf_op jit(solution)/shard_map/ppermute | solution.py:612
  91.6 27.7 %collective-permute-start.21 = (bf16[768,384]{1,0:T(8,128)(2,1)S(1)}, bf16[768,384]{1,0:T(8,128)(2,1)S(1)}, u32[]{:S(2)}, u32[]{:S(2)}) collective-permute-start(bf16[768,384]{1,0:T(8,128)(2,1)S(1)} %constant_dynamic-update-slice_fusion.7.refs_0_), channel_id=1, source_target_pairs={{0,16},{4,20},{8,24},{12,28},{16,0},{20,4},{24,8},{28,12},{1,17},{... | collective-permute-start | bytes 1769480 | tf_op jit(solution)/shard_map/ppermute | solution.py:612
  92.6 26.7 %collective-permute-start.20 = (bf16[768,384]{1,0:T(8,128)(2,1)S(1)}, bf16[768,384]{1,0:T(8,128)(2,1)S(1)}, u32[]{:S(2)}, u32[]{:S(2)}) collective-permute-start(bf16[768,384]{1,0:T(8,128)(2,1)S(1)} %constant_dynamic-update-slice_fusion.7.refs_0_), channel_id=1, source_target_pairs={{0,8},{4,12},{8,0},{12,4},{16,24},{20,28},{24,16},{28,20},{1,9},{5... | collective-permute-start | bytes 1769480 | tf_op jit(solution)/shard_map/ppermute | solution.py:612
  200.1 28.6 %collective-permute-start.27 = (bf16[4,640,384]{2,1,0:T(8,128)(2,1)}, bf16[4,640,384]{2,1,0:T(8,128)(2,1)S(1)}, u32[]{:S(2)}, u32[]{:S(2)}) collective-permute-start(bf16[4,640,384]{2,1,0:T(8,128)(2,1)} %get-tuple-element.216), channel_id=1, source_target_pairs={{0,4},{4,0},{8,12},{12,8},{16,20},{20,16},{24,28},{28,24},{1,5},{5... | collective-permute-start | bytes 5898248 | tf_op jit(solution)/shard_map/ppermute | solution.py:612
  228.3 47.0 %collective-permute-start.31 = (bf16[4,384,384]{2,1,0:T(8,128)(2,1)}, bf16[4,384,384]{2,1,0:T(8,128)(2,1)S(1)}, u32[]{:S(2)}, u32[]{:S(2)}) collective-permute-start(bf16[4,384,384]{2,1,0:T(8,128)(2,1)} %get-tuple-element.235), channel_id=1, source_target_pairs={{0,4},{4,0},{8,12},{12,8},{16,20},{20,16},{24,28},{28,24},{1,5},{5... | collective-permute-start | bytes 3538952 | tf_op jit(solution)/shard_map/ppermute | solution.py:612
  234.5 40.7 %collective-permute-start.30 = (bf16[4,160,384]{2,1,0:T(8,128)(2,1)}, bf16[4,160,384]{2,1,0:T(8,128)(2,1)S(1)}, u32[]{:S(2)}, u32[]{:S(2)}) collective-permute-start(bf16[4,160,384]{2,1,0:T(8,128)(2,1)} %get-tuple-element.220), channel_id=1, source_target_pairs={{0,24},{4,28},{8,16},{12,20},{16,8},{20,12},{24,0},{28,4},{1,25},{... | collective-permute-start | bytes 1474568 | tf_op jit(solution)/shard_map/ppermute | solution.py:612
  235.7 39.6 %collective-permute-start.29 = (bf16[4,160,384]{2,1,0:T(8,128)(2,1)}, bf16[4,160,384]{2,1,0:T(8,128)(2,1)S(1)}, u32[]{:S(2)}, u32[]{:S(2)}) collective-permute-start(bf16[4,160,384]{2,1,0:T(8,128)(2,1)} %get-tuple-element.219), channel_id=1, source_target_pairs={{0,16},{4,20},{8,24},{12,28},{16,0},{20,4},{24,8},{28,12},{1,17},{... | collective-permute-start | bytes 1474568 | tf_op jit(solution)/shard_map/ppermute | solution.py:612
  236.7 38.6 %collective-permute-start.28 = (bf16[4,160,384]{2,1,0:T(8,128)(2,1)}, bf16[4,160,384]{2,1,0:T(8,128)(2,1)S(1)}, u32[]{:S(2)}, u32[]{:S(2)}) collective-permute-start(bf16[4,160,384]{2,1,0:T(8,128)(2,1)} %get-tuple-element.218), channel_id=1, source_target_pairs={{0,8},{4,12},{8,0},{12,4},{16,24},{20,28},{24,16},{28,20},{1,9},{5... | collective-permute-start | bytes 1474568 | tf_op jit(solution)/shard_map/ppermute | solution.py:612
  275.2 33.4 %collective-permute-start.35 = (bf16[4,640,384]{2,1,0:T(8,128)(2,1)}, bf16[4,640,384]{2,1,0:T(8,128)(2,1)S(1)}, u32[]{:S(2)}, u32[]{:S(2)}) collective-permute-start(bf16[4,640,384]{2,1,0:T(8,128)(2,1)} %get-tuple-element.254), channel_id=1, source_target_pairs={{0,4},{4,0},{8,12},{12,8},{16,20},{20,16},{24,28},{28,24},{1,5},{5... | collective-permute-start | bytes 5898248 | tf_op jit(solution)/shard_map/ppermute | solution.py:612
  281.2 18.6 %collective-permute-start.34 = (bf16[4,96,384]{2,1,0:T(8,128)(2,1)}, bf16[4,96,384]{2,1,0:T(8,128)(2,1)S(1)}, u32[]{:S(2)}, u32[]{:S(2)}) collective-permute-start(bf16[4,96,384]{2,1,0:T(8,128)(2,1)} %get-tuple-element.243), channel_id=1, source_target_pairs={{0,24},{4,28},{8,16},{12,20},{16,8},{20,12},{24,0},{28,4},{1,25},{... | collective-permute-start | bytes 884744 | tf_op jit(solution)/shard_map/ppermute | solution.py:612
  282.4 17.4 %collective-permute-start.33 = (bf16[4,96,384]{2,1,0:T(8,128)(2,1)}, bf16[4,96,384]{2,1,0:T(8,128)(2,1)S(1)}, u32[]{:S(2)}, u32[]{:S(2)}) collective-permute-start(bf16[4,96,384]{2,1,0:T(8,128)(2,1)} %get-tuple-element.242), channel_id=1, source_target_pairs={{0,16},{4,20},{8,24},{12,28},{16,0},{20,4},{24,8},{28,12},{1,17},{... | collective-permute-start | bytes 884744 | tf_op jit(solution)/shard_map/ppermute | solution.py:612
  283.4 16.4 %collective-permute-start.32 = (bf16[4,96,384]{2,1,0:T(8,128)(2,1)}, bf16[4,96,384]{2,1,0:T(8,128)(2,1)S(1)}, u32[]{:S(2)}, u32[]{:S(2)}) collective-permute-start(bf16[4,96,384]{2,1,0:T(8,128)(2,1)} %get-tuple-element.238), channel_id=1, source_target_pairs={{0,8},{4,12},{8,0},{12,4},{16,24},{20,28},{24,16},{28,20},{1,9},{5... | collective-permute-start | bytes 884744 | tf_op jit(solution)/shard_map/ppermute | solution.py:612
  304.2 28.8 %collective-permute-start.42 = (bf16[256,384]{1,0:T(8,128)(2,1)}, bf16[256,384]{1,0:T(8,128)(2,1)S(1)}, u32[]{:S(2)}, u32[]{:S(2)}) collective-permute-start(bf16[256,384]{1,0:T(8,128)(2,1)} %get-tuple-element.252), channel_id=1, source_target_pairs={{0,3},{1,2},{2,1},{3,0},{4,7},{5,6},{6,5},{7,4},{8,11},{9,10},{10,... | collective-permute-start | bytes 589832 | tf_op jit(solution)/shard_map/ppermute | solution.py:612
  306.2 28.2 %collective-permute-start.41 = (bf16[256,384]{1,0:T(8,128)(2,1)}, bf16[256,384]{1,0:T(8,128)(2,1)S(1)}, u32[]{:S(2)}, u32[]{:S(2)}) collective-permute-start(bf16[256,384]{1,0:T(8,128)(2,1)} %get-tuple-element.251), channel_id=1, source_target_pairs={{0,2},{1,3},{2,0},{3,1},{4,6},{5,7},{6,4},{7,5},{8,10},{9,11},{10,... | collective-permute-start | bytes 589832 | tf_op jit(solution)/shard_map/ppermute | solution.py:612
  306.8 27.6 %collective-permute-start.40 = (bf16[256,384]{1,0:T(8,128)(2,1)}, bf16[256,384]{1,0:T(8,128)(2,1)S(1)}, u32[]{:S(2)}, u32[]{:S(2)}) collective-permute-start(bf16[256,384]{1,0:T(8,128)(2,1)} %get-tuple-element.250), channel_id=1, source_target_pairs={{0,1},{1,0},{2,3},{3,2},{4,5},{5,4},{6,7},{7,6},{8,9},{9,8},{10,11... | collective-permute-start | bytes 589832 | tf_op jit(solution)/shard_map/ppermute | solution.py:612
  314.3 28.2 %collective-permute-start.38 = (bf16[4,160,384]{2,1,0:T(8,128)(2,1)}, bf16[4,160,384]{2,1,0:T(8,128)(2,1)S(1)}, u32[]{:S(2)}, u32[]{:S(2)}) collective-permute-start(bf16[4,160,384]{2,1,0:T(8,128)(2,1)} %get-tuple-element.260), channel_id=1, source_target_pairs={{0,24},{4,28},{8,16},{12,20},{16,8},{20,12},{24,0},{28,4},{1,25},{... | collective-permute-start | bytes 1474568 | tf_op jit(solution)/shard_map/ppermute | solution.py:612
  315.5 27.0 %collective-permute-start.37 = (bf16[4,160,384]{2,1,0:T(8,128)(2,1)}, bf16[4,160,384]{2,1,0:T(8,128)(2,1)S(1)}, u32[]{:S(2)}, u32[]{:S(2)}) collective-permute-start(bf16[4,160,384]{2,1,0:T(8,128)(2,1)} %get-tuple-element.259), channel_id=1, source_target_pairs={{0,16},{4,20},{8,24},{12,28},{16,0},{20,4},{24,8},{28,12},{1,17},{... | collective-permute-start | bytes 1474568 | tf_op jit(solution)/shard_map/ppermute | solution.py:612
  352.5 15.7 %collective-permute-start.56 = (bf16[256,384]{1,0:T(8,128)(2,1)S(1)}, bf16[256,384]{1,0:T(8,128)(2,1)S(1)}, u32[]{:S(2)}, u32[]{:S(2)}) collective-permute-start(bf16[256,384]{1,0:T(8,128)(2,1)S(1)} %copy-done.19), channel_id=1, source_target_pairs={{0,8},{4,12},{8,0},{12,4},{16,24},{20,28},{24,16},{28,20},{1,9},{5... | collective-permute-start | bytes 589832 | tf_op jit(solution)/shard_map/ppermute | solution.py:612
  353.8 16.3 %collective-permute-start.57 = (bf16[256,384]{1,0:T(8,128)(2,1)S(1)}, bf16[256,384]{1,0:T(8,128)(2,1)S(1)}, u32[]{:S(2)}, u32[]{:S(2)}) collective-permute-start(bf16[256,384]{1,0:T(8,128)(2,1)S(1)} %copy-done.19), channel_id=1, source_target_pairs={{0,16},{4,20},{8,24},{12,28},{16,0},{20,4},{24,8},{28,12},{1,17},{... | collective-permute-start | bytes 589832 | tf_op jit(solution)/shard_map/ppermute | solution.py:612
  357.1 13.1 %collective-permute-start.58 = (bf16[256,384]{1,0:T(8,128)(2,1)S(1)}, bf16[256,384]{1,0:T(8,128)(2,1)S(1)}, u32[]{:S(2)}, u32[]{:S(2)}) collective-permute-start(bf16[256,384]{1,0:T(8,128)(2,1)S(1)} %copy-done.19), channel_id=1, source_target_pairs={{0,24},{4,28},{8,16},{12,20},{16,8},{20,12},{24,0},{28,4},{1,25},{... | collective-permute-start | bytes 589832 | tf_op jit(solution)/shard_map/ppermute | solution.py:612
  370.2 12.3 %collective-permute-start.60 = (bf16[256,384]{1,0:T(8,128)(2,1)S(1)}, bf16[256,384]{1,0:T(8,128)(2,1)S(1)}, u32[]{:S(2)}, u32[]{:S(2)}) collective-permute-start(bf16[256,384]{1,0:T(8,128)(2,1)S(1)} %collective-permute-done.56.refs_1_), channel_id=1, source_target_pairs={{0,4},{4,0},{8,12},{12,8},{16,20},{20,16},{24,28},{28,24},{1,5},{5... | collective-permute-start | bytes 589832 | tf_op jit(solution)/shard_map/ppermute | solution.py:612
  380.6 14.4 %collective-permute-start.49 = (bf16[352,384]{1,0:T(8,128)(2,1)}, bf16[352,384]{1,0:T(8,128)(2,1)S(1)}, u32[]{:S(2)}, u32[]{:S(2)}) collective-permute-start(bf16[352,384]{1,0:T(8,128)(2,1)} %shard_map.276.refs_0_), channel_id=1, source_target_pairs={{0,8},{4,12},{8,0},{12,4},{16,24},{20,28},{24,16},{28,20},{1,9},{5... | collective-permute-start | bytes 811016 | tf_op jit(solution)/shard_map/ppermute | solution.py:612
  381.4 14.0 %collective-permute-start.50 = (bf16[352,384]{1,0:T(8,128)(2,1)}, bf16[352,384]{1,0:T(8,128)(2,1)S(1)}, u32[]{:S(2)}, u32[]{:S(2)}) collective-permute-start(bf16[352,384]{1,0:T(8,128)(2,1)} %shard_map.276.refs_0_), channel_id=1, source_target_pairs={{0,16},{4,20},{8,24},{12,28},{16,0},{20,4},{24,8},{28,12},{1,17},{... | collective-permute-start | bytes 811016 | tf_op jit(solution)/shard_map/ppermute | solution.py:612
  382.5 13.5 %collective-permute-start.51 = (bf16[352,384]{1,0:T(8,128)(2,1)}, bf16[352,384]{1,0:T(8,128)(2,1)S(1)}, u32[]{:S(2)}, u32[]{:S(2)}) collective-permute-start(bf16[352,384]{1,0:T(8,128)(2,1)} %shard_map.276.refs_0_), channel_id=1, source_target_pairs={{0,24},{4,28},{8,16},{12,20},{16,8},{20,12},{24,0},{28,4},{1,25},{... | collective-permute-start | bytes 811016 | tf_op jit(solution)/shard_map/ppermute | solution.py:612
  (95 other events, 641.1 us)

commit v3 on v2

--- a/solution.py
+++ b/solution.py
@@ -62,52 +62,78 @@
     return jnp.where(keep, x, jnp.zeros_like(x))
 
 
-def attention_forward(qkv_ref, b, lse_ref, att_ref, att_lanes):
-    for pair in range(HEADS // 2):
-        lo = 2 * HEAD_DIM * pair
-        q2 = qkv_ref[b, lo : lo + 128, :]
-        k2 = qkv_ref[b, D + lo : D + lo + 128, :].T
-        for half in range(2):
-            head = 2 * pair + half
-            scores = mm(k2, half_zero(q2, half))
-            peak = jnp.max(scores, axis=0, keepdims=True)
-            exps = jnp.exp(scores - peak)
-            total = jnp.sum(exps, axis=0, keepdims=True)
-            vrow = 2 * D + HEAD_DIM * head
-            out = mm(qkv_ref[b, vrow : vrow + HEAD_DIM, :], exps.astype(BF))
-            att_ref[HEAD_DIM * head : HEAD_DIM * (head + 1), att_lanes] = (
-                out * (1.0 / total)
-            ).astype(BF)
-            lse_ref[b, head : head + 1, :] = peak + jnp.log(total)
-
-
-def attention_backward(qkv_ref, b, lse_ref, go_ref, gqkv_ref, lanes):
-    for pair in range(HEADS // 2):
-        lo = 2 * HEAD_DIM * pair
-        q2 = qkv_ref[b, lo : lo + 128, :]
-        k2 = qkv_ref[b, D + lo : D + lo + 128, :].T
-        v2 = qkv_ref[b, 2 * D + lo : 2 * D + lo + 128, :].T
-        g2 = go_ref[b, lo : lo + 128, :]
-        for half in range(2):
-            head = 2 * pair + half
-            row = HEAD_DIM * head
-            scores = mm(k2, half_zero(q2, half))
-            probs = jnp.exp(scores - lse_ref[b, head : head + 1, :])
-            gprobs = mm(v2, half_zero(g2, half))
-            inner = jnp.sum(probs * gprobs, axis=0, keepdims=True)
-            gscores = (probs * (gprobs - inner)).astype(BF)
-            gq = mm(qkv_ref[b, D + row : D + row + HEAD_DIM, :], gscores)
-            gk = mm_nt(qkv_ref[b, row : row + HEAD_DIM, :], gscores)
-            gv = mm_nt(go_ref[b, row : row + HEAD_DIM, :], probs.astype(BF))
-            gqkv_ref[row : row + HEAD_DIM, lanes] = (gq * (1.0 / math.sqrt(HEAD_DIM))).astype(BF)
-            gqkv_ref[D + row : D + row + HEAD_DIM, lanes] = gk.astype(BF)
-            gqkv_ref[2 * D + row : 2 * D + row + HEAD_DIM, lanes] = gv.astype(BF)
-
-
-def project_qkv(wqkv_t_ref, normed_ref, lanes, qkv_ref, b):
-    qkv = mm(wqkv_t_ref[...], normed_ref[:, lanes])
-    qkv_ref[b, 0:D, :] = (qkv[0:D] * (1.0 / math.sqrt(HEAD_DIM))).astype(BF)
-    qkv_ref[b, D:, :] = qkv[D:].astype(BF)
+def head_groups(B):
+    work = [(b, h) for b in range(B) for h in range(HEADS)]
+    return [work[i : i + HEAD_GROUP] for i in range(0, len(work), HEAD_GROUP)]
+
+
+def pair_rows(ref, b, h, base=0):
+    lo = base + 2 * HEAD_DIM * (h // 2)
+    return ref[b, lo : lo + 2 * HEAD_DIM, :]
+
+
+def head_rows(ref, b, h, base=0):
+    return ref[b, base + HEAD_DIM * h : base + HEAD_DIM * (h + 1), :]
+
+
+def attention_forward(qkv_ref, B, lse_ref, att_ref):
+    for work in head_groups(B):
+        scores = [
+            mm(pair_rows(qkv_ref, b, h, D).T, half_zero(pair_rows(qkv_ref, b, h), h % 2)) for b, h in work
+        ]
+        peaks = [jnp.max(x, axis=0, keepdims=True) for x in scores]
+        exps = [jnp.exp(x - p) for x, p in zip(scores, peaks)]
+        totals = [jnp.sum(x, axis=0, keepdims=True) for x in exps]
+        outs = [mm(head_rows(qkv_ref, b, h, 2 * D), x.astype(BF)) for (b, h), x in zip(work, exps)]
+        for (b, h), out, total, peak in zip(work, outs, totals, peaks):
+            att_ref[HEAD_DIM * h : HEAD_DIM * (h + 1), lanes_of(b)] = (out * (1.0 / total)).astype(BF)
+            lse_ref[b, h : h + 1, :] = peak + jnp.log(total)
+
+
+def attention_backward(qkv_ref, B, lse_ref, go_ref, gqkv_ref):
+    for work in head_groups(B):
+        scores = [
+            mm(pair_rows(qkv_ref, b, h, D).T, half_zero(pair_rows(qkv_ref, b, h), h % 2)) for b, h in work
+        ]
+        gprobs = [
+            mm(pair_rows(qkv_ref, b, h, 2 * D).T, half_zero(pair_rows(go_ref, b, h), h % 2)) for b, h in work
+        ]
+        probs = [jnp.exp(x - lse_ref[b, h : h + 1, :]) for x, (b, h) in zip(scores, work)]
+        inners = [jnp.sum(p * g, axis=0, keepdims=True) for p, g in zip(probs, gprobs)]
+        gscores = [(p * (g - i)).astype(BF) for p, g, i in zip(probs, gprobs, inners)]
+        gqs = [mm(head_rows(qkv_ref, b, h, D), g) for (b, h), g in zip(work, gscores)]
+        gks = [mm_nt(head_rows(qkv_ref, b, h), g) for (b, h), g in zip(work, gscores)]
+        gvs = [mm_nt(head_rows(go_ref, b, h), p.astype(BF)) for (b, h), p in zip(work, probs)]
+        for (b, h), gq, gk, gv in zip(work, gqs, gks, gvs):
+            row = HEAD_DIM * h
+            for base, value in ((0, gq * (1.0 / math.sqrt(HEAD_DIM))), (D, gk), (2 * D, gv)):
+                gqkv_ref[base + row : base + row + HEAD_DIM, lanes_of(b)] = value.astype(BF)
+
+
+def project_qkv(wqkv_t_ref, normed_ref, qkv_ref, B):
+    for part in range(3):
+        qkv = mm(wqkv_t_ref[D * part : D * (part + 1), :], normed_ref[...])
+        if part == 0:
+            qkv = qkv * (1.0 / math.sqrt(HEAD_DIM))
+        qkv = qkv.astype(BF)
+        for b in range(B):
+            qkv_ref[b, D * part : D * (part + 1), :] = qkv[:, TOK * b : TOK * (b + 1)]
+
+
+def lanes_of(b):
+    return slice(TOK * b, TOK * (b + 1))
+
+
+def modulate_into(normed_ref, b, normed, scale1, shift):
+    normed_ref[:, lanes_of(b)] = (normed * scale1 + shift).astype(BF)
+
+
+def ffn_chunks():
+    return [slice(f, f + FF_CHUNK) for f in range(0, FF, FF_CHUNK)]
+
+
+def add_up(total, part):
+    return part if total is None else total + part
 
 
 GELU_C = 0.7978845608
@@ -127,17 +153,13 @@
     return v * (0.5 + 0.5 * t)
 
 
-def accumulate(acc_ref, value, first):
-    @pl.when(first)
-    def _():
-        acc_ref[...] = value
-
-    @pl.when(jnp.logical_not(first))
-    def _():
-        acc_ref[...] += value
-
-
-FF_CHUNK = 512
+def clear(*refs):
+    for ref in refs:
+        ref[...] = jnp.zeros_like(ref)
+
+
+FF_CHUNK = 768
+HEAD_GROUP = 12
 
 
 def pack_blocks(pack_ref, start, value):
@@ -187,15 +209,13 @@
     step = pl.program_id(0)
     for b in range(B):
         image = (offset + step) * B + b
-        lanes = slice(TOK * b, TOK * (b + 1))
         hidden = mm(wp_t_ref[...], noisy_ref[b]) + pos_ref[...]
         normed, _ = norm_parts(hidden)
-        normed_ref[:, lanes] = (
-            normed * (1.0 + column(mods_ref, 1, image)) + column(mods_ref, 0, image)
-        ).astype(BF)
-        project_qkv(wqkv_t_ref, normed_ref, lanes, qkv_ref, b)
-        attention_forward(qkv_ref, b, lse_ref, att_ref, lanes)
-        att_out_ref[b] = att_ref[:, lanes]
+        modulate_into(normed_ref, b, normed, 1.0 + column(mods_ref, 1, image), column(mods_ref, 0, image))
+    project_qkv(wqkv_t_ref, normed_ref, qkv_ref, B)
+    attention_forward(qkv_ref, B, lse_ref, att_ref)
+    for b in range(B):
+        att_out_ref[b] = att_ref[:, lanes_of(b)]
 
 
 def ffn_fwd_kernel(B, noisy_ref, wp_t_ref, pos_ref, att_ref, mods_a_ref, mods_b_ref, wo_t_ref, wf_t_ref,
@@ -203,29 +223,21 @@
     step = pl.program_id(0)
     for b in range(B):
         image = step * B + b
-        lanes = slice(TOK * b, TOK * (b + 1))
         hidden = mm(wp_t_ref[...], noisy_ref[b]) + pos_ref[...]
         branch_a = mm(wo_t_ref[...], att_ref[b])
         bra_ref[b] = branch_a
         mid = hidden + column(mods_a_ref, 2, image) * branch_a
         mid_ref[b] = mid
         normed, _ = norm_parts(mid)
-        normed_ref[:, lanes] = (
-            normed * (1.0 + column(mods_b_ref, 1, image)) + column(mods_b_ref, 0, image)
-        ).astype(BF)
-        branch = None
-        for f in range(0, FF, FF_CHUNK):
-            pre = mm(wf_t_ref[f : f + FF_CHUNK, :], normed_ref[:, lanes])
-            part = mm(wg_t_ref[:, f : f + FF_CHUNK], gelu_one(pre).astype(BF))
-            branch = part if branch is None else branch + part
-        brb_ref[b] = branch
-        hid_ref[b] = mid + column(mods_b_ref, 2, image) * branch
-
-
-def out_bwd(b, image, lanes, gmid, branch, gate, wo_ref, gba_ref, go_ref, gm_ref, gm_base):
-    put_column(gm_ref, gm_base, image, gmid * branch)
-    gba_ref[:, lanes] = (gate * gmid).astype(BF)
-    go_ref[b] = mm(wo_ref[...], gba_ref[:, lanes]).astype(BF)
+        modulate_into(normed_ref, b, normed, 1.0 + column(mods_b_ref, 1, image), column(mods_b_ref, 0, image))
+    branch = None
+    for rows in ffn_chunks():
+        act = gelu_one(mm(wf_t_ref[rows, :], normed_ref[...])).astype(BF)
+        branch = add_up(branch, mm(wg_t_ref[:, rows], act))
+    for b in range(B):
+        own = branch[:, lanes_of(b)]
+        brb_ref[b] = own
+        hid_ref[b] = mid_ref[b] + column(mods_b_ref, 2, step * B + b) * own
 
 
 def block_kernel(B, entries, table_ref, hid_ref, noise_ref, mods_ref, modf_ref, wqkv_t_ref, wo_t_ref, wf_t_ref,
@@ -233,71 +245,72 @@
                  qkv_ref, lse_ref, go_ref, gmid_ref, gm_ref, gmf_ref, loss_ref,
                  keep_ref, send_ref,
                  pack_ref, normed_ref, att_ref, slope_ref, act_ref, gpre_ref, gba_ref, gbb_ref, normf_ref, gout_ref,
-                 awo_ref, awf_ref, awg_ref, awy_ref):
+                 awo_ref, awf_ref, awg_ref, awy_ref, bra_ref, ghid_ref):
     step = pl.program_id(0)
     first = step == 0
 
     @pl.when(first)
     def _():
-        gm_ref[...] = jnp.zeros_like(gm_ref)
-        gmf_ref[...] = jnp.zeros_like(gmf_ref)
-        loss_ref[...] = jnp.zeros_like(loss_ref)
-
-    for b in range(B):
-        image = step * B + b
-        lanes = slice(TOK * b, TOK * (b + 1))
-        hidden = hid_ref[b]
-        normed, _ = norm_parts(hidden)
-        normed_ref[:, lanes] = (
-            normed * (1.0 + column(mods_ref, 1, image)) + column(mods_ref, 0, image)
-        ).astype(BF)
-        project_qkv(wqkv_t_ref, normed_ref, lanes, qkv_ref, b)
-        attention_forward(qkv_ref, b, lse_ref, att_ref, lanes)
-        branch_a = mm(wo_t_ref[...], att_ref[:, lanes])
-        gate_a = column(mods_ref, 2, image)
-        mid = hidden + gate_a * branch_a
-        normed_b, inv_b = norm_parts(mid)
-        scale_b = 1.0 + column(mods_ref, 4, image)
-        normed_ref[:, lanes] = (normed_b * scale_b + column(mods_ref, 3, image)).astype(BF)
-        branch_b = None
-        for f in range(0, FF, FF_CHUNK):
-            rows = slice(f, f + FF_CHUNK)
-            pre = mm(wf_t_ref[rows, :], normed_ref[:, lanes])
-            act, slope = gelu_both(pre)
-            slope_ref[rows, :] = slope
-            act_ref[rows, lanes] = act.astype(BF)
-            part = mm(wg_t_ref[:, rows], act_ref[rows, lanes])
-            branch_b = part if branch_b is None else branch_b + part
-        gate_b = column(mods_ref, 5, image)
-        hidden2 = mid + gate_b * branch_b
-        normed_f, inv_f = norm_parts(hidden2)
-        scale_f = 1.0 + column(modf_ref, 1, image)
-        normf_ref[:, lanes] = (normed_f * scale_f + column(modf_ref, 0, image)).astype(BF)
+        clear(gm_ref, gmf_ref, loss_ref, awo_ref, awf_ref, awg_ref, awy_ref)
+
+    image = lambda b: step * B + b
+    for b in range(B):
+        normed, _ = norm_parts(hid_ref[b])
+        modulate_into(normed_ref, b, normed, 1.0 + column(mods_ref, 1, image(b)), column(mods_ref, 0, image(b)))
+    project_qkv(wqkv_t_ref, normed_ref, qkv_ref, B)
+    attention_forward(qkv_ref, B, lse_ref, att_ref)
+    branch_a = mm(wo_t_ref[...], att_ref[...])
+    for b in range(B):
+        own = branch_a[:, lanes_of(b)]
+        bra_ref[b] = own
+        mid = hid_ref[b] + column(mods_ref, 2, image(b)) * own
+        gmid_ref[b] = mid
+        normed, _ = norm_parts(mid)
+        modulate_into(normed_ref, b, normed, 1.0 + column(mods_ref, 4, image(b)), column(mods_ref, 3, image(b)))
+    branch_b = None
+    for rows in ffn_chunks():
+        act, slope = gelu_both(mm(wf_t_ref[rows, :], normed_ref[...]))
+        slope_ref[rows, :] = slope
+        act_ref[rows, :] = act.astype(BF)
+        branch_b = add_up(branch_b, mm(wg_t_ref[:, rows], act_ref[rows, :]))
+    for b in range(B):
+        lanes = lanes_of(b)
+        own = branch_b[:, lanes]
+        gate_b = column(mods_ref, 5, image(b))
+        normed_f, inv_f = norm_parts(gmid_ref[b] + gate_b * own)
+        scale_f = 1.0 + column(modf_ref, 1, image(b))
+        modulate_into(normf_ref, b, normed_f, scale_f, column(modf_ref, 0, image(b)))
         residue = mm(wy_t_ref[...], normf_ref[:, lanes]) - noise_ref[b].astype(F32)
         loss_ref[...] += residue * residue
         gout_ref[:, lanes] = ((2.0 / entries) * residue).astype(BF)
         gnf = mm(wy_ref[...], gout_ref[:, lanes])
-        put_column(gmf_ref, 0, image, gnf)
-        put_column(gmf_ref, 1, image, gnf * normed_f)
+        put_column(gmf_ref, 0, image(b), gnf)
+        put_column(gmf_ref, 1, image(b), gnf * normed_f)
         ghid = norm_back(gnf, normed_f, inv_f, scale_f)
-        put_column(gm_ref, 3, image, ghid * branch_b)
+        ghid_ref[b] = ghid
+        put_column(gm_ref, 3, image(b), ghid * own)
         gbb_ref[:, lanes] = (gate_b * ghid).astype(BF)
-        gnb = None
-        for f in range(0, FF, FF_CHUNK):
-            rows = slice(f, f + FF_CHUNK)
-            gact = mm(wg_ref[rows, :], gbb_ref[:, lanes])
-            gpre_ref[rows, lanes] = (gact * slope_ref[rows, :]).astype(BF)
-            part = mm(wf_ref[:, rows], gpre_ref[rows, lanes])
-            gnb = part if gnb is None else gnb + part
-        put_column(gm_ref, 1, image, gnb)
-        put_column(gm_ref, 2, image, gnb * normed_b)
-        gmid = ghid + norm_back(gnb, normed_b, inv_b, scale_b)
+    gnb = None
+    for rows in ffn_chunks():
+        gact = mm(wg_ref[rows, :], gbb_ref[...])
+        gpre_ref[rows, :] = (gact * slope_ref[rows, :]).astype(BF)
+        gnb = add_up(gnb, mm(wf_ref[:, rows], gpre_ref[rows, :]))
+        awf_ref[:, rows] += mm_nt(normed_ref[...], gpre_ref[rows, :])
+        awg_ref[rows, :] += mm_nt(act_ref[rows, :], gbb_ref[...])
+    for b in range(B):
+        own = gnb[:, lanes_of(b)]
+        normed, inv = norm_parts(gmid_ref[b])
+        put_column(gm_ref, 1, image(b), own)
+        put_column(gm_ref, 2, image(b), own * normed)
+        gmid = ghid_ref[b] + norm_back(own, normed, inv, 1.0 + column(mods_ref, 4, image(b)))
         gmid_ref[b] = gmid
-        out_bwd(b, image, lanes, gmid, branch_a, gate_a, wo_ref, gba_ref, go_ref, gm_ref, 0)
-    accumulate(awo_ref, mm_nt(att_ref[...], gba_ref[...]), first)
-    accumulate(awf_ref, mm_nt(normed_ref[...], gpre_ref[...]), first)
-    accumulate(awg_ref, mm_nt(act_ref[...], gbb_ref[...]), first)
-    accumulate(awy_ref, mm_nt(gout_ref[...], normf_ref[...]), first)
+        put_column(gm_ref, 0, image(b), gmid * bra_ref[b])
+        gba_ref[:, lanes_of(b)] = (column(mods_ref, 2, image(b)) * gmid).astype(BF)
+    go = mm(wo_ref[...], gba_ref[...]).astype(BF)
+    for b in range(B):
+        go_ref[b] = go[:, lanes_of(b)]
+    awo_ref[...] += mm_nt(att_ref[...], gba_ref[...])
+    awy_ref[...] += mm_nt(gout_ref[...], normf_ref[...])
 
     @pl.when(step == pl.num_programs(0) - 1)
     def _():
@@ -315,36 +328,39 @@
 
     @pl.when(first)
     def _():
-        gm_ref[...] = jnp.zeros_like(gm_ref)
-
-    for b in range(B):
-        image = step * B + b
-        lanes = slice(TOK * b, TOK * (b + 1))
+        clear(gm_ref, awo_ref, awf_ref, awg_ref)
+
+    image = lambda b: step * B + b
+    for b in range(B):
+        lanes = lanes_of(b)
         ghid = ghid_ref[b]
-        put_column(gm_ref, 3, image, ghid * brb_ref[b])
-        gbb_ref[:, lanes] = (column(mods_b_ref, 2, image) * ghid).astype(BF)
-        normed_b, inv_b = norm_parts(mid_ref[b])
-        scale_b = 1.0 + column(mods_b_ref, 1, image)
-        normed_ref[:, lanes] = (normed_b * scale_b + column(mods_b_ref, 0, image)).astype(BF)
+        put_column(gm_ref, 3, image(b), ghid * brb_ref[b])
+        gbb_ref[:, lanes] = (column(mods_b_ref, 2, image(b)) * ghid).astype(BF)
+        normed, _ = norm_parts(mid_ref[b])
+        modulate_into(normed_ref, b, normed, 1.0 + column(mods_b_ref, 1, image(b)), column(mods_b_ref, 0, image(b)))
         atts_ref[:, lanes] = att_ref[b]
-        gnb = None
-        for f in range(0, FF, FF_CHUNK):
-            rows = slice(f, f + FF_CHUNK)
-            act, slope = gelu_both(mm(wf_t_ref[rows, :], normed_ref[:, lanes]))
-            act_ref[rows, lanes] = act.astype(BF)
-            gact = mm(wg_ref[rows, :], gbb_ref[:, lanes])
-            gpre_ref[rows, lanes] = (gact * slope).astype(BF)
-            part = mm(wf_ref[:, rows], gpre_ref[rows, lanes])
-            gnb = part if gnb is None else gnb + part
-        put_column(gm_ref, 1, image, gnb)
-        put_column(gm_ref, 2, image, gnb * normed_b)
-        gmid = ghid + norm_back(gnb, normed_b, inv_b, scale_b)
+    gnb = None
+    for rows in ffn_chunks():
+        act, slope = gelu_both(mm(wf_t_ref[rows, :], normed_ref[...]))
+        act_ref[rows, :] = act.astype(BF)
+        gact = mm(wg_ref[rows, :], gbb_ref[...])
+        gpre_ref[rows, :] = (gact * slope).astype(BF)
+        gnb = add_up(gnb, mm(wf_ref[:, rows], gpre_ref[rows, :]))
+        awf_ref[:, rows] += mm_nt(normed_ref[...], gpre_ref[rows, :])
+        awg_ref[rows, :] += mm_nt(act_ref[rows, :], gbb_ref[...])
+    for b in range(B):
+        own = gnb[:, lanes_of(b)]
+        normed, inv = norm_parts(mid_ref[b])
+        put_column(gm_ref, 1, image(b), own)
+        put_column(gm_ref, 2, image(b), own * normed)
+        gmid = ghid_ref[b] + norm_back(own, normed, inv, 1.0 + column(mods_b_ref, 1, image(b)))
         gmid_ref[b] = gmid
-        out_bwd(b, image, lanes, gmid, bra_ref[b], column(mods_a_ref, 2, image), wo_ref, gba_ref, go_ref,
-                gm_ref, 0)
-    accumulate(awo_ref, mm_nt(atts_ref[...], gba_ref[...]), first)
-    accumulate(awf_ref, mm_nt(normed_ref[...], gpre_ref[...]), first)
-    accumulate(awg_ref, mm_nt(act_ref[...], gbb_ref[...]), first)
+        put_column(gm_ref, 0, image(b), gmid * bra_ref[b])
+        gba_ref[:, lanes_of(b)] = (column(mods_a_ref, 2, image(b)) * gmid).astype(BF)
+    go = mm(wo_ref[...], gba_ref[...]).astype(BF)
+    for b in range(B):
+        go_ref[b] = go[:, lanes_of(b)]
+    awo_ref[...] += mm_nt(atts_ref[...], gba_ref[...])
 
     @pl.when(step == pl.num_programs(0) - 1)
     def _():
@@ -390,21 +406,22 @@
             for to_ref, from_ref in zip([gm_ref] + accs, before):
                 to_ref[...] = from_ref[...]
 
-    for b in range(B):
-        image = (offset + step) * B + b
-        lanes = slice(TOK * b, TOK * (b + 1))
-        hidden = mm(wp_t_ref[...], noisy_ref[b]) + pos_ref[...] if bottom else hid_ref[b]
-        normed, inv = norm_parts(hidden)
-        scale = 1.0 + column(mods_ref, 1, image)
-        normed_ref[:, lanes] = (normed * scale + column(mods_ref, 0, image)).astype(BF)
-        attention_backward(qkv_ref, b, lse_ref, go_ref, gqkv_ref, lanes)
-        gna = mm(wqkv_ref[...], gqkv_ref[:, lanes])
-        put_column(gm_ref, 0, image, gna)
-        put_column(gm_ref, 1, image, gna * normed)
-        ghid = gmid_ref[b] + norm_back(gna, normed, inv, scale)
+    image = lambda b: (offset + step) * B + b
+    source = lambda b: mm(wp_t_ref[...], noisy_ref[b]) + pos_ref[...] if bottom else hid_ref[b]
+    for b in range(B):
+        normed, _ = norm_parts(source(b))
+        modulate_into(normed_ref, b, normed, 1.0 + column(mods_ref, 1, image(b)), column(mods_ref, 0, image(b)))
+    attention_backward(qkv_ref, B, lse_ref, go_ref, gqkv_ref)
+    gna = mm(wqkv_ref[...], gqkv_ref[...])
+    for b in range(B):
+        own = gna[:, lanes_of(b)]
+        normed, inv = norm_parts(source(b))
+        put_column(gm_ref, 0, image(b), own)
+        put_column(gm_ref, 1, image(b), own * normed)
+        ghid = gmid_ref[b] + norm_back(own, normed, inv, 1.0 + column(mods_ref, 1, image(b)))
         if bottom:
-            tok_ref[:, lanes] = ghid.astype(BF)
-            noi_ref[:, lanes] = noisy_ref[b]
+            tok_ref[:, lanes_of(b)] = ghid.astype(BF)
+            noi_ref[:, lanes_of(b)] = noisy_ref[b]
         else:
             ghid_ref[b] = ghid
     accs[0][...] += mm_nt(normed_ref[...], gqkv_ref[...])
@@ -507,9 +524,9 @@
          (full, (n, D, TOK), BF), (full, (n, D, TOK), F32),
          (whole(4 * D, 128), (4 * D, 128), F32), (whole(2 * D, 128), (2 * D, 128), F32),
          (whole(PATCH_IN, TOK), (PATCH_IN, TOK), F32)] + halves(pack),
-        [(pack, BF), ((D, T), BF), ((D, T), BF), ((FF, TOK), F32), ((FF, T), BF), ((FF, T), BF), ((D, T), BF),
+        [(pack, BF), ((D, T), BF), ((D, T), BF), ((FF, T), F32), ((FF, T), BF), ((FF, T), BF), ((D, T), BF),
          ((D, T), BF), ((D, T), BF), ((PATCH_IN, T), BF), ((D, D), F32), ((D, FF), F32), ((FF, D), F32),
-         ((PATCH_IN, D), F32)],
+         ((PATCH_IN, D), F32), ((B, D, TOK), F32), ((B, D, TOK), F32)],
         2 * n * TOK * (4 * D * D + 2 * D * TOK + 6 * D * FF + 2 * D * D),
         (table, hid, noise, mods, modf, wqkv_t, wo_t, wf_t, wg_t, wo, wf, wg, wy_t, wy, cond))
 

time: 420 us -> 367 us (0.87)
  Pallas kernels: 287 us -> 231 us
    pallas_call x8, Pallas kernels: 208 us -> 152 us  [run_kernel(): pl.pallas_call(kernel, grid=(steps,), in_specs=in_specs, out_specs=out_sp...]
  transfers between devices with their start and end apart: 63 -> 63, of which waited for: 17 -> 16; matrix products, arithmetic and copies ran while one was open for 2% -> 2% of each run, Pallas kernels for 46% -> 44%
where the time goes in v3:
time: 367 us; the launch traced here: 362 us
  Pallas kernels  231 us (63%)
  starting transfers between devices  60.3 us (16%)
  waiting for transfers between devices  45.6 us (12%)
  local copies, waits for them, and re-layouts  15.2 us (4%)
  other arithmetic  7.41 us (2%)
    pallas_call x8, Pallas kernels, run_kernel(): pl.pallas_call(kernel, grid=(steps,), in_specs=in_specs, out_specs=out_sp...  152 us
    ppermute x63, starting transfers between devices, swap(): return lax.ppermute(x, axis, pairs)  60.3 us
    ppermute x63, waiting for transfers between devices, swap(): return lax.ppermute(x, axis, pairs)  45.6 us
    pallas_call x9, Pallas kernels, small_kernel(): pl.pallas_call(kernel, in_specs=[SCALARS] * scalars + [in_vmem()] * (len(...  38.8 us
    pallas_call x2, Pallas kernels, update(): pl.pallas_call(functools.partial(update_kernel, masks, offsets['place'],...  17.5 us
    pallas_call x4, Pallas kernels, reduce_outer(): pl.pallas_call(functools.partial(rows_kernel, len(parts), offsets[shift])...  16.2 us
    unnamed x135, local copies, waits for them, and re-layouts  10.9 us
  transfers between devices with their start and end apart: 63, of which 16 were waited for; matrix products, arithmetic and copies ran while one was open for 2% of the time, Pallas kernels for 44%

profile of v3, /device:TPU:0, one launch (start us, length us, event | category | flops | bytes accessed | tf_op | source)
XLA Modules:
  0.0 361.7 jit_solution(5074561702146254256)
XLA Ops:
  1.4 2.7 shard_map.255
  4.0 3.0 collective-permute-start
  7.1 2.6 collective-permute-start.1
  10.5 4.0 %shard_map.256 = (bf16[1152,384]{1,0:T(8,128)(2,1)}, bf16[2048,384]{1,0:T(8,128)(2,1)}, bf16[400,384]{1,0:T(8,128)(2,1)}) custom-call(s32[19]{0:T(128)} %stack.88.table_ref.refs_0_, f32[2,480,384]{2,1,0:T(8,128)} %refs_8_.3, f32[2,96,4992]{2,1,0:T(8,128)} %refs_11_.3, f32[2,96,4992]{2,1,0:T(8,128)} %refs_11_.3, f32[2,96,4992]{2,1,0:T(8,128)} %refs_11_.3, ...), custom_call_target="tpu_custom_call" | custom-call | tf_op jit(solution)/shard_map/pallas_call | solution.py:856
  14.5 3.2 collective-permute-done.1
  22.1 5.6 %collective-permute-done.3 = bf16[384,384]{1,0:T(8,128)(2,1)S(1)} collective-permute-done((bf16[384,384]{1,0:T(8,128)(2,1)S(1)}, bf16[384,384]{1,0:T(8,128)(2,1)S(1)}, u32[]{:S(2)}, u32[]{:S(2)}) %collective-permute-start.3) | collective-permute-done | bytes 294944 | tf_op jit(solution)/shard_map/ppermute | solution.py:629
  27.8 5.2 %collective-permute-done.4 = bf16[384,384]{1,0:T(8,128)(2,1)S(1)} collective-permute-done((bf16[384,384]{1,0:T(8,128)(2,1)S(1)}, bf16[384,384]{1,0:T(8,128)(2,1)S(1)}, u32[]{:S(2)}, u32[]{:S(2)}) %collective-permute-start.4) | collective-permute-done | bytes 294944 | tf_op jit(solution)/shard_map/ppermute | solution.py:629
  40.9 8.6 %collective-permute-done.8 = bf16[144,384]{1,0:T(8,128)(2,1)S(1)} collective-permute-done((bf16[144,384]{1,0:T(8,128)(2,1)S(1)}, bf16[144,384]{1,0:T(8,128)(2,1)S(1)}, u32[]{:S(2)}, u32[]{:S(2)}) %collective-permute-start.8) | collective-permute-done | bytes 110624 | tf_op jit(solution)/shard_map/ppermute | solution.py:629
  56.5 5.0 %shard_map.257 = (bf16[384,16]{1,0:T(8,128)(2,1)}, bf16[384,384]{1,0:T(8,128)(2,1)}, bf16[384,1152]{1,0:T(8,128)(2,1)}, bf16[384,1152]{1,0:T(8,128)(2,1)}, bf16[...) custom-call(s32[19]{0:T(128)} %stack.88.table_ref.refs_0_, ...), custom_call_target="tpu_custom_call" | custom-call | flops 8000000000 | tf_op jit(solution)/shard_map/pallas_call | solution.py:672
  61.6 7.1 %shard_map.258 = (bf16[8,1152,256]{2,1,0:T(8,128)(2,1)}, f32[8,8,256]{2,1,0:T(8,128)}, bf16[8,384,256]{2,1,0:T(8,128)(2,1)}) custom-call(bf16[8,16,256]{2,1,0:T(8,128)(2,1)} %add_convert_fusion.noisy_ref.refs_1_, bf16[384,16]{1,0:T(8,128)(2,1)} %get-tuple-element.167.wp_t_ref.refs_2_, f32[384,256]{1,0:T(8,128)} %pad_maximum_fusion.pos_ref.refs_3_, ...), custom_call_target="tpu_custom_call" | custom-call | flops 10468982784 | bytes 8302592 | tf_op jit(solution)/shard_map/pallas_call | solution.py:460
  70.3 7.2 %shard_map.259 = (bf16[8,1152,256]{2,1,0:T(8,128)(2,1)}, f32[8,8,256]{2,1,0:T(8,128)}, bf16[8,384,256]{2,1,0:T(8,128)(2,1)}) custom-call(bf16[8,16,256]{2,1,0:T(8,128)(2,1)} %add_convert_fusion.noisy_ref.refs_1_, bf16[384,16]{1,0:T(8,128)(2,1)} %get-tuple-element.167.wp_t_ref.refs_2_, ...), custom_call_target="tpu_custom_call", output_to_operand_aliasing={{0}: (5, {}), {1}: (6, {}), {2}: (7, {})} | custom-call | flops 10468982784 | bytes 14659584 | tf_op jit(solution)/shard_map/pallas_call | solution.py:460
  83.0 5.4 %shard_map.260 = (bf16[384,384]{1,0:T(8,128)(2,1)}, bf16[1536,384]{1,0:T(8,128)(2,1)}, bf16[384,384]{1,0:T(8,128)(2,1)}, bf16[384,1536]{1,0:T(8,128)(2,1)}, bf16...) custom-call(s32[19]{0:T(128)} %stack.88.table_ref.refs_0_, ...), custom_call_target="tpu_custom_call" | custom-call | flops 8000000000 | tf_op jit(solution)/shard_map/pallas_call | solution.py:672
  88.4 13.8 %shard_map.261 = (f32[8,384,256]{2,1,0:T(8,128)}, f32[8,384,256]{2,1,0:T(8,128)}, f32[8,384,256]{2,1,0:T(8,128)}, f32[8,384,256]{2,1,0:T(8,128)}) custom-call(bf16[8,16,256]{2,1,0:T(8,128)(2,1)} %add_convert_fusion.noisy_ref.refs_1_, bf16[384,16]{1,0:T(8,128)(2,1)} %get-tuple-element.167.wp_t_ref.refs_2_, f32[384,256]{1,0:T(8,128)} %pad_maximum_fusion.pos_ref.refs_3_, ...), custom_call_target="tpu_custom_call" | custom-call | flops 43486543872 | bytes 18460672 | tf_op jit(solution)/shard_map/pallas_call | solution.py:460
  102.9 4.5 %collective-permute-done.21.refs_2_ = bf16[768,384]{1,0:T(8,128)(2,1)S(1)} collective-permute-done((bf16[768,384]{1,0:T(8,128)(2,1)S(1)}, bf16[768,384]{1,0:T(8,128)(2,1)S(1)}, u32[]{:S(2)}, u32[]{:S(2)}) %collective-permute-start.21) | collective-permute-done | bytes 589856 | tf_op jit(solution)/shard_map/ppermute | solution.py:629
  110.4 7.9 %shard_map.262 = (bf16[384,384]{1,0:T(8,128)(2,1)}, bf16[1536,384]{1,0:T(8,128)(2,1)}, bf16[384,384]{1,0:T(8,128)(2,1)}, bf16[384,1536]{1,0:T(8,128)(2,1)}, bf16...) custom-call(s32[19]{0:T(128)} %stack.88.table_ref.refs_0_, ...), custom_call_target="tpu_custom_call" | custom-call | flops 8000000000 | tf_op jit(solution)/shard_map/pallas_call | solution.py:672
  118.3 44.7 %shard_map.263 = (bf16[8,1152,256]{2,1,0:T(8,128)(2,1)}, f32[8,8,256]{2,1,0:T(8,128)}, bf16[8,384,256]{2,1,0:T(8,128)(2,1)}, f32[8,384,256]{2,1,0:T(8,128)}, f32...) custom-call(s32[19]{0:T(128)} %stack.88.table_ref.refs_0_, ...), custom_call_target="tpu_custom_call" | custom-call | flops 151397597184 | bytes 25731148 | tf_op jit(solution)/shard_map/pallas_call | solution.py:460
  163.2 22.3 %shard_map.264 = (f32[8,384,256]{2,1,0:T(8,128)}, f32[768,128]{1,0:T(8,128)}, bf16[4,384,384]{2,1,0:T(8,128)(2,1)}, bf16[4,384,384]{2,1,0:T(8,128)(2,1)}) custom-call(s32[19]{0:T(128)} %stack.88.table_ref.refs_0_, f32[8,384,256]{2,1,0:T(8,128)} %get-tuple-element.191.hid_ref.refs_1_, bf16[8,1152,256]{2,1,0:T(8,128)(2,1)} %get-tuple-element.208.refs_2_, ...), custom_call_target="tpu_custom_call" | custom-call | flops 45097156608 | bytes 21102668 | tf_op jit(solution)/shard_map/pallas_call | solution.py:460
  187.4 4.4 %shard_map.265 = (bf16[4,160,384]{2,1,0:T(8,128)(2,1)}, bf16[4,160,384]{2,1,0:T(8,128)(2,1)}, bf16[4,160,384]{2,1,0:T(8,128)(2,1)}, bf16[4,160,384]{2,1,0:T(8,128)(2,1)}) custom-call(s32[19]{0:T(128)} %stack.88.table_ref.refs_0_, bf16[4,640,384]{2,1,0:T(8,128)(2,1)} %get-tuple-element.215.refs_0_, bf16[4,640,384]{2,1,0:T(8,128)(2,1)} %copy-done.2), custom_call_target="tpu_custom_call" | custom-call | tf_op jit(solution)/shard_map/pallas_call | solution.py:757
  195.3 30.3 %shard_map.266 = (bf16[8,384,256]{2,1,0:T(8,128)(2,1)}, f32[8,384,256]{2,1,0:T(8,128)}, f32[1536,128]{1,0:T(8,128)}, bf16[4,640,384]{2,1,0:T(8,128)(2,1)}, bf16[4,640,384]{2,1,0:T(8,128)(2,1)}) custom-call(s32[19]{0:T(128)} %stack.88.table_ref.refs_0_, f32[8,384,256]{2,1,0:T(8,128)} %get-tuple-element.221.ghid_ref, ...), custom_call_target="tpu_custom_call" | custom-call | flops 106300440576 | bytes 28704844 | tf_op jit(solution)/shard_map/pallas_call | solution.py:460
  227.9 3.8 %shard_map.267 = (bf16[4,96,384]{2,1,0:T(8,128)(2,1)}, bf16[4,96,384]{2,1,0:T(8,128)(2,1)}, bf16[4,96,384]{2,1,0:T(8,128)(2,1)}, bf16[4,96,384]{2,1,0:T(8,128)(2,1)}) custom-call(s32[19]{0:T(128)} %stack.88.table_ref.refs_0_, bf16[4,384,384]{2,1,0:T(8,128)(2,1)} %get-tuple-element.234.refs_0_, bf16[4,384,384]{2,1,0:T(8,128)(2,1)} %copy-done.4), custom_call_target="tpu_custom_call" | custom-call | tf_op jit(solution)/shard_map/pallas_call | solution.py:757
  235.2 12.8 %shard_map.268 = (f32[768,128]{1,0:T(8,128)}, f32[384,1152]{1,0:T(8,128)}, f32[16,384]{1,0:T(8,128)}) custom-call(s32[19]{0:T(128)} %stack.88.table_ref.refs_0_, bf16[8,16,256]{2,1,0:T(8,128)(2,1)} %add_convert_fusion.noisy_ref.refs_1_, bf16[384,16]{1,0:T(8,128)(2,1)} %get-tuple-element.167.wp_t_ref.refs_2_, f32[384,256]{1,0:T(8,128)} %pad_maximum_fusion.pos_ref.refs_3_, ...), custom_call_target="tpu_custom_call" | custom-call | flops 22548578304 | bytes 13733964 | tf_op jit(solution)/shard_map/pallas_call | solution.py:460
  249.3 3.4 shard_map.269
  258.5 4.4 %shard_map.270 = (bf16[4,160,384]{2,1,0:T(8,128)(2,1)}, bf16[4,160,384]{2,1,0:T(8,128)(2,1)}, bf16[4,160,384]{2,1,0:T(8,128)(2,1)}, bf16[4,160,384]{2,1,0:T(8,128)(2,1)}) custom-call(s32[19]{0:T(128)} %stack.88.table_ref.refs_0_, bf16[4,640,384]{2,1,0:T(8,128)(2,1)} %get-tuple-element.253.refs_0_, bf16[4,640,384]{2,1,0:T(8,128)(2,1)} %copy-done.1), custom_call_target="tpu_custom_call" | custom-call | tf_op jit(solution)/shard_map/pallas_call | solution.py:757
  265.1 13.9 %shard_map.271 = (f32[768,128]{1,0:T(8,128)}, bf16[4,256,384]{2,1,0:T(8,128)(2,1)}, bf16[4,256,384]{2,1,0:T(8,128)(2,1)}) custom-call(s32[19]{0:T(128)} %stack.88.table_ref.refs_0_, bf16[8,16,256]{2,1,0:T(8,128)(2,1)} %add_convert_fusion.noisy_ref.refs_1_, bf16[384,16]{1,0:T(8,128)(2,1)} %get-tuple-element.167.wp_t_ref.refs_2_, ...), custom_call_target="tpu_custom_call" | custom-call | flops 22548578304 | bytes 15700044 | tf_op jit(solution)/shard_map/pallas_call | solution.py:460
  283.2 5.4 %shard_map.273.refs_8_ = bf16[32,384]{1,0:T(8,128)(2,1)} custom-call(s32[19]{0:T(128)} %stack.88.table_ref.refs_0_, f32[768,128]{1,0:T(8,128)} %get-tuple-element.274.gma0_ref, f32[1536,128]{1,0:T(8,128)} %get-tuple-element.275.gmb0_ref, f32[768,128]{1,0:T(8,128)} %get-tuple-element.276.gma1_ref, f32[1536,128]{1,0:T(8,128)} %get-tuple-element.277.gmb1_ref, ...), custom_call_target="tpu_custom_call" | custom-call | flops 8000000000 | tf_op jit(solution)/shard_map/pallas_call | solution.py:672
  291.8 3.6 shard_map.274
  305.2 3.8 %collective-permute-done.44.refs_6_ = bf16[4,64,384]{2,1,0:T(8,128)(2,1)S(1)} collective-permute-done((bf16[4,64,384]{2,1,0:T(8,128)(2,1)}, bf16[4,64,384]{2,1,0:T(8,128)(2,1)S(1)}, u32[]{:S(2)}, u32[]{:S(2)}) %collective-permute-start.44) | collective-permute-done | bytes 196640 | tf_op jit(solution)/shard_map/ppermute | solution.py:629
  309.7 3.2 shard_map.275
  320.4 3.9 %collective-permute-done.47.refs_2_ = bf16[256,384]{1,0:T(8,128)(2,1)S(1)} collective-permute-done((bf16[256,384]{1,0:T(8,128)(2,1)}, bf16[256,384]{1,0:T(8,128)(2,1)S(1)}, u32[]{:S(2)}, u32[]{:S(2)}) %collective-permute-start.47) | collective-permute-done | bytes 196640 | tf_op jit(solution)/shard_map/ppermute | solution.py:629
  330.6 8.8 %shard_map.278 = (f32[2,480,384]{2,1,0:T(8,128)}, f32[2,480,384]{2,1,0:T(8,128)}, f32[2,480,384]{2,1,0:T(8,128)}, f32[2,96,4992]{2,1,0:T(8,128)}, f32[2,96,4992]...) custom-call(s32[19]{0:T(128)} %stack.88.table_ref.refs_0_, ...), custom_call_target="tpu_custom_call" | custom-call | tf_op jit(solution)/shard_map/pallas_call | solution.py:1084
  345.1 8.7 %shard_map.279 = (f32[2,480,384]{2,1,0:T(8,128)}, f32[2,480,384]{2,1,0:T(8,128)}, f32[2,480,384]{2,1,0:T(8,128)}, f32[2,96,4992]{2,1,0:T(8,128)}, f32[2,96,4992]...) custom-call(s32[19]{0:T(128)} %stack.88.table_ref.refs_0_, ...), custom_call_target="tpu_custom_call", output_to_operand_aliasing={{0}: (15, {}), {1}: (16, {}), {2}: (17, {}), {3}: (18, {}),... | custom-call | tf_op jit(solution)/shard_map/pallas_call | solution.py:1084
  354.6 4.3 %shard_map.277 = (f32[1664,384]{1,0:T(8,128)}, f32[1,1]{1,0:T(1,128)}) custom-call(s32[19]{0:T(128)} %stack.88.table_ref.refs_0_, bf16[352,384]{1,0:T(8,128)(2,1)} %shard_map.276.refs_0_, bf16[352,384]{1,0:T(8,128)(2,1)} %copy-done.12, bf16[352,384]{1,0:T(8,128)(2,1)} %copy-done.13, bf16[352,384]{1,0:T(8,128)(2,1)} %copy-done.14, ...), custom_call_target="tpu_custom_call" | custom-call | flops 8000000000 | tf_op jit(solution)/shard_map/pallas_call | solution.py:672
  (287 shorter events, 92.3 us)
Async XLA Ops:
  20.1 12.9 %collective-permute-start.4 = (bf16[384,384]{1,0:T(8,128)(2,1)S(1)}, bf16[384,384]{1,0:T(8,128)(2,1)S(1)}, u32[]{:S(2)}, u32[]{:S(2)}) collective-permute-start(bf16[384,384]{1,0:T(8,128)(2,1)S(1)} %pad_maximum_fusion.2), channel_id=1, source_target_pairs={{0,16},{4,20},{8,24},{12,28},{16,0},{20,4},{24,8},{28,12},{1,17},{... | collective-permute-start | bytes 884744 | tf_op jit(solution)/shard_map/ppermute | solution.py:629
  33.1 22.4 %collective-permute-start.6 = (bf16[1536,384]{1,0:T(8,128)(2,1)S(1)}, bf16[1536,384]{1,0:T(8,128)(2,1)S(1)}, u32[]{:S(2)}, u32[]{:S(2)}) collective-permute-start(bf16[1536,384]{1,0:T(8,128)(2,1)S(1)} %constant_dynamic-update-slice_fusion.refs_0_), channel_id=1, source_target_pairs={{0,4},{4,0},{8,12},{12,8},{16,20},{20,16},{24,28},{28,24},{1,5},{5... | collective-permute-start | bytes 3538952 | tf_op jit(solution)/shard_map/ppermute | solution.py:629
  49.6 19.2 %collective-permute-start.12 = (bf16[256,384]{1,0:T(8,128)(2,1)S(1)}, bf16[256,384]{1,0:T(8,128)(2,1)S(1)}, u32[]{:S(2)}, u32[]{:S(2)}) collective-permute-start(bf16[256,384]{1,0:T(8,128)(2,1)S(1)} %slice.15), channel_id=1, source_target_pairs={{0,3},{1,2},{2,1},{3,0},{4,7},{5,6},{6,5},{7,4},{8,11},{9,10},{10,... | collective-permute-start | bytes 589832 | tf_op jit(solution)/shard_map/ppermute | solution.py:629
  51.6 18.6 %collective-permute-start.11 = (bf16[256,384]{1,0:T(8,128)(2,1)S(1)}, bf16[256,384]{1,0:T(8,128)(2,1)S(1)}, u32[]{:S(2)}, u32[]{:S(2)}) collective-permute-start(bf16[256,384]{1,0:T(8,128)(2,1)S(1)} %slice.15), channel_id=1, source_target_pairs={{0,2},{1,3},{2,0},{3,1},{4,6},{5,7},{6,4},{7,5},{8,10},{9,11},{10,... | collective-permute-start | bytes 589832 | tf_op jit(solution)/shard_map/ppermute | solution.py:629
  53.1 17.1 %collective-permute-start.10 = (bf16[256,384]{1,0:T(8,128)(2,1)S(1)}, bf16[256,384]{1,0:T(8,128)(2,1)S(1)}, u32[]{:S(2)}, u32[]{:S(2)}) collective-permute-start(bf16[256,384]{1,0:T(8,128)(2,1)S(1)} %slice.15), channel_id=1, source_target_pairs={{0,1},{1,0},{2,3},{3,2},{4,5},{5,4},{6,7},{7,6},{8,9},{9,8},{10,11... | collective-permute-start | bytes 589832 | tf_op jit(solution)/shard_map/ppermute | solution.py:629
  54.0 23.5 %collective-permute-start.15 = (bf16[432,384]{1,0:T(8,128)(2,1)S(1)}, bf16[432,384]{1,0:T(8,128)(2,1)S(1)}, u32[]{:S(2)}, u32[]{:S(2)}) collective-permute-start(bf16[432,384]{1,0:T(8,128)(2,1)S(1)} %constant_dynamic-update-slice_fusion.4.refs_0_), channel_id=1, source_target_pairs={{0,24},{4,28},{8,16},{12,20},{16,8},{20,12},{24,0},{28,4},{1,25},{... | collective-permute-start | bytes 995336 | tf_op jit(solution)/shard_map/ppermute | solution.py:629
  55.5 22.1 %collective-permute-start.14 = (bf16[432,384]{1,0:T(8,128)(2,1)S(1)}, bf16[432,384]{1,0:T(8,128)(2,1)S(1)}, u32[]{:S(2)}, u32[]{:S(2)}) collective-permute-start(bf16[432,384]{1,0:T(8,128)(2,1)S(1)} %constant_dynamic-update-slice_fusion.4.refs_0_), channel_id=1, source_target_pairs={{0,16},{4,20},{8,24},{12,28},{16,0},{20,4},{24,8},{28,12},{1,17},{... | collective-permute-start | bytes 995336 | tf_op jit(solution)/shard_map/ppermute | solution.py:629
  78.7 23.7 %collective-permute-start.22 = (bf16[768,384]{1,0:T(8,128)(2,1)S(1)}, bf16[768,384]{1,0:T(8,128)(2,1)S(1)}, u32[]{:S(2)}, u32[]{:S(2)}) collective-permute-start(bf16[768,384]{1,0:T(8,128)(2,1)S(1)} %constant_dynamic-update-slice_fusion.7.refs_0_), channel_id=1, source_target_pairs={{0,24},{4,28},{8,16},{12,20},{16,8},{20,12},{24,0},{28,4},{1,25},{... | collective-permute-start | bytes 1769480 | tf_op jit(solution)/shard_map/ppermute | solution.py:629
  79.7 27.7 %collective-permute-start.21 = (bf16[768,384]{1,0:T(8,128)(2,1)S(1)}, bf16[768,384]{1,0:T(8,128)(2,1)S(1)}, u32[]{:S(2)}, u32[]{:S(2)}) collective-permute-start(bf16[768,384]{1,0:T(8,128)(2,1)S(1)} %constant_dynamic-update-slice_fusion.7.refs_0_), channel_id=1, source_target_pairs={{0,16},{4,20},{8,24},{12,28},{16,0},{20,4},{24,8},{28,12},{1,17},{... | collective-permute-start | bytes 1769480 | tf_op jit(solution)/shard_map/ppermute | solution.py:629
  80.7 26.7 %collective-permute-start.20 = (bf16[768,384]{1,0:T(8,128)(2,1)S(1)}, bf16[768,384]{1,0:T(8,128)(2,1)S(1)}, u32[]{:S(2)}, u32[]{:S(2)}) collective-permute-start(bf16[768,384]{1,0:T(8,128)(2,1)S(1)} %constant_dynamic-update-slice_fusion.7.refs_0_), channel_id=1, source_target_pairs={{0,8},{4,12},{8,0},{12,4},{16,24},{20,28},{24,16},{28,20},{1,9},{5... | collective-permute-start | bytes 1769480 | tf_op jit(solution)/shard_map/ppermute | solution.py:629
  163.0 23.0 %collective-permute-start.27 = (bf16[4,640,384]{2,1,0:T(8,128)(2,1)}, bf16[4,640,384]{2,1,0:T(8,128)(2,1)S(1)}, u32[]{:S(2)}, u32[]{:S(2)}) collective-permute-start(bf16[4,640,384]{2,1,0:T(8,128)(2,1)} %get-tuple-element.216), channel_id=1, source_target_pairs={{0,4},{4,0},{8,12},{12,8},{16,20},{20,16},{24,28},{28,24},{1,5},{5... | collective-permute-start | bytes 5898248 | tf_op jit(solution)/shard_map/ppermute | solution.py:629
  185.6 40.2 %collective-permute-start.31 = (bf16[4,384,384]{2,1,0:T(8,128)(2,1)}, bf16[4,384,384]{2,1,0:T(8,128)(2,1)S(1)}, u32[]{:S(2)}, u32[]{:S(2)}) collective-permute-start(bf16[4,384,384]{2,1,0:T(8,128)(2,1)} %get-tuple-element.235), channel_id=1, source_target_pairs={{0,4},{4,0},{8,12},{12,8},{16,20},{20,16},{24,28},{28,24},{1,5},{5... | collective-permute-start | bytes 3538952 | tf_op jit(solution)/shard_map/ppermute | solution.py:629
  191.8 33.9 %collective-permute-start.30 = (bf16[4,160,384]{2,1,0:T(8,128)(2,1)}, bf16[4,160,384]{2,1,0:T(8,128)(2,1)S(1)}, u32[]{:S(2)}, u32[]{:S(2)}) collective-permute-start(bf16[4,160,384]{2,1,0:T(8,128)(2,1)} %get-tuple-element.220), channel_id=1, source_target_pairs={{0,24},{4,28},{8,16},{12,20},{16,8},{20,12},{24,0},{28,4},{1,25},{... | collective-permute-start | bytes 1474568 | tf_op jit(solution)/shard_map/ppermute | solution.py:629
  193.0 32.8 %collective-permute-start.29 = (bf16[4,160,384]{2,1,0:T(8,128)(2,1)}, bf16[4,160,384]{2,1,0:T(8,128)(2,1)S(1)}, u32[]{:S(2)}, u32[]{:S(2)}) collective-permute-start(bf16[4,160,384]{2,1,0:T(8,128)(2,1)} %get-tuple-element.219), channel_id=1, source_target_pairs={{0,16},{4,20},{8,24},{12,28},{16,0},{20,4},{24,8},{28,12},{1,17},{... | collective-permute-start | bytes 1474568 | tf_op jit(solution)/shard_map/ppermute | solution.py:629
  194.0 31.8 %collective-permute-start.28 = (bf16[4,160,384]{2,1,0:T(8,128)(2,1)}, bf16[4,160,384]{2,1,0:T(8,128)(2,1)S(1)}, u32[]{:S(2)}, u32[]{:S(2)}) collective-permute-start(bf16[4,160,384]{2,1,0:T(8,128)(2,1)} %get-tuple-element.218), channel_id=1, source_target_pairs={{0,8},{4,12},{8,0},{12,4},{16,24},{20,28},{24,16},{28,20},{1,9},{5... | collective-permute-start | bytes 1474568 | tf_op jit(solution)/shard_map/ppermute | solution.py:629
  225.7 31.5 %collective-permute-start.35 = (bf16[4,640,384]{2,1,0:T(8,128)(2,1)}, bf16[4,640,384]{2,1,0:T(8,128)(2,1)S(1)}, u32[]{:S(2)}, u32[]{:S(2)}) collective-permute-start(bf16[4,640,384]{2,1,0:T(8,128)(2,1)} %get-tuple-element.254), channel_id=1, source_target_pairs={{0,4},{4,0},{8,12},{12,8},{16,20},{20,16},{24,28},{28,24},{1,5},{5... | collective-permute-start | bytes 5898248 | tf_op jit(solution)/shard_map/ppermute | solution.py:629
  231.7 16.3 %collective-permute-start.34 = (bf16[4,96,384]{2,1,0:T(8,128)(2,1)}, bf16[4,96,384]{2,1,0:T(8,128)(2,1)S(1)}, u32[]{:S(2)}, u32[]{:S(2)}) collective-permute-start(bf16[4,96,384]{2,1,0:T(8,128)(2,1)} %get-tuple-element.243), channel_id=1, source_target_pairs={{0,24},{4,28},{8,16},{12,20},{16,8},{20,12},{24,0},{28,4},{1,25},{... | collective-permute-start | bytes 884744 | tf_op jit(solution)/shard_map/ppermute | solution.py:629
  232.9 15.7 %collective-permute-start.33 = (bf16[4,96,384]{2,1,0:T(8,128)(2,1)}, bf16[4,96,384]{2,1,0:T(8,128)(2,1)S(1)}, u32[]{:S(2)}, u32[]{:S(2)}) collective-permute-start(bf16[4,96,384]{2,1,0:T(8,128)(2,1)} %get-tuple-element.242), channel_id=1, source_target_pairs={{0,16},{4,20},{8,24},{12,28},{16,0},{20,4},{24,8},{28,12},{1,17},{... | collective-permute-start | bytes 884744 | tf_op jit(solution)/shard_map/ppermute | solution.py:629
  233.9 14.7 %collective-permute-start.32 = (bf16[4,96,384]{2,1,0:T(8,128)(2,1)}, bf16[4,96,384]{2,1,0:T(8,128)(2,1)S(1)}, u32[]{:S(2)}, u32[]{:S(2)}) collective-permute-start(bf16[4,96,384]{2,1,0:T(8,128)(2,1)} %get-tuple-element.238), channel_id=1, source_target_pairs={{0,8},{4,12},{8,0},{12,4},{16,24},{20,28},{24,16},{28,20},{1,9},{5... | collective-permute-start | bytes 884744 | tf_op jit(solution)/shard_map/ppermute | solution.py:629
  252.8 26.2 %collective-permute-start.42 = (bf16[256,384]{1,0:T(8,128)(2,1)}, bf16[256,384]{1,0:T(8,128)(2,1)S(1)}, u32[]{:S(2)}, u32[]{:S(2)}) collective-permute-start(bf16[256,384]{1,0:T(8,128)(2,1)} %get-tuple-element.252), channel_id=1, source_target_pairs={{0,3},{1,2},{2,1},{3,0},{4,7},{5,6},{6,5},{7,4},{8,11},{9,10},{10,... | collective-permute-start | bytes 589832 | tf_op jit(solution)/shard_map/ppermute | solution.py:629
  254.9 25.5 %collective-permute-start.41 = (bf16[256,384]{1,0:T(8,128)(2,1)}, bf16[256,384]{1,0:T(8,128)(2,1)S(1)}, u32[]{:S(2)}, u32[]{:S(2)}) collective-permute-start(bf16[256,384]{1,0:T(8,128)(2,1)} %get-tuple-element.251), channel_id=1, source_target_pairs={{0,2},{1,3},{2,0},{3,1},{4,6},{5,7},{6,4},{7,5},{8,10},{9,11},{10,... | collective-permute-start | bytes 589832 | tf_op jit(solution)/shard_map/ppermute | solution.py:629
  255.4 25.0 %collective-permute-start.40 = (bf16[256,384]{1,0:T(8,128)(2,1)}, bf16[256,384]{1,0:T(8,128)(2,1)S(1)}, u32[]{:S(2)}, u32[]{:S(2)}) collective-permute-start(bf16[256,384]{1,0:T(8,128)(2,1)} %get-tuple-element.250), channel_id=1, source_target_pairs={{0,1},{1,0},{2,3},{3,2},{4,5},{5,4},{6,7},{7,6},{8,9},{9,8},{10,11... | collective-permute-start | bytes 589832 | tf_op jit(solution)/shard_map/ppermute | solution.py:629
  262.9 25.7 %collective-permute-start.38 = (bf16[4,160,384]{2,1,0:T(8,128)(2,1)}, bf16[4,160,384]{2,1,0:T(8,128)(2,1)S(1)}, u32[]{:S(2)}, u32[]{:S(2)}) collective-permute-start(bf16[4,160,384]{2,1,0:T(8,128)(2,1)} %get-tuple-element.260), channel_id=1, source_target_pairs={{0,24},{4,28},{8,16},{12,20},{16,8},{20,12},{24,0},{28,4},{1,25},{... | collective-permute-start | bytes 1474568 | tf_op jit(solution)/shard_map/ppermute | solution.py:629
  264.1 24.5 %collective-permute-start.37 = (bf16[4,160,384]{2,1,0:T(8,128)(2,1)}, bf16[4,160,384]{2,1,0:T(8,128)(2,1)S(1)}, u32[]{:S(2)}, u32[]{:S(2)}) collective-permute-start(bf16[4,160,384]{2,1,0:T(8,128)(2,1)} %get-tuple-element.259), channel_id=1, source_target_pairs={{0,16},{4,20},{8,24},{12,28},{16,0},{20,4},{24,8},{28,12},{1,17},{... | collective-permute-start | bytes 1474568 | tf_op jit(solution)/shard_map/ppermute | solution.py:629
  279.0 11.8 %collective-permute-start.36 = (bf16[4,160,384]{2,1,0:T(8,128)(2,1)S(1)}, bf16[4,160,384]{2,1,0:T(8,128)(2,1)S(1)}, u32[]{:S(2)}, u32[]{:S(2)}) collective-permute-start(bf16[4,160,384]{2,1,0:T(8,128)(2,1)S(1)} %copy-done.40), channel_id=1, source_target_pairs={{0,8},{4,12},{8,0},{12,4},{16,24},{20,28},{24,16},{28,20},{1,9},{5... | collective-permute-start | bytes 1474568 | tf_op jit(solution)/shard_map/ppermute | solution.py:629
  296.7 12.2 %collective-permute-start.44 = (bf16[4,64,384]{2,1,0:T(8,128)(2,1)}, bf16[4,64,384]{2,1,0:T(8,128)(2,1)S(1)}, u32[]{:S(2)}, u32[]{:S(2)}) collective-permute-start(bf16[4,64,384]{2,1,0:T(8,128)(2,1)} %get-tuple-element.290), channel_id=1, source_target_pairs={{0,16},{4,20},{8,24},{12,28},{16,0},{20,4},{24,8},{28,12},{1,17},{... | collective-permute-start | bytes 589832 | tf_op jit(solution)/shard_map/ppermute | solution.py:629
  298.9 16.7 %collective-permute-start.56 = (bf16[256,384]{1,0:T(8,128)(2,1)S(1)}, bf16[256,384]{1,0:T(8,128)(2,1)S(1)}, u32[]{:S(2)}, u32[]{:S(2)}) collective-permute-start(bf16[256,384]{1,0:T(8,128)(2,1)S(1)} %copy-done.19), channel_id=1, source_target_pairs={{0,8},{4,12},{8,0},{12,4},{16,24},{20,28},{24,16},{28,20},{1,9},{5... | collective-permute-start | bytes 589832 | tf_op jit(solution)/shard_map/ppermute | solution.py:629
  300.2 17.1 %collective-permute-start.57 = (bf16[256,384]{1,0:T(8,128)(2,1)S(1)}, bf16[256,384]{1,0:T(8,128)(2,1)S(1)}, u32[]{:S(2)}, u32[]{:S(2)}) collective-permute-start(bf16[256,384]{1,0:T(8,128)(2,1)S(1)} %copy-done.19), channel_id=1, source_target_pairs={{0,16},{4,20},{8,24},{12,28},{16,0},{20,4},{24,8},{28,12},{1,17},{... | collective-permute-start | bytes 589832 | tf_op jit(solution)/shard_map/ppermute | solution.py:629
  303.4 13.9 %collective-permute-start.58 = (bf16[256,384]{1,0:T(8,128)(2,1)S(1)}, bf16[256,384]{1,0:T(8,128)(2,1)S(1)}, u32[]{:S(2)}, u32[]{:S(2)}) collective-permute-start(bf16[256,384]{1,0:T(8,128)(2,1)S(1)} %copy-done.19), channel_id=1, source_target_pairs={{0,24},{4,28},{8,16},{12,20},{16,8},{20,12},{24,0},{28,4},{1,25},{... | collective-permute-start | bytes 589832 | tf_op jit(solution)/shard_map/ppermute | solution.py:629
  327.0 14.4 %collective-permute-start.49 = (bf16[352,384]{1,0:T(8,128)(2,1)}, bf16[352,384]{1,0:T(8,128)(2,1)S(1)}, u32[]{:S(2)}, u32[]{:S(2)}) collective-permute-start(bf16[352,384]{1,0:T(8,128)(2,1)} %shard_map.276.refs_0_), channel_id=1, source_target_pairs={{0,8},{4,12},{8,0},{12,4},{16,24},{20,28},{24,16},{28,20},{1,9},{5... | collective-permute-start | bytes 811016 | tf_op jit(solution)/shard_map/ppermute | solution.py:629
  328.0 14.6 %collective-permute-start.50 = (bf16[352,384]{1,0:T(8,128)(2,1)}, bf16[352,384]{1,0:T(8,128)(2,1)S(1)}, u32[]{:S(2)}, u32[]{:S(2)}) collective-permute-start(bf16[352,384]{1,0:T(8,128)(2,1)} %shard_map.276.refs_0_), channel_id=1, source_target_pairs={{0,16},{4,20},{8,24},{12,28},{16,0},{20,4},{24,8},{28,12},{1,17},{... | collective-permute-start | bytes 811016 | tf_op jit(solution)/shard_map/ppermute | solution.py:629
  329.0 13.6 %collective-permute-start.51 = (bf16[352,384]{1,0:T(8,128)(2,1)}, bf16[352,384]{1,0:T(8,128)(2,1)S(1)}, u32[]{:S(2)}, u32[]{:S(2)}) collective-permute-start(bf16[352,384]{1,0:T(8,128)(2,1)} %shard_map.276.refs_0_), channel_id=1, source_target_pairs={{0,24},{4,28},{8,16},{12,20},{16,8},{20,12},{24,0},{28,4},{1,25},{... | collective-permute-start | bytes 811016 | tf_op jit(solution)/shard_map/ppermute | solution.py:629
  (95 other events, 624.0 us)

commit v4 on v3

--- a/solution.py
+++ b/solution.py
@@ -693,10 +693,13 @@
     return pieces
 
 
-def spread_core(pieces, n):
+def spread_core(pieces, n, marks=()):
     if n == 1:
         return pieces
-    return pieces + [(tuple(m ^ 1 for m in masks), swap(value, "rep", 1)) for masks, value in pieces]
+    return pieces + [
+        (tuple(m ^ 1 for m in masks), swap(after(value, *marks) if marks else value, "rep", 1))
+        for masks, value in pieces
+    ]
 
 
 def gather_members(mine):
@@ -999,8 +1002,9 @@
     rows_ref[2 * n : 4 * n, :] = jnp.concatenate([gcond[0:n], feats], axis=0).astype(BF)
 
 
-def emb_grad_kernel(n, inv_entries, counts, extra, table_ref, *refs):
-    pieces, (grad_ref, loss_ref, left_ref, right_ref) = refs[: len(counts)], refs[len(counts) :]
+def emb_kernel(n, inv_entries, counts, extra, member, emb_rows, table_ref, patch_ref, w_ref, m_ref, e_ref, *refs):
+    pieces, refs = refs[: len(counts)], refs[len(counts) :]
+    new_w_ref, new_m_ref, new_e_ref, loss_ref, left_ref, right_ref, grad_ref, own_ref = refs
     at = 0
     for ref, count in zip(pieces, counts):
         each = ref.shape[0] // count
@@ -1021,19 +1025,28 @@
     label = (tags[3:4, :] * 32.0 + tags[4:5, :]).astype(jnp.int32)
     label = pltpu.roll(jnp.broadcast_to(label, (8, total)), total - n, 1)[0:1, :]
     hot = label == lax.broadcasted_iota(jnp.int32, (CLASSES + 8, total), 0)
-    grad_ref[0:PATCH_IN, :] = jnp.zeros((PATCH_IN, D), F32)
+    grad_ref[0:PATCH_IN, :] = patch_ref[0:PATCH_IN, :]
     grad_ref[PATCH_IN : PATCH_IN + FREQ, :] = mm(feats.T, gpre)
     grad_ref[PATCH_IN + FREQ : PATCH_IN + FREQ + D, :] = mm(act.T, gcond)
-    grad_ref[PATCH_IN + FREQ + D :, :] = mm(jnp.where(hot, 1.0, 0.0).astype(BF), gcond)
+    grad_ref[PATCH_IN + FREQ + D : PATCH_IN + FREQ + D + CLASSES + 8, :] = mm(jnp.where(hot, 1.0, 0.0).astype(BF), gcond)
+    rows = own_ref.shape[0]
+    start = emb_rows * table_ref[member]
+    low = start // 8 * 8
+    block = grad_ref[pl.ds(pl.multiple_of(low, 8), rows), :]
+    own_ref[...] = pltpu.roll(block, lax.rem(rows - (start - low), rows), 0)
+    new = advance(w_ref[...], m_ref[...], e_ref[...], own_ref[0:emb_rows, :])
+    new_w_ref[...], new_m_ref[...], new_e_ref[...] = new
     spot = lax.broadcasted_iota(jnp.int32, tags.shape, 1) % (2 * n) >= n
     spot &= lax.broadcasted_iota(jnp.int32, tags.shape, 0) < 3
     loss_ref[...] = jnp.sum(jnp.where(spot, tags, 0.0)).reshape(1, 1) * inv_entries
 
 
-def update_kernel(masks, place, sizes, step_rows, layout, extra, n_chain, table_ref, *refs):
+def update_kernel(masks, place, member, sizes, step_rows, layout, has_head, n_chain, table_ref, *refs):
     pieces, refs = refs[: len(masks)], refs[len(masks) :]
-    states, refs = refs[:6], refs[6 + n_chain :]
-    news, rest_refs, shard_refs = refs[:6], refs[6 : 6 + len(sizes)], refs[6 + len(sizes) :]
+    count = 9 if has_head else 6
+    states, refs = refs[:count], refs[count + n_chain :]
+    news, refs = refs[:count], refs[count:]
+    rest_ref, shard_refs = (None, refs) if has_head else (refs[0], refs[1:])
     step = pl.program_id(0)
 
     @pl.when(step == 0)
@@ -1046,8 +1059,24 @@
                     at = pl.ds(pl.multiple_of(table_ref[place + mask] * rows, rows), rows)
                     shard_ref[at, :] = ref[start : start + rows, :]
                     start += rows
-        for rest_ref, shard_ref in zip(rest_refs, shard_refs):
+        if not has_head:
+            shard_ref = shard_refs[1]
             rest_ref[...] = shard_ref[shard_ref.shape[0] - rest_ref.shape[0] :, :].astype(F32)
+        else:
+            rows = states[6].shape[0]
+            state = [r[...] for r in states[6:]]
+            start = layout[-1][1] + rows
+            for c in range(2):
+                cols = slice(D * c, D * (c + 1))
+                grad = shard_refs[1][start + rows * c : start + rows * (c + 1), :].astype(F32)
+                for ref, value in zip(news[6:], advance(*(x[:, cols] for x in state), grad)):
+                    ref[:, cols] = value
+            start = layout[7][1] + rows
+            flat = shard_refs[0][start : start + PATCH_IN, :].astype(F32)
+            turn = jnp.where(table_ref[member] == 0, 0, D - rows * table_ref[member])
+            grad = pltpu.roll(flat, turn, 1)[:, 0:128].T[0:rows, :]
+            for ref, value in zip(news[6:], advance(*(x[:, 2 * D :] for x in state), grad)):
+                ref[:, 2 * D :] = value
 
     out_rows = states[0].shape[1]
     at = pl.multiple_of(step * out_rows, 16)
@@ -1058,11 +1087,11 @@
         cols = slice(D * block, D * (block + 1))
         at = pl.multiple_of(row + step * step_rows, 16)
         grad = shard_refs[group][pl.ds(at, step_rows), :].astype(F32)
-        for ref, value in zip(news[3:], advance(*(r[0, :, cols] for r in states[3:]), grad)):
+        for ref, value in zip(news[3:6], advance(*(r[0, :, cols] for r in states[3:6]), grad)):
             ref[0, :, cols] = value
 
 
-def update(table, offsets, pieces, layer, packs, extra, outer, inner, chain):
+def update(table, offsets, pieces, layer, packs, outer, inner, head, chain):
     nr = lax.axis_size("rep")
     rows, wide = inner[0].shape[1], inner[0].shape[2]
     rows_out = outer[0].shape[1]
@@ -1074,16 +1103,17 @@
     layout = [(0, rows_out + rows * i, 9 + i) for i in range(4)]
     layout += [(0, rows_out + rows * (4 + i), 2 + i) for i in range(4)]
     layout += [(1, rows * i, 6 + i) for i in range(3)] + [(1, rows * (3 + i), i) for i in range(2)]
-    rests = [packs[0][1] - rows_out - 8 * rows, packs[1][1] - 5 * rows]
+    rests = [] if head else [packs[1][1] - 5 * rows]
     in_spec = pl.BlockSpec((1, step_rows, wide), lambda i: (layer, i, 0))
     out_spec = pl.BlockSpec((1, rows_out // steps, D), lambda i: (layer, i, 0))
-    states = list(outer) + list(inner)
-    specs = [out_spec] * 3 + [in_spec] * 3
+    states = list(outer) + list(inner) + list(head or ())
+    specs = [out_spec] * 3 + [in_spec] * 3 + [whole(*h.shape) for h in head or ()]
     chain = list(chain) if chain else []
     first = 1 + len(arrays) + len(states)
     return pl.pallas_call(
         functools.partial(
-            update_kernel, masks, offsets["place"], sizes, step_rows, tuple(layout), extra, len(chain)
+            update_kernel, masks, offsets["place"], offsets["member"], sizes, step_rows, tuple(layout), bool(head),
+            len(chain),
         ),
         grid=(steps,),
         in_specs=[SCALARS] + [whole(*a.shape) for a in arrays] + specs
@@ -1131,10 +1161,12 @@
     around1 = spread_outer(after(got1, mine23), nr)
     cut2 = shard2.shape[0] // nr
     came1 = [v for m, v in around1 if m != (0,)]
-    got2 = gather_members(after(mine23[:cut2], came1[0]))
+    mine2 = after(mine23[:cut2], got1)
+    parts2 = [swap(after(mine2, came1[0]) if k == 3 else mine2, "grp", k) for k in range(1, ng)]
+    got2 = jnp.concatenate(parts2, axis=0)
     around2 = spread_outer(got2, nr)
-    mine3 = after(mine23[cut2:], *came1, got2)
-    got3 = [swap(mine3, "grp", k) for k in range(1, ng)]
+    mine3 = mine23[cut2:]
+    got3 = [swap(after(mine3, *parts2, *came1), "grp", k) for k in range(1, ng)]
 
     levels = plan(timesteps)
     noise_level = jnp.sqrt(jnp.maximum(1.0 - levels, 0.0))
@@ -1150,7 +1182,7 @@
     pos = positions()
 
     pieces1 = spread_core(
-        [(sum((m for m, _ in around1), ()), jnp.concatenate([v for _, v in around1], axis=0))], nr
+        [(sum((m for m, _ in around1), ()), jnp.concatenate([v for _, v in around1], axis=0))], nr, parts2[:2]
     )
     wp_t, w2, wa0a, wqkv0, wqkv0_t, mods0a, time_act, pre_time, cond, act_t = assemble(
         functools.partial(first_kernel, emb_rows, seg), table, offsets, shard1, pieces1,
@@ -1236,26 +1268,23 @@
     parts_a0, sends_a0 = outer_stage(held(parts_a0, rows0, *parts_f0[1:]))
     pieces_1 = spread_core(spread_outer(piece_1, nr), nr)
     outer_state, inner_state = (w_out, out_mom, out_ema), (w_in, in_mom, in_ema)
-    new_1 = update(table, offsets, pieces_1, 1, (outer_pack, qkv_pack1), 0, outer_state, inner_state, None)
+    new_1 = update(table, offsets, pieces_1, 1, (outer_pack, qkv_pack1), outer_state, inner_state, (head, head_mom, head_ema), None)
     parts_0, sends_0 = member_stage([parts_f0, parts_a0], rows0)
     piece_0 = reduce_last(parts_0, 4 * n, table)
-    pieces_0 = spread_core(spread_outer(piece_0, nr), nr)
+    pieces_0 = spread_core([(m, after(v, new_1[0])) for m, v in spread_outer(piece_0, nr)], nr)
     extra = ng * 4 * n
-    new_0 = update(table, offsets, pieces_0, 0, (outer_pack, qkv_pack0), extra, outer_state, inner_state, new_1[:6])
-    emb_grad, loss_value = small_kernel(
-        functools.partial(emb_grad_kernel, n, 1.0 / entries, tuple(len(m) for m, _ in pieces_0), extra),
-        [((emb_full, D), F32), ((1, 1), F32)], [((2 * n * nr * ng, D), BF)] * 2,
-        (table, *[v for _, v in pieces_0]),
-    )
-    emb_grad = lax.dynamic_slice_in_dim(emb_grad, member * emb_rows, emb_rows, 0)
-    patch_grad = jnp.where(member == 0, new_0[7][:PATCH_IN], 0.0)
-    emb_new = advance(
-        emb_table, emb_mom, emb_ema, emb_grad + jnp.pad(patch_grad, ((0, emb_rows - PATCH_IN), (0, 0)))
-    )
-    wm_grad = new_1[7][: 2 * rows_d].reshape(2, rows_d, D).transpose(1, 0, 2).reshape(rows_d, 2 * D)
-    wy_grad = lax.dynamic_slice_in_dim(new_1[6][:PATCH_IN], member * rows_d, rows_d, 1).T
-    head_new = advance(head, head_mom, head_ema, jnp.concatenate([wm_grad, wy_grad], axis=1))
-    return (loss_value.reshape(()), *emb_new, *new_0[3:6], *new_0[:3], *head_new)
+    new_0 = update(table, offsets, pieces_0, 0, (outer_pack, qkv_pack0), outer_state, inner_state, None, new_1[:6])
+    own_rows = -(-(emb_rows + 7) // 8) * 8
+    grad_rows = max(emb_full, emb_rows * (ng - 1) // 8 * 8 + own_rows)
+    new_emb = small_kernel(
+        functools.partial(
+            emb_kernel, n, 1.0 / entries, tuple(len(m) for m, _ in pieces_0), extra, offsets["member"], emb_rows
+        ),
+        [(emb_table.shape, F32)] * 3 + [((1, 1), F32)],
+        [((2 * n * nr * ng, D), BF)] * 2 + [((grad_rows, D), F32), ((own_rows, D), F32)],
+        (table, new_0[6], emb_table, emb_mom, emb_ema, *[v for _, v in pieces_0]),
+    )
+    return (new_emb[3].reshape(()), *new_emb[:3], *new_0[3:6], *new_0[:3], *new_1[6:9])
 
 
 def solution(mesh):

time: 367 us -> 359 us (0.978)
  waiting for transfers between devices: 45.6 us -> 41.2 us
  other arithmetic: 7.41 us -> 3.07 us
    ppermute x63, waiting for transfers between devices: 45.6 us -> 41.2 us  [swap(): return lax.ppermute(x, axis, pairs)]
    unnamed x135 -> x129, local copies, waits for them, and re-layouts: 10.9 us -> 11.4 us
  transfers between devices with their start and end apart: 63 -> 63, of which waited for: 16 -> 20; matrix products, arithmetic and copies ran while one was open for 2% -> 2% of each run, Pallas kernels for 44% -> 45%
where the time goes in v4:
time: 359 us; the launch traced here: 354 us
  Pallas kernels  233 us (65%)
  starting transfers between devices  60.3 us (17%)
  waiting for transfers between devices  41.2 us (11%)
  local copies, waits for them, and re-layouts  14.6 us (4%)
    pallas_call x8, Pallas kernels, run_kernel(): pl.pallas_call(kernel, grid=(steps,), in_specs=in_specs, out_specs=out_sp...  152 us
    ppermute x63, starting transfers between devices, swap(): return lax.ppermute(x, axis, pairs)  60.3 us
    ppermute x63, waiting for transfers between devices, swap(): return lax.ppermute(x, axis, pairs)  41.2 us
    pallas_call x9, Pallas kernels, small_kernel(): pl.pallas_call(kernel, in_specs=[SCALARS] * scalars + [in_vmem()] * (len(...  39.4 us
    pallas_call x2, Pallas kernels, update(): pl.pallas_call(functools.partial(update_kernel, masks, offsets['place'],...  18 us
    pallas_call x4, Pallas kernels, reduce_outer(): pl.pallas_call(functools.partial(rows_kernel, len(parts), offsets[shift])...  16.3 us
    unnamed x129, local copies, waits for them, and re-layouts  11.4 us
  transfers between devices with their start and end apart: 63, of which 20 were waited for; matrix products, arithmetic and copies ran while one was open for 2% of the time, Pallas kernels for 45%

profile of v4, /device:TPU:0, one launch (start us, length us, event | category | flops | bytes accessed | tf_op | source)
XLA Modules:
  0.0 353.7 jit_solution(15436995677705680205)
XLA Ops:
  1.3 2.7 shard_map.255
  4.0 3.0 collective-permute-start
  7.0 2.6 collective-permute-start.1
  9.6 4.0 %shard_map.256 = (bf16[1152,384]{1,0:T(8,128)(2,1)}, bf16[2048,384]{1,0:T(8,128)(2,1)}, bf16[400,384]{1,0:T(8,128)(2,1)}) custom-call(s32[19]{0:T(128)} %stack.88.table_ref.refs_0_, f32[2,480,384]{2,1,0:T(8,128)} %refs_8_.3, f32[2,96,4992]{2,1,0:T(8,128)} %refs_11_.3, f32[2,96,4992]{2,1,0:T(8,128)} %refs_11_.3, f32[2,96,4992]{2,1,0:T(8,128)} %refs_11_.3, ...), custom_call_target="tpu_custom_call" | custom-call | tf_op jit(solution)/shard_map/pallas_call | solution.py:859
  14.4 3.2 collective-permute-done.1
  26.2 5.4 %collective-permute-done.4 = bf16[384,384]{1,0:T(8,128)(2,1)S(1)} collective-permute-done((bf16[384,384]{1,0:T(8,128)(2,1)S(1)}, bf16[384,384]{1,0:T(8,128)(2,1)S(1)}, u32[]{:S(2)}, u32[]{:S(2)}) %collective-permute-start.4) | collective-permute-done | bytes 294944 | tf_op jit(solution)/shard_map/ppermute | solution.py:629
  37.8 5.4 %collective-permute-done.9 = bf16[144,384]{1,0:T(8,128)(2,1)S(1)} collective-permute-done((bf16[144,384]{1,0:T(8,128)(2,1)S(1)}, bf16[144,384]{1,0:T(8,128)(2,1)S(1)}, u32[]{:S(2)}, u32[]{:S(2)}) %collective-permute-start.9) | collective-permute-done | bytes 110624 | tf_op jit(solution)/shard_map/ppermute | solution.py:629
  49.7 5.1 %shard_map.257 = (bf16[384,16]{1,0:T(8,128)(2,1)}, bf16[384,384]{1,0:T(8,128)(2,1)}, bf16[384,1152]{1,0:T(8,128)(2,1)}, bf16[384,1152]{1,0:T(8,128)(2,1)}, bf16[...) custom-call(s32[19]{0:T(128)} %stack.88.table_ref.refs_0_, ...), custom_call_target="tpu_custom_call" | custom-call | flops 8000000000 | tf_op jit(solution)/shard_map/pallas_call | solution.py:672
  54.7 7.2 %shard_map.258 = (bf16[8,1152,256]{2,1,0:T(8,128)(2,1)}, f32[8,8,256]{2,1,0:T(8,128)}, bf16[8,384,256]{2,1,0:T(8,128)(2,1)}) custom-call(bf16[8,16,256]{2,1,0:T(8,128)(2,1)} %add_convert_fusion.noisy_ref.refs_1_, bf16[384,16]{1,0:T(8,128)(2,1)} %get-tuple-element.178.wp_t_ref.refs_2_, f32[384,256]{1,0:T(8,128)} %pad_maximum_fusion.pos_ref.refs_3_, ...), custom_call_target="tpu_custom_call" | custom-call | flops 10468982784 | bytes 8302592 | tf_op jit(solution)/shard_map/pallas_call | solution.py:460
  63.7 7.2 %shard_map.259 = (bf16[8,1152,256]{2,1,0:T(8,128)(2,1)}, f32[8,8,256]{2,1,0:T(8,128)}, bf16[8,384,256]{2,1,0:T(8,128)(2,1)}) custom-call(bf16[8,16,256]{2,1,0:T(8,128)(2,1)} %add_convert_fusion.noisy_ref.refs_1_, bf16[384,16]{1,0:T(8,128)(2,1)} %get-tuple-element.178.wp_t_ref.refs_2_, ...), custom_call_target="tpu_custom_call", output_to_operand_aliasing={{0}: (5, {}), {1}: (6, {}), {2}: (7, {})} | custom-call | flops 10468982784 | bytes 14659584 | tf_op jit(solution)/shard_map/pallas_call | solution.py:460
  76.4 5.4 %shard_map.260 = (bf16[384,384]{1,0:T(8,128)(2,1)}, bf16[1536,384]{1,0:T(8,128)(2,1)}, bf16[384,384]{1,0:T(8,128)(2,1)}, bf16[384,1536]{1,0:T(8,128)(2,1)}, bf16...) custom-call(s32[19]{0:T(128)} %stack.88.table_ref.refs_0_, ...), custom_call_target="tpu_custom_call" | custom-call | flops 8000000000 | tf_op jit(solution)/shard_map/pallas_call | solution.py:672
  81.8 13.9 %shard_map.261 = (f32[8,384,256]{2,1,0:T(8,128)}, f32[8,384,256]{2,1,0:T(8,128)}, f32[8,384,256]{2,1,0:T(8,128)}, f32[8,384,256]{2,1,0:T(8,128)}) custom-call(bf16[8,16,256]{2,1,0:T(8,128)(2,1)} %add_convert_fusion.noisy_ref.refs_1_, bf16[384,16]{1,0:T(8,128)(2,1)} %get-tuple-element.178.wp_t_ref.refs_2_, f32[384,256]{1,0:T(8,128)} %pad_maximum_fusion.pos_ref.refs_3_, ...), custom_call_target="tpu_custom_call" | custom-call | flops 43486543872 | bytes 18460672 | tf_op jit(solution)/shard_map/pallas_call | solution.py:460
  96.3 4.6 %collective-permute-done.21.refs_2_ = bf16[768,384]{1,0:T(8,128)(2,1)S(1)} collective-permute-done((bf16[768,384]{1,0:T(8,128)(2,1)S(1)}, bf16[768,384]{1,0:T(8,128)(2,1)S(1)}, u32[]{:S(2)}, u32[]{:S(2)}) %collective-permute-start.21) | collective-permute-done | bytes 589856 | tf_op jit(solution)/shard_map/ppermute | solution.py:629
  103.9 7.9 %shard_map.262 = (bf16[384,384]{1,0:T(8,128)(2,1)}, bf16[1536,384]{1,0:T(8,128)(2,1)}, bf16[384,384]{1,0:T(8,128)(2,1)}, bf16[384,1536]{1,0:T(8,128)(2,1)}, bf16...) custom-call(s32[19]{0:T(128)} %stack.88.table_ref.refs_0_, ...), custom_call_target="tpu_custom_call" | custom-call | flops 8000000000 | tf_op jit(solution)/shard_map/pallas_call | solution.py:672
  111.8 44.8 %shard_map.263 = (bf16[8,1152,256]{2,1,0:T(8,128)(2,1)}, f32[8,8,256]{2,1,0:T(8,128)}, bf16[8,384,256]{2,1,0:T(8,128)(2,1)}, f32[8,384,256]{2,1,0:T(8,128)}, f32...) custom-call(s32[19]{0:T(128)} %stack.88.table_ref.refs_0_, ...), custom_call_target="tpu_custom_call" | custom-call | flops 151397597184 | bytes 25731148 | tf_op jit(solution)/shard_map/pallas_call | solution.py:460
  156.8 22.3 %shard_map.264 = (f32[8,384,256]{2,1,0:T(8,128)}, f32[768,128]{1,0:T(8,128)}, bf16[4,384,384]{2,1,0:T(8,128)(2,1)}, bf16[4,384,384]{2,1,0:T(8,128)(2,1)}) custom-call(s32[19]{0:T(128)} %stack.88.table_ref.refs_0_, f32[8,384,256]{2,1,0:T(8,128)} %get-tuple-element.202.hid_ref.refs_1_, bf16[8,1152,256]{2,1,0:T(8,128)(2,1)} %get-tuple-element.219.refs_2_, ...), custom_call_target="tpu_custom_call" | custom-call | flops 45097156608 | bytes 21102668 | tf_op jit(solution)/shard_map/pallas_call | solution.py:460
  181.0 4.4 %shard_map.265 = (bf16[4,160,384]{2,1,0:T(8,128)(2,1)}, bf16[4,160,384]{2,1,0:T(8,128)(2,1)}, bf16[4,160,384]{2,1,0:T(8,128)(2,1)}, bf16[4,160,384]{2,1,0:T(8,128)(2,1)}) custom-call(s32[19]{0:T(128)} %stack.88.table_ref.refs_0_, bf16[4,640,384]{2,1,0:T(8,128)(2,1)} %get-tuple-element.226.refs_0_, bf16[4,640,384]{2,1,0:T(8,128)(2,1)} %copy-done.1), custom_call_target="tpu_custom_call" | custom-call | tf_op jit(solution)/shard_map/pallas_call | solution.py:760
  188.9 30.4 %shard_map.266 = (bf16[8,384,256]{2,1,0:T(8,128)(2,1)}, f32[8,384,256]{2,1,0:T(8,128)}, f32[1536,128]{1,0:T(8,128)}, bf16[4,640,384]{2,1,0:T(8,128)(2,1)}, bf16[4,640,384]{2,1,0:T(8,128)(2,1)}) custom-call(s32[19]{0:T(128)} %stack.88.table_ref.refs_0_, f32[8,384,256]{2,1,0:T(8,128)} %get-tuple-element.232.ghid_ref, ...), custom_call_target="tpu_custom_call" | custom-call | flops 106300440576 | bytes 28704844 | tf_op jit(solution)/shard_map/pallas_call | solution.py:460
  221.4 3.8 %shard_map.267 = (bf16[4,96,384]{2,1,0:T(8,128)(2,1)}, bf16[4,96,384]{2,1,0:T(8,128)(2,1)}, bf16[4,96,384]{2,1,0:T(8,128)(2,1)}, bf16[4,96,384]{2,1,0:T(8,128)(2,1)}) custom-call(s32[19]{0:T(128)} %stack.88.table_ref.refs_0_, bf16[4,384,384]{2,1,0:T(8,128)(2,1)} %get-tuple-element.245.refs_0_, bf16[4,384,384]{2,1,0:T(8,128)(2,1)} %copy-done.2), custom_call_target="tpu_custom_call" | custom-call | tf_op jit(solution)/shard_map/pallas_call | solution.py:760
  228.8 12.8 %shard_map.268 = (f32[768,128]{1,0:T(8,128)}, f32[384,1152]{1,0:T(8,128)}, f32[16,384]{1,0:T(8,128)}) custom-call(s32[19]{0:T(128)} %stack.88.table_ref.refs_0_, bf16[8,16,256]{2,1,0:T(8,128)(2,1)} %add_convert_fusion.noisy_ref.refs_1_, bf16[384,16]{1,0:T(8,128)(2,1)} %get-tuple-element.178.wp_t_ref.refs_2_, f32[384,256]{1,0:T(8,128)} %pad_maximum_fusion.pos_ref.refs_3_, ...), custom_call_target="tpu_custom_call" | custom-call | flops 22548578304 | bytes 13733964 | tf_op jit(solution)/shard_map/pallas_call | solution.py:460
  242.9 3.4 shard_map.269
  252.0 4.4 %shard_map.270 = (bf16[4,160,384]{2,1,0:T(8,128)(2,1)}, bf16[4,160,384]{2,1,0:T(8,128)(2,1)}, bf16[4,160,384]{2,1,0:T(8,128)(2,1)}, bf16[4,160,384]{2,1,0:T(8,128)(2,1)}) custom-call(s32[19]{0:T(128)} %stack.88.table_ref.refs_0_, bf16[4,640,384]{2,1,0:T(8,128)(2,1)} %get-tuple-element.264.refs_0_, bf16[4,640,384]{2,1,0:T(8,128)(2,1)} %copy-done), custom_call_target="tpu_custom_call" | custom-call | tf_op jit(solution)/shard_map/pallas_call | solution.py:760
  258.8 13.9 %shard_map.271 = (f32[768,128]{1,0:T(8,128)}, bf16[4,256,384]{2,1,0:T(8,128)(2,1)}, bf16[4,256,384]{2,1,0:T(8,128)(2,1)}) custom-call(s32[19]{0:T(128)} %stack.88.table_ref.refs_0_, bf16[8,16,256]{2,1,0:T(8,128)(2,1)} %add_convert_fusion.noisy_ref.refs_1_, bf16[384,16]{1,0:T(8,128)(2,1)} %get-tuple-element.178.wp_t_ref.refs_2_, ...), custom_call_target="tpu_custom_call" | custom-call | flops 22548578304 | bytes 15700044 | tf_op jit(solution)/shard_map/pallas_call | solution.py:460
  276.7 5.4 %shard_map.273.refs_8_ = bf16[32,384]{1,0:T(8,128)(2,1)} custom-call(s32[19]{0:T(128)} %stack.88.table_ref.refs_0_, f32[768,128]{1,0:T(8,128)} %get-tuple-element.285.gma0_ref, f32[1536,128]{1,0:T(8,128)} %get-tuple-element.286.gmb0_ref, f32[768,128]{1,0:T(8,128)} %get-tuple-element.287.gma1_ref, f32[1536,128]{1,0:T(8,128)} %get-tuple-element.288.gmb1_ref, ...), custom_call_target="tpu_custom_call" | custom-call | flops 8000000000 | tf_op jit(solution)/shard_map/pallas_call | solution.py:672
  285.5 3.6 %shard_map.274 = (bf16[4,64,384]{2,1,0:T(8,128)(2,1)}, bf16[4,64,384]{2,1,0:T(8,128)(2,1)}, bf16[4,64,384]{2,1,0:T(8,128)(2,1)}, bf16[4,64,384]{2,1,0:T(8,128)(2,1)}) custom-call(s32[19]{0:T(128)} %stack.88.table_ref.refs_0_, bf16[4,256,384]{2,1,0:T(8,128)(2,1)} %get-tuple-element.279.refs_0_, bf16[4,256,384]{2,1,0:T(8,128)(2,1)} %copy-done.3), custom_call_target="tpu_custom_call" | custom-call | tf_op jit(solution)/shard_map/pallas_call | solution.py:760
  293.8 3.4 collective-permute-done.43.refs_5_
  297.2 3.5 collective-permute-done.45.refs_7_
  301.4 3.2 shard_map.275
  312.3 5.5 %collective-permute-done.47.refs_2_ = bf16[256,384]{1,0:T(8,128)(2,1)S(1)} collective-permute-done((bf16[256,384]{1,0:T(8,128)(2,1)}, bf16[256,384]{1,0:T(8,128)(2,1)S(1)}, u32[]{:S(2)}, u32[]{:S(2)}) %collective-permute-start.47) | collective-permute-done | bytes 196640 | tf_op jit(solution)/shard_map/ppermute | solution.py:629
  327.0 9.3 %shard_map.277 = (f32[2,480,384]{2,1,0:T(8,128)}, f32[2,480,384]{2,1,0:T(8,128)}, f32[2,480,384]{2,1,0:T(8,128)}, f32[2,96,4992]{2,1,0:T(8,128)}, f32[2,96,4992]...) custom-call(s32[19]{0:T(128)} %stack.88.table_ref.refs_0_, ...), custom_call_target="tpu_custom_call" | custom-call | tf_op jit(solution)/shard_map/pallas_call | solution.py:1113
  339.8 8.7 %shard_map.278 = (f32[2,480,384]{2,1,0:T(8,128)}, f32[2,480,384]{2,1,0:T(8,128)}, f32[2,480,384]{2,1,0:T(8,128)}, f32[2,96,4992]{2,1,0:T(8,128)}, f32[2,96,4992]...) custom-call(s32[19]{0:T(128)} %stack.88.table_ref.refs_0_, ...), custom_call_target="tpu_custom_call", output_to_operand_aliasing={{0}: (15, {}), {1}: (16, {}), {2}: (17, {}), {3}: (18, {}),... | custom-call | tf_op jit(solution)/shard_map/pallas_call | solution.py:1113
  348.5 5.0 %shard_map.279 = (f32[414,384]{1,0:T(8,128)}, f32[414,384]{1,0:T(8,128)}, f32[414,384]{1,0:T(8,128)}, f32[1,1]{1,0:T(1,128)}) custom-call(s32[19]{0:T(128)} %stack.88.table_ref.refs_0_, f32[32,384]{1,0:T(8,128)} %get-tuple-element.317.patch_ref, f32[414,384]{1,0:T(8,128)} %w_ref.1, f32[414,384]{1,0:T(8,128)} %m_ref.1, f32[414,384]{1,0:T(8,128)} %e_ref.1, ...), custom_call_target="tpu_custom_call" | custom-call | flops 8000000000 | tf_op jit(solution)/shard_map/pallas_call | solution.py:672
  (273 shorter events, 86.6 us)
Async XLA Ops:
  19.4 12.2 %collective-permute-start.4 = (bf16[384,384]{1,0:T(8,128)(2,1)S(1)}, bf16[384,384]{1,0:T(8,128)(2,1)S(1)}, u32[]{:S(2)}, u32[]{:S(2)}) collective-permute-start(bf16[384,384]{1,0:T(8,128)(2,1)S(1)} %constant_dynamic-update-slice_fusion), channel_id=1, source_target_pairs={{0,16},{4,20},{8,24},{12,28},{16,0},{20,4},{24,8},{28,12},{1,17},{... | collective-permute-start | bytes 884744 | tf_op jit(solution)/shard_map/ppermute | solution.py:629
  33.3 15.2 %collective-permute-start.8 = (bf16[1536,384]{1,0:T(8,128)(2,1)S(1)}, bf16[1536,384]{1,0:T(8,128)(2,1)S(1)}, u32[]{:S(2)}, u32[]{:S(2)}) collective-permute-start(bf16[1536,384]{1,0:T(8,128)(2,1)S(1)} %constant_dynamic-update-slice_fusion.3.refs_0_), channel_id=1, source_target_pairs={{0,4},{4,0},{8,12},{12,8},{16,20},{20,16},{24,28},{28,24},{1,5},{5... | collective-permute-start | bytes 3538952 | tf_op jit(solution)/shard_map/ppermute | solution.py:629
  43.2 18.7 %collective-permute-start.12 = (bf16[256,384]{1,0:T(8,128)(2,1)S(1)}, bf16[256,384]{1,0:T(8,128)(2,1)S(1)}, u32[]{:S(2)}, u32[]{:S(2)}) collective-permute-start(bf16[256,384]{1,0:T(8,128)(2,1)S(1)} %slice.7), channel_id=1, source_target_pairs={{0,3},{1,2},{2,1},{3,0},{4,7},{5,6},{6,5},{7,4},{8,11},{9,10},{10,... | collective-permute-start | bytes 589832 | tf_op jit(solution)/shard_map/ppermute | solution.py:629
  45.0 18.7 %collective-permute-start.11 = (bf16[256,384]{1,0:T(8,128)(2,1)S(1)}, bf16[256,384]{1,0:T(8,128)(2,1)S(1)}, u32[]{:S(2)}, u32[]{:S(2)}) collective-permute-start(bf16[256,384]{1,0:T(8,128)(2,1)S(1)} %slice.7), channel_id=1, source_target_pairs={{0,2},{1,3},{2,0},{3,1},{4,6},{5,7},{6,4},{7,5},{8,10},{9,11},{10,... | collective-permute-start | bytes 589832 | tf_op jit(solution)/shard_map/ppermute | solution.py:629
  46.6 17.0 %collective-permute-start.10 = (bf16[256,384]{1,0:T(8,128)(2,1)S(1)}, bf16[256,384]{1,0:T(8,128)(2,1)S(1)}, u32[]{:S(2)}, u32[]{:S(2)}) collective-permute-start(bf16[256,384]{1,0:T(8,128)(2,1)S(1)} %slice.7), channel_id=1, source_target_pairs={{0,1},{1,0},{2,3},{3,2},{4,5},{5,4},{6,7},{7,6},{8,9},{9,8},{10,11... | collective-permute-start | bytes 589832 | tf_op jit(solution)/shard_map/ppermute | solution.py:629
  47.6 23.4 %collective-permute-start.15 = (bf16[432,384]{1,0:T(8,128)(2,1)S(1)}, bf16[432,384]{1,0:T(8,128)(2,1)S(1)}, u32[]{:S(2)}, u32[]{:S(2)}) collective-permute-start(bf16[432,384]{1,0:T(8,128)(2,1)S(1)} %constant_dynamic-update-slice_fusion.7.refs_0_), channel_id=1, source_target_pairs={{0,24},{4,28},{8,16},{12,20},{16,8},{20,12},{24,0},{28,4},{1,25},{... | collective-permute-start | bytes 995336 | tf_op jit(solution)/shard_map/ppermute | solution.py:629
  48.5 22.5 %collective-permute-start.14 = (bf16[432,384]{1,0:T(8,128)(2,1)S(1)}, bf16[432,384]{1,0:T(8,128)(2,1)S(1)}, u32[]{:S(2)}, u32[]{:S(2)}) collective-permute-start(bf16[432,384]{1,0:T(8,128)(2,1)S(1)} %constant_dynamic-update-slice_fusion.7.refs_0_), channel_id=1, source_target_pairs={{0,16},{4,20},{8,24},{12,28},{16,0},{20,4},{24,8},{28,12},{1,17},{... | collective-permute-start | bytes 995336 | tf_op jit(solution)/shard_map/ppermute | solution.py:629
  72.1 23.8 %collective-permute-start.22 = (bf16[768,384]{1,0:T(8,128)(2,1)S(1)}, bf16[768,384]{1,0:T(8,128)(2,1)S(1)}, u32[]{:S(2)}, u32[]{:S(2)}) collective-permute-start(bf16[768,384]{1,0:T(8,128)(2,1)S(1)} %constant_dynamic-update-slice_fusion.10.refs_0_), channel_id=1, source_target_pairs={{0,24},{4,28},{8,16},{12,20},{16,8},{20,12},{24,0},{28,4},{1,25},{... | collective-permute-start | bytes 1769480 | tf_op jit(solution)/shard_map/ppermute | solution.py:629
  73.2 27.7 %collective-permute-start.21 = (bf16[768,384]{1,0:T(8,128)(2,1)S(1)}, bf16[768,384]{1,0:T(8,128)(2,1)S(1)}, u32[]{:S(2)}, u32[]{:S(2)}) collective-permute-start(bf16[768,384]{1,0:T(8,128)(2,1)S(1)} %constant_dynamic-update-slice_fusion.10.refs_0_), channel_id=1, source_target_pairs={{0,16},{4,20},{8,24},{12,28},{16,0},{20,4},{24,8},{28,12},{1,17},{... | collective-permute-start | bytes 1769480 | tf_op jit(solution)/shard_map/ppermute | solution.py:629
  74.3 26.5 %collective-permute-start.20 = (bf16[768,384]{1,0:T(8,128)(2,1)S(1)}, bf16[768,384]{1,0:T(8,128)(2,1)S(1)}, u32[]{:S(2)}, u32[]{:S(2)}) collective-permute-start(bf16[768,384]{1,0:T(8,128)(2,1)S(1)} %constant_dynamic-update-slice_fusion.10.refs_0_), channel_id=1, source_target_pairs={{0,8},{4,12},{8,0},{12,4},{16,24},{20,28},{24,16},{28,20},{1,9},{5... | collective-permute-start | bytes 1769480 | tf_op jit(solution)/shard_map/ppermute | solution.py:629
  156.6 23.0 %collective-permute-start.27 = (bf16[4,640,384]{2,1,0:T(8,128)(2,1)}, bf16[4,640,384]{2,1,0:T(8,128)(2,1)S(1)}, u32[]{:S(2)}, u32[]{:S(2)}) collective-permute-start(bf16[4,640,384]{2,1,0:T(8,128)(2,1)} %get-tuple-element.227), channel_id=1, source_target_pairs={{0,4},{4,0},{8,12},{12,8},{16,20},{20,16},{24,28},{28,24},{1,5},{5... | collective-permute-start | bytes 5898248 | tf_op jit(solution)/shard_map/ppermute | solution.py:629
  179.1 40.3 %collective-permute-start.31 = (bf16[4,384,384]{2,1,0:T(8,128)(2,1)}, bf16[4,384,384]{2,1,0:T(8,128)(2,1)S(1)}, u32[]{:S(2)}, u32[]{:S(2)}) collective-permute-start(bf16[4,384,384]{2,1,0:T(8,128)(2,1)} %get-tuple-element.246), channel_id=1, source_target_pairs={{0,4},{4,0},{8,12},{12,8},{16,20},{20,16},{24,28},{28,24},{1,5},{5... | collective-permute-start | bytes 3538952 | tf_op jit(solution)/shard_map/ppermute | solution.py:629
  185.4 33.9 %collective-permute-start.30 = (bf16[4,160,384]{2,1,0:T(8,128)(2,1)}, bf16[4,160,384]{2,1,0:T(8,128)(2,1)S(1)}, u32[]{:S(2)}, u32[]{:S(2)}) collective-permute-start(bf16[4,160,384]{2,1,0:T(8,128)(2,1)} %get-tuple-element.231), channel_id=1, source_target_pairs={{0,24},{4,28},{8,16},{12,20},{16,8},{20,12},{24,0},{28,4},{1,25},{... | collective-permute-start | bytes 1474568 | tf_op jit(solution)/shard_map/ppermute | solution.py:629
  186.6 32.8 %collective-permute-start.29 = (bf16[4,160,384]{2,1,0:T(8,128)(2,1)}, bf16[4,160,384]{2,1,0:T(8,128)(2,1)S(1)}, u32[]{:S(2)}, u32[]{:S(2)}) collective-permute-start(bf16[4,160,384]{2,1,0:T(8,128)(2,1)} %get-tuple-element.230), channel_id=1, source_target_pairs={{0,16},{4,20},{8,24},{12,28},{16,0},{20,4},{24,8},{28,12},{1,17},{... | collective-permute-start | bytes 1474568 | tf_op jit(solution)/shard_map/ppermute | solution.py:629
  187.7 31.7 %collective-permute-start.28 = (bf16[4,160,384]{2,1,0:T(8,128)(2,1)}, bf16[4,160,384]{2,1,0:T(8,128)(2,1)S(1)}, u32[]{:S(2)}, u32[]{:S(2)}) collective-permute-start(bf16[4,160,384]{2,1,0:T(8,128)(2,1)} %get-tuple-element.229), channel_id=1, source_target_pairs={{0,8},{4,12},{8,0},{12,4},{16,24},{20,28},{24,16},{28,20},{1,9},{5... | collective-permute-start | bytes 1474568 | tf_op jit(solution)/shard_map/ppermute | solution.py:629
  219.2 31.5 %collective-permute-start.35 = (bf16[4,640,384]{2,1,0:T(8,128)(2,1)}, bf16[4,640,384]{2,1,0:T(8,128)(2,1)S(1)}, u32[]{:S(2)}, u32[]{:S(2)}) collective-permute-start(bf16[4,640,384]{2,1,0:T(8,128)(2,1)} %get-tuple-element.265), channel_id=1, source_target_pairs={{0,4},{4,0},{8,12},{12,8},{16,20},{20,16},{24,28},{28,24},{1,5},{5... | collective-permute-start | bytes 5898248 | tf_op jit(solution)/shard_map/ppermute | solution.py:629
  225.3 16.3 %collective-permute-start.34 = (bf16[4,96,384]{2,1,0:T(8,128)(2,1)}, bf16[4,96,384]{2,1,0:T(8,128)(2,1)S(1)}, u32[]{:S(2)}, u32[]{:S(2)}) collective-permute-start(bf16[4,96,384]{2,1,0:T(8,128)(2,1)} %get-tuple-element.254), channel_id=1, source_target_pairs={{0,24},{4,28},{8,16},{12,20},{16,8},{20,12},{24,0},{28,4},{1,25},{... | collective-permute-start | bytes 884744 | tf_op jit(solution)/shard_map/ppermute | solution.py:629
  226.5 15.7 %collective-permute-start.33 = (bf16[4,96,384]{2,1,0:T(8,128)(2,1)}, bf16[4,96,384]{2,1,0:T(8,128)(2,1)S(1)}, u32[]{:S(2)}, u32[]{:S(2)}) collective-permute-start(bf16[4,96,384]{2,1,0:T(8,128)(2,1)} %get-tuple-element.253), channel_id=1, source_target_pairs={{0,16},{4,20},{8,24},{12,28},{16,0},{20,4},{24,8},{28,12},{1,17},{... | collective-permute-start | bytes 884744 | tf_op jit(solution)/shard_map/ppermute | solution.py:629
  227.6 14.5 %collective-permute-start.32 = (bf16[4,96,384]{2,1,0:T(8,128)(2,1)}, bf16[4,96,384]{2,1,0:T(8,128)(2,1)S(1)}, u32[]{:S(2)}, u32[]{:S(2)}) collective-permute-start(bf16[4,96,384]{2,1,0:T(8,128)(2,1)} %get-tuple-element.249), channel_id=1, source_target_pairs={{0,8},{4,12},{8,0},{12,4},{16,24},{20,28},{24,16},{28,20},{1,9},{5... | collective-permute-start | bytes 884744 | tf_op jit(solution)/shard_map/ppermute | solution.py:629
  246.4 26.3 %collective-permute-start.42 = (bf16[256,384]{1,0:T(8,128)(2,1)}, bf16[256,384]{1,0:T(8,128)(2,1)S(1)}, u32[]{:S(2)}, u32[]{:S(2)}) collective-permute-start(bf16[256,384]{1,0:T(8,128)(2,1)} %get-tuple-element.263), channel_id=1, source_target_pairs={{0,3},{1,2},{2,1},{3,0},{4,7},{5,6},{6,5},{7,4},{8,11},{9,10},{10,... | collective-permute-start | bytes 589832 | tf_op jit(solution)/shard_map/ppermute | solution.py:629
  248.5 25.5 %collective-permute-start.41 = (bf16[256,384]{1,0:T(8,128)(2,1)}, bf16[256,384]{1,0:T(8,128)(2,1)S(1)}, u32[]{:S(2)}, u32[]{:S(2)}) collective-permute-start(bf16[256,384]{1,0:T(8,128)(2,1)} %get-tuple-element.262), channel_id=1, source_target_pairs={{0,2},{1,3},{2,0},{3,1},{4,6},{5,7},{6,4},{7,5},{8,10},{9,11},{10,... | collective-permute-start | bytes 589832 | tf_op jit(solution)/shard_map/ppermute | solution.py:629
  249.0 25.0 %collective-permute-start.40 = (bf16[256,384]{1,0:T(8,128)(2,1)}, bf16[256,384]{1,0:T(8,128)(2,1)S(1)}, u32[]{:S(2)}, u32[]{:S(2)}) collective-permute-start(bf16[256,384]{1,0:T(8,128)(2,1)} %get-tuple-element.261), channel_id=1, source_target_pairs={{0,1},{1,0},{2,3},{3,2},{4,5},{5,4},{6,7},{7,6},{8,9},{9,8},{10,11... | collective-permute-start | bytes 589832 | tf_op jit(solution)/shard_map/ppermute | solution.py:629
  256.4 25.7 %collective-permute-start.38 = (bf16[4,160,384]{2,1,0:T(8,128)(2,1)}, bf16[4,160,384]{2,1,0:T(8,128)(2,1)S(1)}, u32[]{:S(2)}, u32[]{:S(2)}) collective-permute-start(bf16[4,160,384]{2,1,0:T(8,128)(2,1)} %get-tuple-element.271), channel_id=1, source_target_pairs={{0,24},{4,28},{8,16},{12,20},{16,8},{20,12},{24,0},{28,4},{1,25},{... | collective-permute-start | bytes 1474568 | tf_op jit(solution)/shard_map/ppermute | solution.py:629
  257.6 24.5 %collective-permute-start.37 = (bf16[4,160,384]{2,1,0:T(8,128)(2,1)}, bf16[4,160,384]{2,1,0:T(8,128)(2,1)S(1)}, u32[]{:S(2)}, u32[]{:S(2)}) collective-permute-start(bf16[4,160,384]{2,1,0:T(8,128)(2,1)} %get-tuple-element.270), channel_id=1, source_target_pairs={{0,16},{4,20},{8,24},{12,28},{16,0},{20,4},{24,8},{28,12},{1,17},{... | collective-permute-start | bytes 1474568 | tf_op jit(solution)/shard_map/ppermute | solution.py:629
  272.7 11.8 %collective-permute-start.36 = (bf16[4,160,384]{2,1,0:T(8,128)(2,1)S(1)}, bf16[4,160,384]{2,1,0:T(8,128)(2,1)S(1)}, u32[]{:S(2)}, u32[]{:S(2)}) collective-permute-start(bf16[4,160,384]{2,1,0:T(8,128)(2,1)S(1)} %copy-done.36), channel_id=1, source_target_pairs={{0,8},{4,12},{8,0},{12,4},{16,24},{20,28},{24,16},{28,20},{1,9},{5... | collective-permute-start | bytes 1474568 | tf_op jit(solution)/shard_map/ppermute | solution.py:629
  292.6 17.4 %collective-permute-start.49 = (bf16[256,384]{1,0:T(8,128)(2,1)S(1)}, bf16[256,384]{1,0:T(8,128)(2,1)S(1)}, u32[]{:S(2)}, u32[]{:S(2)}) collective-permute-start(bf16[256,384]{1,0:T(8,128)(2,1)S(1)} %copy-done.13), channel_id=1, source_target_pairs={{0,8},{4,12},{8,0},{12,4},{16,24},{20,28},{24,16},{28,20},{1,9},{5... | collective-permute-start | bytes 589832 | tf_op jit(solution)/shard_map/ppermute | solution.py:629
  305.0 12.9 %collective-permute-start.47 = (bf16[256,384]{1,0:T(8,128)(2,1)}, bf16[256,384]{1,0:T(8,128)(2,1)S(1)}, u32[]{:S(2)}, u32[]{:S(2)}) collective-permute-start(bf16[256,384]{1,0:T(8,128)(2,1)} %get-tuple-element.305), channel_id=1, source_target_pairs={{0,2},{1,3},{2,0},{3,1},{4,6},{5,7},{6,4},{7,5},{8,10},{9,11},{10,... | collective-permute-start | bytes 589832 | tf_op jit(solution)/shard_map/ppermute | solution.py:629
  309.0 12.9 %collective-permute-start.50 = (bf16[256,384]{1,0:T(8,128)(2,1)S(1)}, bf16[256,384]{1,0:T(8,128)(2,1)S(1)}, u32[]{:S(2)}, u32[]{:S(2)}) collective-permute-start(bf16[256,384]{1,0:T(8,128)(2,1)S(1)} %copy-done.13), channel_id=1, source_target_pairs={{0,16},{4,20},{8,24},{12,28},{16,0},{20,4},{24,8},{28,12},{1,17},{... | collective-permute-start | bytes 589832 | tf_op jit(solution)/shard_map/ppermute | solution.py:629
  310.0 13.2 %collective-permute-start.51 = (bf16[256,384]{1,0:T(8,128)(2,1)S(1)}, bf16[256,384]{1,0:T(8,128)(2,1)S(1)}, u32[]{:S(2)}, u32[]{:S(2)}) collective-permute-start(bf16[256,384]{1,0:T(8,128)(2,1)S(1)} %copy-done.13), channel_id=1, source_target_pairs={{0,24},{4,28},{8,16},{12,20},{16,8},{20,12},{24,0},{28,4},{1,25},{... | collective-permute-start | bytes 589832 | tf_op jit(solution)/shard_map/ppermute | solution.py:629
  320.7 15.9 %collective-permute-start.58 = (bf16[352,384]{1,0:T(8,128)(2,1)}, bf16[352,384]{1,0:T(8,128)(2,1)S(1)}, u32[]{:S(2)}, u32[]{:S(2)}) collective-permute-start(bf16[352,384]{1,0:T(8,128)(2,1)} %shard_map.276.refs_0_), channel_id=1, source_target_pairs={{0,24},{4,28},{8,16},{12,20},{16,8},{20,12},{24,0},{28,4},{1,25},{... | collective-permute-start | bytes 811016 | tf_op jit(solution)/shard_map/ppermute | solution.py:629
  321.9 15.0 %collective-permute-start.57 = (bf16[352,384]{1,0:T(8,128)(2,1)}, bf16[352,384]{1,0:T(8,128)(2,1)S(1)}, u32[]{:S(2)}, u32[]{:S(2)}) collective-permute-start(bf16[352,384]{1,0:T(8,128)(2,1)} %shard_map.276.refs_0_), channel_id=1, source_target_pairs={{0,16},{4,20},{8,24},{12,28},{16,0},{20,4},{24,8},{28,12},{1,17},{... | collective-permute-start | bytes 811016 | tf_op jit(solution)/shard_map/ppermute | solution.py:629
  323.2 13.8 %collective-permute-start.56 = (bf16[352,384]{1,0:T(8,128)(2,1)}, bf16[352,384]{1,0:T(8,128)(2,1)S(1)}, u32[]{:S(2)}, u32[]{:S(2)}) collective-permute-start(bf16[352,384]{1,0:T(8,128)(2,1)} %shard_map.276.refs_0_), channel_id=1, source_target_pairs={{0,8},{4,12},{8,0},{12,4},{16,24},{20,28},{24,16},{28,20},{1,9},{5... | collective-permute-start | bytes 811016 | tf_op jit(solution)/shard_map/ppermute | solution.py:629
  (91 other events, 515.2 us)

commit v5 on v4

--- a/solution.py
+++ b/solution.py
@@ -225,7 +225,7 @@
         image = step * B + b
         hidden = mm(wp_t_ref[...], noisy_ref[b]) + pos_ref[...]
         branch_a = mm(wo_t_ref[...], att_ref[b])
-        bra_ref[b] = branch_a
+        bra_ref[b] = branch_a.astype(BF)
         mid = hidden + column(mods_a_ref, 2, image) * branch_a
         mid_ref[b] = mid
         normed, _ = norm_parts(mid)
@@ -236,7 +236,7 @@
         branch = add_up(branch, mm(wg_t_ref[:, rows], act))
     for b in range(B):
         own = branch[:, lanes_of(b)]
-        brb_ref[b] = own
+        brb_ref[b] = own.astype(BF)
         hid_ref[b] = mid_ref[b] + column(mods_b_ref, 2, step * B + b) * own
 
 
@@ -506,7 +506,7 @@
         functools.partial(ffn_fwd_kernel, B), n // B,
         [images(B, PATCH_IN, TOK), whole(D, PATCH_IN), whole(D, TOK), full, HALF_MODS, HALF_MODS, whole(D, D),
          whole(FF, D), whole(D, FF)],
-        [(full, (n, D, TOK), F32)] * 4,
+        [(full, (n, D, TOK), F32), (full, (n, D, TOK), BF), (full, (n, D, TOK), BF), (full, (n, D, TOK), F32)],
         [((D, T), BF)],
         2 * n * TOK * (2 * D * FF + D * D), (noisy, wp_t, pos, att, mods_a, mods_b, wo_t, wf_t, wg_t))
 
@@ -1203,7 +1203,7 @@
          ((D, 3 * D), BF), ((3 * D, 128), F32)],
         [],
     )
-    mid0, bra0, brb0, hid1 = ffn_forward(noisy, wp_t, pos, att0, mods0a, mods0b, wo0_t, wf0_t, wg0_t, B)
+    mid0, bra0, brb0, hid1 = ffn_forward(noisy, wp_t, pos, att0, mods0a, mods0b, wo0_t, wf0_t, wg0_t, 2 * B)
     pieces3 = spread_core([(m, after(v, hid1)) for m, v in around3], nr)
     (wo1, wg1, wo1_t, wg1_t, wf1, wf1_t, wqkv1, wqkv1_t, wa1, wm, wy, wy_t, mods1, modf) = assemble(
         third_kernel, table, offsets, shard3, pieces3, (act_t,),

time: 359 us -> 359 us (level)
  no operation moved by 1% of the time
where the time goes in v5:
time: 359 us; the launch traced here: 354 us
  Pallas kernels  231 us (64%)
  starting transfers between devices  60.4 us (17%)
  waiting for transfers between devices  42.6 us (12%)
  local copies, waits for them, and re-layouts  14.4 us (4%)
    pallas_call x8, Pallas kernels, run_kernel(): pl.pallas_call(kernel, grid=(steps,), in_specs=in_specs, out_specs=out_sp...  151 us
    ppermute x63, starting transfers between devices, swap(): return lax.ppermute(x, axis, pairs)  60.4 us
    ppermute x63, waiting for transfers between devices, swap(): return lax.ppermute(x, axis, pairs)  42.6 us
    pallas_call x9, Pallas kernels, small_kernel(): pl.pallas_call(kernel, in_specs=[SCALARS] * scalars + [in_vmem()] * (len(...  39.5 us
    pallas_call x2, Pallas kernels, update(): pl.pallas_call(functools.partial(update_kernel, masks, offsets['place'],...  18 us
    pallas_call x4, Pallas kernels, reduce_outer(): pl.pallas_call(functools.partial(rows_kernel, len(parts), offsets[shift])...  16.2 us
    unnamed x129, local copies, waits for them, and re-layouts  11.3 us
  transfers between devices with their start and end apart: 63, of which 20 were waited for; matrix products, arithmetic and copies ran while one was open for 2% of the time, Pallas kernels for 45%

profile of v5, /device:TPU:0, one launch (start us, length us, event | category | flops | bytes accessed | tf_op | source)
XLA Modules:
  0.0 353.7 jit_solution(18239246545648394326)
XLA Ops:
  1.3 2.7 shard_map.255
  3.9 3.0 collective-permute-start
  7.0 2.6 collective-permute-start.1
  9.6 4.0 %shard_map.256 = (bf16[1152,384]{1,0:T(8,128)(2,1)}, bf16[2048,384]{1,0:T(8,128)(2,1)}, bf16[400,384]{1,0:T(8,128)(2,1)}) custom-call(s32[19]{0:T(128)} %stack.88.table_ref.refs_0_, f32[2,480,384]{2,1,0:T(8,128)} %refs_8_.3, f32[2,96,4992]{2,1,0:T(8,128)} %refs_11_.3, f32[2,96,4992]{2,1,0:T(8,128)} %refs_11_.3, f32[2,96,4992]{2,1,0:T(8,128)} %refs_11_.3, ...), custom_call_target="tpu_custom_call" | custom-call | tf_op jit(solution)/shard_map/pallas_call | solution.py:859
  14.4 3.2 collective-permute-done.1
  26.2 5.4 %collective-permute-done.4 = bf16[384,384]{1,0:T(8,128)(2,1)S(1)} collective-permute-done((bf16[384,384]{1,0:T(8,128)(2,1)S(1)}, bf16[384,384]{1,0:T(8,128)(2,1)S(1)}, u32[]{:S(2)}, u32[]{:S(2)}) %collective-permute-start.4) | collective-permute-done | bytes 294944 | tf_op jit(solution)/shard_map/ppermute | solution.py:629
  37.7 5.4 %collective-permute-done.9 = bf16[144,384]{1,0:T(8,128)(2,1)S(1)} collective-permute-done((bf16[144,384]{1,0:T(8,128)(2,1)S(1)}, bf16[144,384]{1,0:T(8,128)(2,1)S(1)}, u32[]{:S(2)}, u32[]{:S(2)}) %collective-permute-start.9) | collective-permute-done | bytes 110624 | tf_op jit(solution)/shard_map/ppermute | solution.py:629
  49.6 5.1 %shard_map.257 = (bf16[384,16]{1,0:T(8,128)(2,1)}, bf16[384,384]{1,0:T(8,128)(2,1)}, bf16[384,1152]{1,0:T(8,128)(2,1)}, bf16[384,1152]{1,0:T(8,128)(2,1)}, bf16[...) custom-call(s32[19]{0:T(128)} %stack.88.table_ref.refs_0_, ...), custom_call_target="tpu_custom_call" | custom-call | flops 8000000000 | tf_op jit(solution)/shard_map/pallas_call | solution.py:672
  54.7 7.2 %shard_map.258 = (bf16[8,1152,256]{2,1,0:T(8,128)(2,1)}, f32[8,8,256]{2,1,0:T(8,128)}, bf16[8,384,256]{2,1,0:T(8,128)(2,1)}) custom-call(bf16[8,16,256]{2,1,0:T(8,128)(2,1)} %add_convert_fusion.noisy_ref.refs_1_, bf16[384,16]{1,0:T(8,128)(2,1)} %get-tuple-element.178.wp_t_ref.refs_2_, f32[384,256]{1,0:T(8,128)} %pad_maximum_fusion.pos_ref.refs_3_, ...), custom_call_target="tpu_custom_call" | custom-call | flops 10468982784 | bytes 8302592 | tf_op jit(solution)/shard_map/pallas_call | solution.py:460
  63.7 7.2 %shard_map.259 = (bf16[8,1152,256]{2,1,0:T(8,128)(2,1)}, f32[8,8,256]{2,1,0:T(8,128)}, bf16[8,384,256]{2,1,0:T(8,128)(2,1)}) custom-call(bf16[8,16,256]{2,1,0:T(8,128)(2,1)} %add_convert_fusion.noisy_ref.refs_1_, bf16[384,16]{1,0:T(8,128)(2,1)} %get-tuple-element.178.wp_t_ref.refs_2_, ...), custom_call_target="tpu_custom_call", output_to_operand_aliasing={{0}: (5, {}), {1}: (6, {}), {2}: (7, {})} | custom-call | flops 10468982784 | bytes 14659584 | tf_op jit(solution)/shard_map/pallas_call | solution.py:460
  76.4 5.5 %shard_map.260 = (bf16[384,384]{1,0:T(8,128)(2,1)}, bf16[1536,384]{1,0:T(8,128)(2,1)}, bf16[384,384]{1,0:T(8,128)(2,1)}, bf16[384,1536]{1,0:T(8,128)(2,1)}, bf16...) custom-call(s32[19]{0:T(128)} %stack.88.table_ref.refs_0_, ...), custom_call_target="tpu_custom_call" | custom-call | flops 8000000000 | tf_op jit(solution)/shard_map/pallas_call | solution.py:672
  81.8 12.4 %shard_map.261 = (f32[8,384,256]{2,1,0:T(8,128)}, bf16[8,384,256]{2,1,0:T(8,128)(2,1)}, bf16[8,384,256]{2,1,0:T(8,128)(2,1)}, f32[8,384,256]{2,1,0:T(8,128)}) custom-call(bf16[8,16,256]{2,1,0:T(8,128)(2,1)} %add_convert_fusion.noisy_ref.refs_1_, bf16[384,16]{1,0:T(8,128)(2,1)} %get-tuple-element.178.wp_t_ref.refs_2_, ...), custom_call_target="tpu_custom_call" | custom-call | flops 43486543872 | bytes 15314944 | tf_op jit(solution)/shard_map/pallas_call | solution.py:460
  94.8 6.0 %collective-permute-done.21.refs_2_ = bf16[768,384]{1,0:T(8,128)(2,1)S(1)} collective-permute-done((bf16[768,384]{1,0:T(8,128)(2,1)S(1)}, bf16[768,384]{1,0:T(8,128)(2,1)S(1)}, u32[]{:S(2)}, u32[]{:S(2)}) %collective-permute-start.21) | collective-permute-done | bytes 589856 | tf_op jit(solution)/shard_map/ppermute | solution.py:629
  103.8 7.9 %shard_map.262 = (bf16[384,384]{1,0:T(8,128)(2,1)}, bf16[1536,384]{1,0:T(8,128)(2,1)}, bf16[384,384]{1,0:T(8,128)(2,1)}, bf16[384,1536]{1,0:T(8,128)(2,1)}, bf16...) custom-call(s32[19]{0:T(128)} %stack.88.table_ref.refs_0_, ...), custom_call_target="tpu_custom_call" | custom-call | flops 8000000000 | tf_op jit(solution)/shard_map/pallas_call | solution.py:672
  111.8 44.9 %shard_map.263 = (bf16[8,1152,256]{2,1,0:T(8,128)(2,1)}, f32[8,8,256]{2,1,0:T(8,128)}, bf16[8,384,256]{2,1,0:T(8,128)(2,1)}, f32[8,384,256]{2,1,0:T(8,128)}, f32...) custom-call(s32[19]{0:T(128)} %stack.88.table_ref.refs_0_, ...), custom_call_target="tpu_custom_call" | custom-call | flops 151397597184 | bytes 25731148 | tf_op jit(solution)/shard_map/pallas_call | solution.py:460
  156.9 22.6 %shard_map.264 = (f32[8,384,256]{2,1,0:T(8,128)}, f32[768,128]{1,0:T(8,128)}, bf16[4,384,384]{2,1,0:T(8,128)(2,1)}, bf16[4,384,384]{2,1,0:T(8,128)(2,1)}) custom-call(s32[19]{0:T(128)} %stack.88.table_ref.refs_0_, f32[8,384,256]{2,1,0:T(8,128)} %get-tuple-element.202.hid_ref.refs_1_, bf16[8,1152,256]{2,1,0:T(8,128)(2,1)} %get-tuple-element.219.refs_2_, ...), custom_call_target="tpu_custom_call" | custom-call | flops 45097156608 | bytes 21102668 | tf_op jit(solution)/shard_map/pallas_call | solution.py:460
  181.2 4.4 %shard_map.265 = (bf16[4,160,384]{2,1,0:T(8,128)(2,1)}, bf16[4,160,384]{2,1,0:T(8,128)(2,1)}, bf16[4,160,384]{2,1,0:T(8,128)(2,1)}, bf16[4,160,384]{2,1,0:T(8,128)(2,1)}) custom-call(s32[19]{0:T(128)} %stack.88.table_ref.refs_0_, bf16[4,640,384]{2,1,0:T(8,128)(2,1)} %get-tuple-element.226.refs_0_, bf16[4,640,384]{2,1,0:T(8,128)(2,1)} %copy-done.1), custom_call_target="tpu_custom_call" | custom-call | tf_op jit(solution)/shard_map/pallas_call | solution.py:760
  189.1 30.1 %shard_map.266 = (bf16[8,384,256]{2,1,0:T(8,128)(2,1)}, f32[8,384,256]{2,1,0:T(8,128)}, f32[1536,128]{1,0:T(8,128)}, bf16[4,640,384]{2,1,0:T(8,128)(2,1)}, bf16[4,640,384]{2,1,0:T(8,128)(2,1)}) custom-call(s32[19]{0:T(128)} %stack.88.table_ref.refs_0_, f32[8,384,256]{2,1,0:T(8,128)} %get-tuple-element.232.ghid_ref, ...), custom_call_target="tpu_custom_call" | custom-call | flops 106300440576 | bytes 25559116 | tf_op jit(solution)/shard_map/pallas_call | solution.py:460
  221.4 3.8 %shard_map.267 = (bf16[4,96,384]{2,1,0:T(8,128)(2,1)}, bf16[4,96,384]{2,1,0:T(8,128)(2,1)}, bf16[4,96,384]{2,1,0:T(8,128)(2,1)}, bf16[4,96,384]{2,1,0:T(8,128)(2,1)}) custom-call(s32[19]{0:T(128)} %stack.88.table_ref.refs_0_, bf16[4,384,384]{2,1,0:T(8,128)(2,1)} %get-tuple-element.245.refs_0_, bf16[4,384,384]{2,1,0:T(8,128)(2,1)} %copy-done.2), custom_call_target="tpu_custom_call" | custom-call | tf_op jit(solution)/shard_map/pallas_call | solution.py:760
  228.7 12.8 %shard_map.268 = (f32[768,128]{1,0:T(8,128)}, f32[384,1152]{1,0:T(8,128)}, f32[16,384]{1,0:T(8,128)}) custom-call(s32[19]{0:T(128)} %stack.88.table_ref.refs_0_, bf16[8,16,256]{2,1,0:T(8,128)(2,1)} %add_convert_fusion.noisy_ref.refs_1_, bf16[384,16]{1,0:T(8,128)(2,1)} %get-tuple-element.178.wp_t_ref.refs_2_, f32[384,256]{1,0:T(8,128)} %pad_maximum_fusion.pos_ref.refs_3_, ...), custom_call_target="tpu_custom_call" | custom-call | flops 22548578304 | bytes 13733964 | tf_op jit(solution)/shard_map/pallas_call | solution.py:460
  242.9 3.4 shard_map.269
  252.0 4.4 %shard_map.270 = (bf16[4,160,384]{2,1,0:T(8,128)(2,1)}, bf16[4,160,384]{2,1,0:T(8,128)(2,1)}, bf16[4,160,384]{2,1,0:T(8,128)(2,1)}, bf16[4,160,384]{2,1,0:T(8,128)(2,1)}) custom-call(s32[19]{0:T(128)} %stack.88.table_ref.refs_0_, bf16[4,640,384]{2,1,0:T(8,128)(2,1)} %get-tuple-element.264.refs_0_, bf16[4,640,384]{2,1,0:T(8,128)(2,1)} %copy-done), custom_call_target="tpu_custom_call" | custom-call | tf_op jit(solution)/shard_map/pallas_call | solution.py:760
  258.7 13.9 %shard_map.271 = (f32[768,128]{1,0:T(8,128)}, bf16[4,256,384]{2,1,0:T(8,128)(2,1)}, bf16[4,256,384]{2,1,0:T(8,128)(2,1)}) custom-call(s32[19]{0:T(128)} %stack.88.table_ref.refs_0_, bf16[8,16,256]{2,1,0:T(8,128)(2,1)} %add_convert_fusion.noisy_ref.refs_1_, bf16[384,16]{1,0:T(8,128)(2,1)} %get-tuple-element.178.wp_t_ref.refs_2_, ...), custom_call_target="tpu_custom_call" | custom-call | flops 22548578304 | bytes 15700044 | tf_op jit(solution)/shard_map/pallas_call | solution.py:460
  276.6 5.4 %shard_map.273.refs_8_ = bf16[32,384]{1,0:T(8,128)(2,1)} custom-call(s32[19]{0:T(128)} %stack.88.table_ref.refs_0_, f32[768,128]{1,0:T(8,128)} %get-tuple-element.285.gma0_ref, f32[1536,128]{1,0:T(8,128)} %get-tuple-element.286.gmb0_ref, f32[768,128]{1,0:T(8,128)} %get-tuple-element.287.gma1_ref, f32[1536,128]{1,0:T(8,128)} %get-tuple-element.288.gmb1_ref, ...), custom_call_target="tpu_custom_call" | custom-call | flops 8000000000 | tf_op jit(solution)/shard_map/pallas_call | solution.py:672
  285.4 3.6 %shard_map.274 = (bf16[4,64,384]{2,1,0:T(8,128)(2,1)}, bf16[4,64,384]{2,1,0:T(8,128)(2,1)}, bf16[4,64,384]{2,1,0:T(8,128)(2,1)}, bf16[4,64,384]{2,1,0:T(8,128)(2,1)}) custom-call(s32[19]{0:T(128)} %stack.88.table_ref.refs_0_, bf16[4,256,384]{2,1,0:T(8,128)(2,1)} %get-tuple-element.279.refs_0_, bf16[4,256,384]{2,1,0:T(8,128)(2,1)} %copy-done.3), custom_call_target="tpu_custom_call" | custom-call | tf_op jit(solution)/shard_map/pallas_call | solution.py:760
  293.7 3.4 collective-permute-done.43.refs_5_
  297.1 3.5 collective-permute-done.45.refs_7_
  301.3 3.2 shard_map.275
  312.2 5.6 %collective-permute-done.47.refs_2_ = bf16[256,384]{1,0:T(8,128)(2,1)S(1)} collective-permute-done((bf16[256,384]{1,0:T(8,128)(2,1)}, bf16[256,384]{1,0:T(8,128)(2,1)S(1)}, u32[]{:S(2)}, u32[]{:S(2)}) %collective-permute-start.47) | collective-permute-done | bytes 196640 | tf_op jit(solution)/shard_map/ppermute | solution.py:629
  327.0 9.3 %shard_map.277 = (f32[2,480,384]{2,1,0:T(8,128)}, f32[2,480,384]{2,1,0:T(8,128)}, f32[2,480,384]{2,1,0:T(8,128)}, f32[2,96,4992]{2,1,0:T(8,128)}, f32[2,96,4992]...) custom-call(s32[19]{0:T(128)} %stack.88.table_ref.refs_0_, ...), custom_call_target="tpu_custom_call" | custom-call | tf_op jit(solution)/shard_map/pallas_call | solution.py:1113
  339.8 8.7 %shard_map.278 = (f32[2,480,384]{2,1,0:T(8,128)}, f32[2,480,384]{2,1,0:T(8,128)}, f32[2,480,384]{2,1,0:T(8,128)}, f32[2,96,4992]{2,1,0:T(8,128)}, f32[2,96,4992]...) custom-call(s32[19]{0:T(128)} %stack.88.table_ref.refs_0_, ...), custom_call_target="tpu_custom_call", output_to_operand_aliasing={{0}: (15, {}), {1}: (16, {}), {2}: (17, {}), {3}: (18, {}),... | custom-call | tf_op jit(solution)/shard_map/pallas_call | solution.py:1113
  348.5 5.0 %shard_map.279 = (f32[414,384]{1,0:T(8,128)}, f32[414,384]{1,0:T(8,128)}, f32[414,384]{1,0:T(8,128)}, f32[1,1]{1,0:T(1,128)}) custom-call(s32[19]{0:T(128)} %stack.88.table_ref.refs_0_, f32[32,384]{1,0:T(8,128)} %get-tuple-element.317.patch_ref, f32[414,384]{1,0:T(8,128)} %w_ref.1, f32[414,384]{1,0:T(8,128)} %m_ref.1, f32[414,384]{1,0:T(8,128)} %e_ref.1, ...), custom_call_target="tpu_custom_call" | custom-call | flops 8000000000 | tf_op jit(solution)/shard_map/pallas_call | solution.py:672
  (273 shorter events, 86.4 us)
Async XLA Ops:
  19.3 12.2 %collective-permute-start.4 = (bf16[384,384]{1,0:T(8,128)(2,1)S(1)}, bf16[384,384]{1,0:T(8,128)(2,1)S(1)}, u32[]{:S(2)}, u32[]{:S(2)}) collective-permute-start(bf16[384,384]{1,0:T(8,128)(2,1)S(1)} %constant_dynamic-update-slice_fusion), channel_id=1, source_target_pairs={{0,16},{4,20},{8,24},{12,28},{16,0},{20,4},{24,8},{28,12},{1,17},{... | collective-permute-start | bytes 884744 | tf_op jit(solution)/shard_map/ppermute | solution.py:629
  33.3 15.2 %collective-permute-start.8 = (bf16[1536,384]{1,0:T(8,128)(2,1)S(1)}, bf16[1536,384]{1,0:T(8,128)(2,1)S(1)}, u32[]{:S(2)}, u32[]{:S(2)}) collective-permute-start(bf16[1536,384]{1,0:T(8,128)(2,1)S(1)} %constant_dynamic-update-slice_fusion.3.refs_0_), channel_id=1, source_target_pairs={{0,4},{4,0},{8,12},{12,8},{16,20},{20,16},{24,28},{28,24},{1,5},{5... | collective-permute-start | bytes 3538952 | tf_op jit(solution)/shard_map/ppermute | solution.py:629
  43.1 18.7 %collective-permute-start.12 = (bf16[256,384]{1,0:T(8,128)(2,1)S(1)}, bf16[256,384]{1,0:T(8,128)(2,1)S(1)}, u32[]{:S(2)}, u32[]{:S(2)}) collective-permute-start(bf16[256,384]{1,0:T(8,128)(2,1)S(1)} %slice.7), channel_id=1, source_target_pairs={{0,3},{1,2},{2,1},{3,0},{4,7},{5,6},{6,5},{7,4},{8,11},{9,10},{10,... | collective-permute-start | bytes 589832 | tf_op jit(solution)/shard_map/ppermute | solution.py:629
  44.9 18.6 %collective-permute-start.11 = (bf16[256,384]{1,0:T(8,128)(2,1)S(1)}, bf16[256,384]{1,0:T(8,128)(2,1)S(1)}, u32[]{:S(2)}, u32[]{:S(2)}) collective-permute-start(bf16[256,384]{1,0:T(8,128)(2,1)S(1)} %slice.7), channel_id=1, source_target_pairs={{0,2},{1,3},{2,0},{3,1},{4,6},{5,7},{6,4},{7,5},{8,10},{9,11},{10,... | collective-permute-start | bytes 589832 | tf_op jit(solution)/shard_map/ppermute | solution.py:629
  46.6 17.0 %collective-permute-start.10 = (bf16[256,384]{1,0:T(8,128)(2,1)S(1)}, bf16[256,384]{1,0:T(8,128)(2,1)S(1)}, u32[]{:S(2)}, u32[]{:S(2)}) collective-permute-start(bf16[256,384]{1,0:T(8,128)(2,1)S(1)} %slice.7), channel_id=1, source_target_pairs={{0,1},{1,0},{2,3},{3,2},{4,5},{5,4},{6,7},{7,6},{8,9},{9,8},{10,11... | collective-permute-start | bytes 589832 | tf_op jit(solution)/shard_map/ppermute | solution.py:629
  47.6 23.3 %collective-permute-start.15 = (bf16[432,384]{1,0:T(8,128)(2,1)S(1)}, bf16[432,384]{1,0:T(8,128)(2,1)S(1)}, u32[]{:S(2)}, u32[]{:S(2)}) collective-permute-start(bf16[432,384]{1,0:T(8,128)(2,1)S(1)} %constant_dynamic-update-slice_fusion.7.refs_0_), channel_id=1, source_target_pairs={{0,24},{4,28},{8,16},{12,20},{16,8},{20,12},{24,0},{28,4},{1,25},{... | collective-permute-start | bytes 995336 | tf_op jit(solution)/shard_map/ppermute | solution.py:629
  48.5 22.5 %collective-permute-start.14 = (bf16[432,384]{1,0:T(8,128)(2,1)S(1)}, bf16[432,384]{1,0:T(8,128)(2,1)S(1)}, u32[]{:S(2)}, u32[]{:S(2)}) collective-permute-start(bf16[432,384]{1,0:T(8,128)(2,1)S(1)} %constant_dynamic-update-slice_fusion.7.refs_0_), channel_id=1, source_target_pairs={{0,16},{4,20},{8,24},{12,28},{16,0},{20,4},{24,8},{28,12},{1,17},{... | collective-permute-start | bytes 995336 | tf_op jit(solution)/shard_map/ppermute | solution.py:629
  72.0 22.3 %collective-permute-start.22 = (bf16[768,384]{1,0:T(8,128)(2,1)S(1)}, bf16[768,384]{1,0:T(8,128)(2,1)S(1)}, u32[]{:S(2)}, u32[]{:S(2)}) collective-permute-start(bf16[768,384]{1,0:T(8,128)(2,1)S(1)} %constant_dynamic-update-slice_fusion.10.refs_0_), channel_id=1, source_target_pairs={{0,24},{4,28},{8,16},{12,20},{16,8},{20,12},{24,0},{28,4},{1,25},{... | collective-permute-start | bytes 1769480 | tf_op jit(solution)/shard_map/ppermute | solution.py:629
  73.1 27.7 %collective-permute-start.21 = (bf16[768,384]{1,0:T(8,128)(2,1)S(1)}, bf16[768,384]{1,0:T(8,128)(2,1)S(1)}, u32[]{:S(2)}, u32[]{:S(2)}) collective-permute-start(bf16[768,384]{1,0:T(8,128)(2,1)S(1)} %constant_dynamic-update-slice_fusion.10.refs_0_), channel_id=1, source_target_pairs={{0,16},{4,20},{8,24},{12,28},{16,0},{20,4},{24,8},{28,12},{1,17},{... | collective-permute-start | bytes 1769480 | tf_op jit(solution)/shard_map/ppermute | solution.py:629
  74.3 26.5 %collective-permute-start.20 = (bf16[768,384]{1,0:T(8,128)(2,1)S(1)}, bf16[768,384]{1,0:T(8,128)(2,1)S(1)}, u32[]{:S(2)}, u32[]{:S(2)}) collective-permute-start(bf16[768,384]{1,0:T(8,128)(2,1)S(1)} %constant_dynamic-update-slice_fusion.10.refs_0_), channel_id=1, source_target_pairs={{0,8},{4,12},{8,0},{12,4},{16,24},{20,28},{24,16},{28,20},{1,9},{5... | collective-permute-start | bytes 1769480 | tf_op jit(solution)/shard_map/ppermute | solution.py:629
  156.7 23.2 %collective-permute-start.27 = (bf16[4,640,384]{2,1,0:T(8,128)(2,1)}, bf16[4,640,384]{2,1,0:T(8,128)(2,1)S(1)}, u32[]{:S(2)}, u32[]{:S(2)}) collective-permute-start(bf16[4,640,384]{2,1,0:T(8,128)(2,1)} %get-tuple-element.227), channel_id=1, source_target_pairs={{0,4},{4,0},{8,12},{12,8},{16,20},{20,16},{24,28},{28,24},{1,5},{5... | collective-permute-start | bytes 5898248 | tf_op jit(solution)/shard_map/ppermute | solution.py:629
  179.5 39.8 %collective-permute-start.31 = (bf16[4,384,384]{2,1,0:T(8,128)(2,1)}, bf16[4,384,384]{2,1,0:T(8,128)(2,1)S(1)}, u32[]{:S(2)}, u32[]{:S(2)}) collective-permute-start(bf16[4,384,384]{2,1,0:T(8,128)(2,1)} %get-tuple-element.246), channel_id=1, source_target_pairs={{0,4},{4,0},{8,12},{12,8},{16,20},{20,16},{24,28},{28,24},{1,5},{5... | collective-permute-start | bytes 3538952 | tf_op jit(solution)/shard_map/ppermute | solution.py:629
  185.6 33.6 %collective-permute-start.30 = (bf16[4,160,384]{2,1,0:T(8,128)(2,1)}, bf16[4,160,384]{2,1,0:T(8,128)(2,1)S(1)}, u32[]{:S(2)}, u32[]{:S(2)}) collective-permute-start(bf16[4,160,384]{2,1,0:T(8,128)(2,1)} %get-tuple-element.231), channel_id=1, source_target_pairs={{0,24},{4,28},{8,16},{12,20},{16,8},{20,12},{24,0},{28,4},{1,25},{... | collective-permute-start | bytes 1474568 | tf_op jit(solution)/shard_map/ppermute | solution.py:629
  186.8 32.5 %collective-permute-start.29 = (bf16[4,160,384]{2,1,0:T(8,128)(2,1)}, bf16[4,160,384]{2,1,0:T(8,128)(2,1)S(1)}, u32[]{:S(2)}, u32[]{:S(2)}) collective-permute-start(bf16[4,160,384]{2,1,0:T(8,128)(2,1)} %get-tuple-element.230), channel_id=1, source_target_pairs={{0,16},{4,20},{8,24},{12,28},{16,0},{20,4},{24,8},{28,12},{1,17},{... | collective-permute-start | bytes 1474568 | tf_op jit(solution)/shard_map/ppermute | solution.py:629
  188.0 31.3 %collective-permute-start.28 = (bf16[4,160,384]{2,1,0:T(8,128)(2,1)}, bf16[4,160,384]{2,1,0:T(8,128)(2,1)S(1)}, u32[]{:S(2)}, u32[]{:S(2)}) collective-permute-start(bf16[4,160,384]{2,1,0:T(8,128)(2,1)} %get-tuple-element.229), channel_id=1, source_target_pairs={{0,8},{4,12},{8,0},{12,4},{16,24},{20,28},{24,16},{28,20},{1,9},{5... | collective-permute-start | bytes 1474568 | tf_op jit(solution)/shard_map/ppermute | solution.py:629
  219.2 31.5 %collective-permute-start.35 = (bf16[4,640,384]{2,1,0:T(8,128)(2,1)}, bf16[4,640,384]{2,1,0:T(8,128)(2,1)S(1)}, u32[]{:S(2)}, u32[]{:S(2)}) collective-permute-start(bf16[4,640,384]{2,1,0:T(8,128)(2,1)} %get-tuple-element.265), channel_id=1, source_target_pairs={{0,4},{4,0},{8,12},{12,8},{16,20},{20,16},{24,28},{28,24},{1,5},{5... | collective-permute-start | bytes 5898248 | tf_op jit(solution)/shard_map/ppermute | solution.py:629
  225.2 16.3 %collective-permute-start.34 = (bf16[4,96,384]{2,1,0:T(8,128)(2,1)}, bf16[4,96,384]{2,1,0:T(8,128)(2,1)S(1)}, u32[]{:S(2)}, u32[]{:S(2)}) collective-permute-start(bf16[4,96,384]{2,1,0:T(8,128)(2,1)} %get-tuple-element.254), channel_id=1, source_target_pairs={{0,24},{4,28},{8,16},{12,20},{16,8},{20,12},{24,0},{28,4},{1,25},{... | collective-permute-start | bytes 884744 | tf_op jit(solution)/shard_map/ppermute | solution.py:629
  226.4 15.7 %collective-permute-start.33 = (bf16[4,96,384]{2,1,0:T(8,128)(2,1)}, bf16[4,96,384]{2,1,0:T(8,128)(2,1)S(1)}, u32[]{:S(2)}, u32[]{:S(2)}) collective-permute-start(bf16[4,96,384]{2,1,0:T(8,128)(2,1)} %get-tuple-element.253), channel_id=1, source_target_pairs={{0,16},{4,20},{8,24},{12,28},{16,0},{20,4},{24,8},{28,12},{1,17},{... | collective-permute-start | bytes 884744 | tf_op jit(solution)/shard_map/ppermute | solution.py:629
  227.6 14.5 %collective-permute-start.32 = (bf16[4,96,384]{2,1,0:T(8,128)(2,1)}, bf16[4,96,384]{2,1,0:T(8,128)(2,1)S(1)}, u32[]{:S(2)}, u32[]{:S(2)}) collective-permute-start(bf16[4,96,384]{2,1,0:T(8,128)(2,1)} %get-tuple-element.249), channel_id=1, source_target_pairs={{0,8},{4,12},{8,0},{12,4},{16,24},{20,28},{24,16},{28,20},{1,9},{5... | collective-permute-start | bytes 884744 | tf_op jit(solution)/shard_map/ppermute | solution.py:629
  246.3 26.4 %collective-permute-start.42 = (bf16[256,384]{1,0:T(8,128)(2,1)}, bf16[256,384]{1,0:T(8,128)(2,1)S(1)}, u32[]{:S(2)}, u32[]{:S(2)}) collective-permute-start(bf16[256,384]{1,0:T(8,128)(2,1)} %get-tuple-element.263), channel_id=1, source_target_pairs={{0,3},{1,2},{2,1},{3,0},{4,7},{5,6},{6,5},{7,4},{8,11},{9,10},{10,... | collective-permute-start | bytes 589832 | tf_op jit(solution)/shard_map/ppermute | solution.py:629
  248.4 25.5 %collective-permute-start.41 = (bf16[256,384]{1,0:T(8,128)(2,1)}, bf16[256,384]{1,0:T(8,128)(2,1)S(1)}, u32[]{:S(2)}, u32[]{:S(2)}) collective-permute-start(bf16[256,384]{1,0:T(8,128)(2,1)} %get-tuple-element.262), channel_id=1, source_target_pairs={{0,2},{1,3},{2,0},{3,1},{4,6},{5,7},{6,4},{7,5},{8,10},{9,11},{10,... | collective-permute-start | bytes 589832 | tf_op jit(solution)/shard_map/ppermute | solution.py:629
  248.9 25.0 %collective-permute-start.40 = (bf16[256,384]{1,0:T(8,128)(2,1)}, bf16[256,384]{1,0:T(8,128)(2,1)S(1)}, u32[]{:S(2)}, u32[]{:S(2)}) collective-permute-start(bf16[256,384]{1,0:T(8,128)(2,1)} %get-tuple-element.261), channel_id=1, source_target_pairs={{0,1},{1,0},{2,3},{3,2},{4,5},{5,4},{6,7},{7,6},{8,9},{9,8},{10,11... | collective-permute-start | bytes 589832 | tf_op jit(solution)/shard_map/ppermute | solution.py:629
  256.4 25.7 %collective-permute-start.38 = (bf16[4,160,384]{2,1,0:T(8,128)(2,1)}, bf16[4,160,384]{2,1,0:T(8,128)(2,1)S(1)}, u32[]{:S(2)}, u32[]{:S(2)}) collective-permute-start(bf16[4,160,384]{2,1,0:T(8,128)(2,1)} %get-tuple-element.271), channel_id=1, source_target_pairs={{0,24},{4,28},{8,16},{12,20},{16,8},{20,12},{24,0},{28,4},{1,25},{... | collective-permute-start | bytes 1474568 | tf_op jit(solution)/shard_map/ppermute | solution.py:629
  257.5 24.5 %collective-permute-start.37 = (bf16[4,160,384]{2,1,0:T(8,128)(2,1)}, bf16[4,160,384]{2,1,0:T(8,128)(2,1)S(1)}, u32[]{:S(2)}, u32[]{:S(2)}) collective-permute-start(bf16[4,160,384]{2,1,0:T(8,128)(2,1)} %get-tuple-element.270), channel_id=1, source_target_pairs={{0,16},{4,20},{8,24},{12,28},{16,0},{20,4},{24,8},{28,12},{1,17},{... | collective-permute-start | bytes 1474568 | tf_op jit(solution)/shard_map/ppermute | solution.py:629
  292.6 17.4 %collective-permute-start.49 = (bf16[256,384]{1,0:T(8,128)(2,1)S(1)}, bf16[256,384]{1,0:T(8,128)(2,1)S(1)}, u32[]{:S(2)}, u32[]{:S(2)}) collective-permute-start(bf16[256,384]{1,0:T(8,128)(2,1)S(1)} %copy-done.13), channel_id=1, source_target_pairs={{0,8},{4,12},{8,0},{12,4},{16,24},{20,28},{24,16},{28,20},{1,9},{5... | collective-permute-start | bytes 589832 | tf_op jit(solution)/shard_map/ppermute | solution.py:629
  304.9 12.9 %collective-permute-start.47 = (bf16[256,384]{1,0:T(8,128)(2,1)}, bf16[256,384]{1,0:T(8,128)(2,1)S(1)}, u32[]{:S(2)}, u32[]{:S(2)}) collective-permute-start(bf16[256,384]{1,0:T(8,128)(2,1)} %get-tuple-element.305), channel_id=1, source_target_pairs={{0,2},{1,3},{2,0},{3,1},{4,6},{5,7},{6,4},{7,5},{8,10},{9,11},{10,... | collective-permute-start | bytes 589832 | tf_op jit(solution)/shard_map/ppermute | solution.py:629
  308.9 12.9 %collective-permute-start.50 = (bf16[256,384]{1,0:T(8,128)(2,1)S(1)}, bf16[256,384]{1,0:T(8,128)(2,1)S(1)}, u32[]{:S(2)}, u32[]{:S(2)}) collective-permute-start(bf16[256,384]{1,0:T(8,128)(2,1)S(1)} %copy-done.13), channel_id=1, source_target_pairs={{0,16},{4,20},{8,24},{12,28},{16,0},{20,4},{24,8},{28,12},{1,17},{... | collective-permute-start | bytes 589832 | tf_op jit(solution)/shard_map/ppermute | solution.py:629
  310.0 13.2 %collective-permute-start.51 = (bf16[256,384]{1,0:T(8,128)(2,1)S(1)}, bf16[256,384]{1,0:T(8,128)(2,1)S(1)}, u32[]{:S(2)}, u32[]{:S(2)}) collective-permute-start(bf16[256,384]{1,0:T(8,128)(2,1)S(1)} %copy-done.13), channel_id=1, source_target_pairs={{0,24},{4,28},{8,16},{12,20},{16,8},{20,12},{24,0},{28,4},{1,25},{... | collective-permute-start | bytes 589832 | tf_op jit(solution)/shard_map/ppermute | solution.py:629
  312.2 11.9 %collective-permute-start.52 = (bf16[256,384]{1,0:T(8,128)(2,1)S(1)}, bf16[256,384]{1,0:T(8,128)(2,1)S(1)}, u32[]{:S(2)}, u32[]{:S(2)}) collective-permute-start(bf16[256,384]{1,0:T(8,128)(2,1)S(1)} %copy-done.13), channel_id=1, source_target_pairs={{0,4},{4,0},{8,12},{12,8},{16,20},{20,16},{24,28},{28,24},{1,5},{5... | collective-permute-start | bytes 589832 | tf_op jit(solution)/shard_map/ppermute | solution.py:629
  320.6 15.9 %collective-permute-start.58 = (bf16[352,384]{1,0:T(8,128)(2,1)}, bf16[352,384]{1,0:T(8,128)(2,1)S(1)}, u32[]{:S(2)}, u32[]{:S(2)}) collective-permute-start(bf16[352,384]{1,0:T(8,128)(2,1)} %shard_map.276.refs_0_), channel_id=1, source_target_pairs={{0,24},{4,28},{8,16},{12,20},{16,8},{20,12},{24,0},{28,4},{1,25},{... | collective-permute-start | bytes 811016 | tf_op jit(solution)/shard_map/ppermute | solution.py:629
  321.8 15.1 %collective-permute-start.57 = (bf16[352,384]{1,0:T(8,128)(2,1)}, bf16[352,384]{1,0:T(8,128)(2,1)S(1)}, u32[]{:S(2)}, u32[]{:S(2)}) collective-permute-start(bf16[352,384]{1,0:T(8,128)(2,1)} %shard_map.276.refs_0_), channel_id=1, source_target_pairs={{0,16},{4,20},{8,24},{12,28},{16,0},{20,4},{24,8},{28,12},{1,17},{... | collective-permute-start | bytes 811016 | tf_op jit(solution)/shard_map/ppermute | solution.py:629
  323.2 13.9 %collective-permute-start.56 = (bf16[352,384]{1,0:T(8,128)(2,1)}, bf16[352,384]{1,0:T(8,128)(2,1)S(1)}, u32[]{:S(2)}, u32[]{:S(2)}) collective-permute-start(bf16[352,384]{1,0:T(8,128)(2,1)} %shard_map.276.refs_0_), channel_id=1, source_target_pairs={{0,8},{4,12},{8,0},{12,4},{16,24},{20,28},{24,16},{28,20},{1,9},{5... | collective-permute-start | bytes 811016 | tf_op jit(solution)/shard_map/ppermute | solution.py:629
  (91 other events, 518.1 us)
